TPU v7x, 128 devices: a whole 4x4x4 slice. The times are simulated.
128 devices in a mesh: grp: 4 (over x), seq: 32 (over y, z, core).
Axes of the slice: x: 4, y: 4, z: 4, core: 2. Of those that a mesh axis runs over, the one named last changes fastest.
Arguments:
- compressed: bfloat16 [524288, 576], P(('grp', 'seq')), may hold values from -6 to 6
- block_channel_scale: float32 [4096, 576], P(('grp', 'seq')), may hold values from 0.2 to 2.5
- outlier_channels: int32 [4096, 16], P(('grp', 'seq')), may hold values from 0 to 575, all different within a row
- outlier_values: bfloat16 [4096, 16, 128], P(('grp', 'seq')), may hold values from -16 to 16
- lengths: int32 [4, 4], replicated, may hold values from 1 to 12, 32 in all within a row
- assignment: int32 [4, 4], replicated, may hold values from 0 to 3, each once within a row
- padding: int32 [4, 4], replicated, may hold values from 0 to 127
- queries: bfloat16 [16, 512, 576], P('grp')
- decode_token_latent: bfloat16 [16, 4, 576], P('grp'), may hold values from -8 to 8
Outputs:
- decode_cache: bfloat16 [4, 4, 32, 12, 128, 576], P('grp', None, 'seq')
- attended: bfloat16 [16, 512, 512], P('grp', 'seq')
Inputs may be any that keep to these rules, and one draw needn't show every extreme that they name: `lengths`: each row sums to 32, and its largest entry is exactly 12. `assignment`: each row is a permutation: every prefill group sends one request to each decode group. `outlier_channels`: the 16 channels of a block are distinct.
All inputs are finite; a program needn't handle non-finite values.
Results may differ from a plain program's by a relative error of at most 0.0087.
The roundings to bfloat16 on the way count: a program that leaves them out, or rounds other values in their place, can miss the bound.
Values may be sent and summed in bfloat16 or wider, within the bound.
No kernel may reach another device: no remote copies, remote signals or barrier semaphores. Data moves between devices by JAX's collectives and lax.ppermute only.
A program may use at most 128 MiB of HBM per device.

v0:
```python
import jax
import jax.numpy as jnp
from jax import lax
from jax.sharding import PartitionSpec as P

LATENT_CHANNELS = 512
MOST_STRIPES = 12


NEG_FILL = -1e30
SCORE_SCALE = 192.0 ** (-0.5)


def dequantize(compressed, block_channel_scale, outlier_channels, outlier_values):
    blocks, channels = block_channel_scale.shape
    channel_ids = jnp.arange(channels, dtype=jnp.int32)
    onehot = (outlier_channels[:, :, None] == channel_ids[None, None, :]).astype(jnp.float32)
    plain_mask = 1.0 - jnp.sum(onehot, axis=1)
    scaled = (
        compressed.reshape(blocks, -1, channels).astype(jnp.float32)
        * (block_channel_scale * plain_mask)[:, None, :]
    )
    outliers = jnp.einsum(
        "bkt,bkc->btc", outlier_values.astype(jnp.float32), onehot, precision=lax.Precision.HIGHEST
    )
    return (scaled + outliers).astype(jnp.bfloat16)


def slot_tables(lengths, assignment, padding, seq_count, rows_per_block):
    groups = lengths.shape[0]
    target = jnp.arange(groups, dtype=jnp.int32)
    matched = assignment[None, :, :] == target[:, None, None]
    offsets = jnp.cumsum(lengths, axis=1) - lengths

    def per_slot(values_table):
        return jnp.sum(jnp.where(matched, values_table[None, :, :], 0), axis=2)

    slot_len = per_slot(lengths)
    slot_off = per_slot(offsets)
    slot_live = slot_len * (seq_count * rows_per_block) - per_slot(padding)
    return (slot_len, slot_off, slot_live)


def finish_rows(local_max, weigh, queries, decode_token_latent):
    head_count = queries.shape[1] // decode_token_latent.shape[1]
    new_scores = (
        jnp.einsum("yeu,ynu->yen", queries, decode_token_latent, preferred_element_type=jnp.float32)
        * SCORE_SCALE
    )
    row_step = jnp.arange(queries.shape[1], dtype=jnp.int32) // head_count
    col_step = jnp.arange(decode_token_latent.shape[1], dtype=jnp.int32)
    causal = col_step[None, :] <= row_step[:, None]
    new_scores = jnp.where(causal[None], new_scores, NEG_FILL)
    row_peak = lax.pmax(jnp.maximum(local_max, jnp.max(new_scores, axis=2)), "seq")
    weighted_values, weight_total_sum = weigh(row_peak)
    weighted_values, weight_total_sum = (
        lax.psum_scatter(weighted_values, "seq", scatter_dimension=1, tiled=True),
        lax.psum_scatter(weight_total_sum, "seq", scatter_dimension=1, tiled=True),
    )
    own_rows = weighted_values.shape[1]
    row_start = lax.axis_index("seq") * own_rows
    own_scores = lax.dynamic_slice_in_dim(new_scores, row_start, own_rows, 1)
    own_peak = lax.dynamic_slice_in_dim(row_peak, row_start, own_rows, 1)
    fresh_weights = jnp.exp(own_scores - own_peak[:, :, None]).astype(jnp.bfloat16)
    weighted_values = weighted_values + jnp.einsum(
        "oep,opf->oef",
        fresh_weights,
        decode_token_latent[:, :, :LATENT_CHANNELS],
        preferred_element_type=jnp.float32,
    )
    weight_total_sum = weight_total_sum + jnp.sum(fresh_weights.astype(jnp.float32), axis=2)
    return (weighted_values / weight_total_sum[:, :, None]).astype(jnp.bfloat16)


def local(
    compressed,
    block_channel_scale,
    outlier_channels,
    outlier_values,
    lengths,
    assignment,
    padding,
    queries,
    decode_token_latent,
):
    seq_count = lax.axis_size("seq")
    group_here = lax.axis_index("grp")
    seq_here = lax.axis_index("seq")
    latent = dequantize(compressed, block_channel_scale, outlier_channels, outlier_values)
    blocks, rows_per_block, channels = latent.shape
    per_device = blocks // seq_count
    latent = latent.reshape(per_device, seq_count, rows_per_block, channels)
    stripes = lax.all_to_all(latent, "seq", split_axis=1, concat_axis=0, tiled=True).reshape(
        blocks, rows_per_block, channels
    )
    slot_len, slot_off, slot_live = slot_tables(
        lengths, assignment, padding, seq_count, rows_per_block
    )
    send_off = lax.dynamic_index_in_dim(slot_off, group_here, 1, keepdims=False)
    stripe_ids = jnp.arange(MOST_STRIPES, dtype=jnp.int32)
    source = jnp.clip(send_off[:, None] + stripe_ids[None, :], 0, blocks - 1)
    outgoing = jnp.take(stripes, source, axis=0)
    incoming = lax.all_to_all(outgoing, "grp", split_axis=0, concat_axis=0, tiled=True)
    recv_live = lax.dynamic_index_in_dim(slot_live, group_here, 0, keepdims=False)
    token_ids = jnp.arange(rows_per_block, dtype=jnp.int32)
    position = (stripe_ids[:, None] * seq_count + seq_here) * rows_per_block + token_ids[None, :]
    live_mask = position[None] < recv_live[:, None, None]
    cache_block = jnp.where(live_mask[..., None], incoming, jnp.zeros((), jnp.bfloat16))
    decode_cache = cache_block[None, :, None]
    groups = cache_block.shape[0]
    cache_keys = cache_block.reshape(groups, -1, channels)
    key_mask = live_mask.reshape(groups, -1)
    scores = (
        jnp.einsum("grc,gkc->grk", queries, cache_keys, preferred_element_type=jnp.float32)
        * SCORE_SCALE
    )
    scores = jnp.where(key_mask[:, None, :], scores, NEG_FILL)
    cache_values = cache_keys[:, :, :LATENT_CHANNELS]

    def weigh_decode(row_peak):
        weights = jnp.exp(scores - row_peak[:, :, None]).astype(jnp.bfloat16)
        weighted_values = jnp.einsum(
            "grk,gkc->grc", weights, cache_values, preferred_element_type=jnp.float32
        )
        return (weighted_values, jnp.sum(weights.astype(jnp.float32), axis=2))

    attended = finish_rows(jnp.max(scores, axis=2), weigh_decode, queries, decode_token_latent)
    return (decode_cache, attended)


def solution(mesh):
    placed = (
        P(("grp", "seq"), None),
        P(("grp", "seq"), None),
        P(("grp", "seq"), None),
        P(("grp", "seq"), None, None),
        P(),
        P(),
        P(),
        P("grp", None, None),
        P("grp", None, None),
    )
    return jax.shard_map(
        local,
        mesh=mesh,
        in_specs=placed,
        out_specs=(P("grp", None, "seq", None, None, None), P("grp", "seq", None)),
        check_vma=False,
    )
```

profile of v0, /device:TPU:1, one launch (start us, length us, event | category | flops | bytes accessed | tf_op | source)
XLA Modules:
  0.0 447.8 jit_solution(8104688424271731627)
XLA Ops:
  7.2 0.9 copy.32
  8.1 0.4 convert_reduce_fusion.1
  8.5 0.9 subtract_multiply_fusion
  9.4 8.2 %fusion.6 = bf16[1,32,128,576]{2,3,0,1:T(8,128)(2,1)} fusion(f32[32,576]{1,0:T(8,128)S(1)} %subtract_multiply_fusion, bf16[32,16,128]{2,1,0:T(8,128)(2,1)} %param.12, s32[32,16]{1,0:T(8,128)S(1)} %copy.32, bf16[4096,576]{0,1:T(8,128)(2,1)} %param.9), kind=kOutput, calls=%fused_computation.15 | convolution fusion | flops 85229568 | bytes 9644032 | tf_op jit(solution)/shard_map/bkt,bkc->btc/dot_general | solution.py:23
  17.6 9.8 %all-to-all-start = ((bf16[1,32,128,576]{2,3,0,1:T(8,128)(2,1)}), bf16[1,32,128,576]{2,3,0,1:T(8,128)(2,1)}, u32[]{:S(2)}, u32[]{:S(2)}) async-start(bf16[1,32,128,576]{2,3,0,1:T(8,128)(2,1)} %fusion.6), calls=%async_computation | async-start | bytes 9437184 | tf_op jit(solution)/shard_map/all_to_all | solution.py:93
  27.6 0.3 select_reduce_fusion.2
  28.4 57.5 %all-to-all-done = bf16[1,32,128,576]{2,3,0,1:T(8,128)(2,1)} async-done(((bf16[1,32,128,576]{2,3,0,1:T(8,128)(2,1)}), bf16[1,32,128,576]{2,3,0,1:T(8,128)(2,1)}, u32[]{:S(2)}, u32[]{:S(2)}) %all-to-all-start) | async-done | bytes 4718624 | tf_op jit(solution)/shard_map/all_to_all | solution.py:93
  85.9 7.8 %gather_fusion = bf16[48,128,576]{1,2,0:T(8,128)(2,1)} fusion(bf16[32,128,576]{1,2,0:T(8,128)(2,1)} %bitcast.4, s32[1024]{0:T(1024)S(1)} %pad_clamp_fusion), kind=kCustom, calls=%fused_computation | custom fusion | bytes 14155968 | tf_op jit(solution)/shard_map/jit(_take)/gather | solution.py:102
  93.6 6.7 %broadcast_select_fusion = bf16[4,12,128,576]{2,3,1,0:T(8,128)(2,1)} fusion(bf16[4,12,128,576]{2,3,1,0:T(8,128)(2,1)} %bitcast.49, pred[4,12]{1,0:T(4,128)(4,1)S(1)} %compare_and_fusion), kind=kLoop, calls=%fused_computation.11 | loop fusion | flops 3538944 | bytes 14155824 | tf_op jit(solution)/shard_map/jit(_take)/select_n | solution.py:102
  100.3 5.5 %all-to-all-start.1 = ((bf16[4,12,128,576]{2,3,1,0:T(8,128)(2,1)}), bf16[4,12,128,576]{2,3,1,0:T(8,128)(2,1)}, u32[]{:S(2)}, u32[]{:S(2)}) async-start(bf16[4,12,128,576]{2,3,1,0:T(8,128)(2,1)} %broadcast_select_fusion), calls=%async_computation.1 | async-start | bytes 14155776 | tf_op jit(solution)/shard_map/all_to_all | solution.py:103
  106.2 0.4 fusion.19
  106.7 78.1 %all-to-all-done.1 = bf16[4,12,128,576]{2,3,1,0:T(8,128)(2,1)} async-done(((bf16[4,12,128,576]{2,3,1,0:T(8,128)(2,1)}), bf16[4,12,128,576]{2,3,1,0:T(8,128)(2,1)}, u32[]{:S(2)}, u32[]{:S(2)}) %all-to-all-start.1) | async-done | bytes 7077920 | tf_op jit(solution)/shard_map/all_to_all | solution.py:103
  184.8 6.5 %broadcast_select_fusion.1 = bf16[4,12,128,576]{2,3,1,0:T(8,128)(2,1)} fusion(bf16[4,12,128,576]{2,3,1,0:T(8,128)(2,1)} %all-to-all-done.1, pred[4,12,128]{2,1,0:T(8,128)(4,1)S(1)} %broadcast_compare_fusion), kind=kLoop, calls=%fused_computation.12 | loop fusion | flops 3538944 | bytes 14161920 | tf_op jit(solution)/shard_map/jit(_where)/select_n | solution.py:108
  191.3 10.1 %copy.35 = bf16[4,12,128,576]{3,2,1,0:T(8,128)(2,1)} copy(bf16[4,12,128,576]{2,3,1,0:T(8,128)(2,1)} %broadcast_select_fusion.1) | data formatting | bytes 14155776 | tf_op jit(solution)/shard_map/jit(_where)/select_n | solution.py:108
  201.4 10.4 %bitcast_reduce_fusion = (f32[4,512]{1,0:T(4,128)S(1)}, f32[4,1536,512]{2,1,0:T(8,128)}) fusion(pred[4,1536]{1,0:T(4,128)(4,1)S(1)} %broadcast_compare_fusion.1, bf16[4,1536,576]{2,1,0:T(8,128)(2,1)} %bitcast.50, bf16[4,512,576]{1,2,0:T(8,128)(2,1)S(1)} %copy-done), kind=kOutput, calls=%fused_computation.2 | convolution fusion | flops 3633313792 | bytes 22034432 | tf_op jit(solution)/shard_map/grc,gkc->grk/dot_general | solution.py:114
  211.7 64.7 %pmax.7 = f32[4,512]{1,0:T(4,128)S(1)} all-reduce(f32[4,512]{1,0:T(4,128)S(1)} %max.15), channel_id=1, replica_groups=mesh['grp'=4,'seq'=32] {'seq'}, use_global_device_ids=true, to_apply=%region_7.8 | all-reduce | flops 2048 | bytes 16384 | tf_op jit(solution)/shard_map/pmax | solution.py:54
  276.5 6.4 %convert_reduce_fusion = f32[4,512]{1,0:T(4,128)S(1)} fusion(f32[4,512]{1,0:T(4,128)S(1)} %pmax.7, f32[4,1536,512]{2,1,0:T(8,128)} %get-tuple-element.6, pred[4,1536]{1,0:T(4,128)(4,1)S(1)} %broadcast_compare_fusion.1), kind=kLoop, calls=%fused_computation.5 | loop fusion | flops 18872320 | bytes 12605440 | tf_op jit(solution)/shard_map/reduce_sum | solution.py:125
  282.9 0.9 copy.40
  284.0 11.2 %fusion.4 = f32[4,512,512]{2,1,0:T(8,128)} fusion(bf16[4,1536,576]{2,1,0:T(8,128)(2,1)} %bitcast.51, f32[4,1536,512]{2,1,0:T(8,128)} %get-tuple-element.6, f32[4,512]{1,0:T(4,128)S(1)} %pmax.7, pred[4,1536]{1,0:T(4,128)(4,1)S(1)} %broadcast_compare_fusion.1), kind=kOutput, calls=%fused_computation.13 | convolution fusion | flops 3233808384 | bytes 23083008 | tf_op jit(solution)/shard_map/grk,gkc->grc/dot_general | solution.py:122
  295.4 6.7 %fusion.25 = bf16[1,4,1,12,128,576]{4,5,3,2,1,0:T(8,128)(2,1)} fusion(bf16[4,12,128,576]{2,3,1,0:T(8,128)(2,1)} %all-to-all-done.1, pred[4,12,128]{2,1,0:T(8,128)(4,1)S(1)} %broadcast_compare_fusion), kind=kLoop, calls=%fused_computation.58 | loop fusion | flops 3538944 | bytes 14161920 | tf_op jit(solution)/shard_map/broadcast_in_dim | solution.py:109
  302.0 51.8 %reduce-scatter.7.cloned.1.call-done = f32[16,4]{1,0:T(8,128)} async-done(((f32[512,4]{1,0:T(8,128)}), f32[16,4]{1,0:T(8,128)}) %reduce-scatter.7.cloned.1.call-update) | async-done | bytes 272
  353.8 0.8 copy.41
  354.6 84.5 %reduce-scatter.5.cloned.1.call-done = f32[4,16,512]{2,1,0:T(8,128)} async-done(((f32[4,512,512]{2,1,0:T(8,128)}), f32[4,16,512]{2,1,0:T(8,128)}) %reduce-scatter.5.cloned.1.call-update) | async-done | bytes 131088 | tf_op jit(solution)/shard_map/reduce_scatter | solution.py:57
  439.1 1.8 fusion.8
  (37 shorter events, 1.5 us)
Async XLA Ops:
  7.2 99.0 %copy-start = (bf16[4,512,576]{1,2,0:T(8,128)(2,1)S(1)}, bf16[4,512,576]{1,2,0:T(8,128)(2,1)}, u32[]{:S(2)}) copy-start(bf16[4,512,576]{1,2,0:T(8,128)(2,1)} %param.16) | copy-start | bytes 7077892
  17.6 9.8 %copy-start.3 = (s32[4,4]{1,0:T(4,128)S(1)}, s32[4,4]{1,0:T(4,128)}, u32[]{:S(2)}) copy-start(s32[4,4]{1,0:T(4,128)} %param.13) | copy-start | bytes 196
  17.6 10.0 %copy-start.4 = (s32[4,4]{1,0:T(4,128)S(1)}, s32[4,4]{1,0:T(4,128)}, u32[]{:S(2)}) copy-start(s32[4,4]{1,0:T(4,128)} %param.14) | copy-start | bytes 196
  17.6 10.0 %copy-start.5 = (s32[4,4]{1,0:T(4,128)S(1)}, s32[4,4]{1,0:T(4,128)}, u32[]{:S(2)}) copy-start(s32[4,4]{1,0:T(4,128)} %param.15) | copy-start | bytes 196
  17.6 68.2 %all-to-all-start = ((bf16[1,32,128,576]{2,3,0,1:T(8,128)(2,1)}), bf16[1,32,128,576]{2,3,0,1:T(8,128)(2,1)}, u32[]{:S(2)}, u32[]{:S(2)}) async-start(bf16[1,32,128,576]{2,3,0,1:T(8,128)(2,1)} %fusion.6), calls=%async_computation | async-start | bytes 9437184 | tf_op jit(solution)/shard_map/all_to_all | solution.py:93
  100.3 5.9 %copy-start.2 = (bf16[4,4,576]{2,1,0:T(4,128)(2,1)S(1)}, bf16[4,4,576]{2,1,0:T(4,128)(2,1)}, u32[]{:S(2)}) copy-start(bf16[4,4,576]{2,1,0:T(4,128)(2,1)} %param.17) | copy-start | bytes 55300
  100.3 84.5 %all-to-all-start.1 = ((bf16[4,12,128,576]{2,3,1,0:T(8,128)(2,1)}), bf16[4,12,128,576]{2,3,1,0:T(8,128)(2,1)}, u32[]{:S(2)}, u32[]{:S(2)}) async-start(bf16[4,12,128,576]{2,3,1,0:T(8,128)(2,1)} %broadcast_select_fusion), calls=%async_computation.1 | async-start | bytes 14155776 | tf_op jit(solution)/shard_map/all_to_all | solution.py:103
  105.8 248.0 %reduce-scatter.7.cloned.1.call-start = ((), (), s32[]{:S(2)}) async-start(), calls=%async_computation.5 | async-start | bytes 270336
  283.8 155.4 %reduce-scatter.5.cloned.1.call-start = ((), (), s32[]{:S(2)}) async-start(), calls=%async_computation.4 | async-start | bytes 4325376 | tf_op jit(solution)/shard_map/reduce_scatter | solution.py:57
  295.3 145.7 %copy-start.1 = (bf16[4,512,576]{1,2,0:T(8,128)(2,1)S(1)}, bf16[4,512,576]{1,2,0:T(8,128)(2,1)}, u32[]{:S(2)}) copy-start(bf16[4,512,576]{1,2,0:T(8,128)(2,1)} %param.16) | copy-start | bytes 7077892
Sparse Core Ops, SparseCore 0:
  283.9 69.9 reduce-scatter.6
  357.5 81.6 reduce-scatter.4
where the time goes:
time: 450 us; the launch traced here: 448 us
  waiting for transfers between devices  272 us (60%)
  blocking collectives  64.7 us (14%)
  matrix products  32 us (7%)
  other arithmetic  28.5 us (6%)
  local copies, waits for them, and re-layouts  20.9 us (5%)
  starting transfers between devices  15.6 us (3%)
  between operations  14.2 us (3%)
    reduce_scatter x1, waiting for transfers between devices, finish_rows(): lax.psum_scatter(weighted_values, 'seq', scatter_dimension=1, tiled=True)  84.5 us
    all_to_all x1, waiting for transfers between devices, local(): lax.all_to_all(outgoing, 'grp', split_axis=0, concat_axis=0, tiled=True)  78.1 us
    pmax x1, blocking collectives, finish_rows(): lax.pmax(jnp.maximum(local_max, jnp.max(new_scores, axis=2)), 'seq')  64.7 us
    all_to_all x1, waiting for transfers between devices, local(): lax.all_to_all(latent, 'seq', split_axis=1, concat_axis=0, tiled=True)  57.5 us
    unnamed x3, waiting for transfers between devices  51.8 us
    dot_general x1, matrix products, weigh_decode(): jnp.einsum('grk,gkc->grc', weights, cache_values, preferred_element_type=...  11.2 us
    dot_general x1, matrix products, local(): jnp.einsum('grc,gkc->grk', queries, cache_keys, preferred_element_type=jn...  10.4 us
    select_n x1, local copies, waits for them, and re-layouts, local(): jnp.where(live_mask[..., None], incoming, jnp.zeros((), jnp.bfloat16))  10.1 us
  transfers between devices with their start and end apart: 4, of which 4 were waited for; matrix products, arithmetic and copies ran while one was open for 5% of the time, Pallas kernels for 0%

commit v1 on v0

v1 whole, which is shorter than its diff:
```python
import functools

import jax
import jax.numpy as jnp
from jax import lax
from jax.experimental import pallas as pl
from jax.experimental.pallas import tpu as pltpu
from jax.sharding import PartitionSpec as P

LATENT_CHANNELS = 512
MOST_STRIPES = 12
HEADS = 128
NEG_FILL = -1e30
SCORE_SCALE = 192.0 ** (-0.5)
CHUNKS = (144, 144, 144, 144)
KEY_TILE = 8
NOTE_LANES = 128

SMEM = pl.BlockSpec(memory_space=pltpu.SMEM)
ANY = pl.BlockSpec(memory_space=pl.ANY)
VMEM = pl.BlockSpec(memory_space=pltpu.VMEM)


def params(**more):
    return pltpu.CompilerParams(vmem_limit_bytes=48 << 20, **more)


def request_for(lengths, assignment, group, target):
    first, count, before = 0, 0, 0
    for r in range(4):
        here = lengths[group, r]
        hit = assignment[group, r] == target
        first = jnp.where(hit, before, first)
        count = jnp.where(hit, here, count)
        before = before + here
    return first, count


def request_of(lengths, assignment, padding, group, stripe):
    target, empty, before = 0, 0, 0
    for r in range(4):
        after = before + lengths[group, r]
        inside = jnp.logical_and(stripe >= before, stripe < after)
        target = jnp.where(inside, assignment[group, r], target)
        empty = jnp.where(stripe == after - 1, padding[group, r], empty)
        before = after
    return target, empty


def dequantize_kernel(start, per_step, total, place, lengths, assignment, padding, packed, scale, channels, values, out):
    rows = packed.shape[0]
    step = pl.program_id(0)
    _, empty = request_of(lengths, assignment, padding, place[0], place[1])
    ids = lax.broadcasted_iota(jnp.int32, (rows, 16), 0) + start
    ones = jnp.ones((16, 128), jnp.bfloat16)
    tokens = lax.broadcasted_iota(jnp.int32, (rows, 128), 1)
    for b in range(per_step):
        onehot = (ids == channels[b : b + 1, :]).astype(jnp.bfloat16)
        spread = jnp.dot(
            onehot, jnp.concatenate([values[b], ones], axis=1), preferred_element_type=jnp.float32
        )
        plain = packed[:, b * 128 : (b + 1) * 128].astype(jnp.float32) * scale[0, :, b : b + 1]
        latent = jnp.where(spread[:, 128:] > 0.5, spread[:, :128], plain)
        if b == per_step - 1:
            limit = jnp.where(step == total - 1, 128 - empty, 128)
            latent = jnp.where(tokens < limit, latent, 0.0)
        out[b] = latent.astype(jnp.bfloat16)


def dequantize(start, rows, place, lengths, assignment, padding, packed, scale, channels, values):
    blocks = channels.shape[0]
    per_step = 8
    steps = blocks // per_step
    assert start % rows == 0
    return pl.pallas_call(
        functools.partial(dequantize_kernel, start, per_step, steps),
        grid=(steps,),
        out_shape=jax.ShapeDtypeStruct((blocks, rows, 128), jnp.bfloat16),
        in_specs=[
            SMEM,
            SMEM,
            SMEM,
            SMEM,
            pl.BlockSpec((rows, per_step * 128), lambda i: (start // rows, i)),
            pl.BlockSpec((1, rows, per_step), lambda i: (i, start // rows, 0)),
            pl.BlockSpec((per_step, 16), lambda i: (i, 0)),
            pl.BlockSpec((per_step, 16, 128), lambda i: (i, 0, 0)),
        ],
        out_specs=pl.BlockSpec((per_step, rows, 128), lambda i: (i, 0, 0)),
        compiler_params=params(),
        cost_estimate=pl.CostEstimate(
            flops=4 * blocks * rows * 128, bytes_accessed=4 * blocks * rows * 128, transcendentals=0
        ),
        name="dequantize",
    )(place, lengths, assignment, padding, packed, scale, channels, values)


def start_request(first, count, stripes, target, zeros, sem):
    for v in range(MOST_STRIPES):

        @pl.when(v < count)
        def _():
            pltpu.make_async_copy(stripes.at[first + v], target(v), sem).start()

        @pl.when(v >= count)
        def _():
            pltpu.make_async_copy(zeros, target(v), sem).start()


def pack_kernel(place, lengths, assignment, stripes, out1, out2, out3, zeros, sems):
    zeros[...] = jnp.zeros_like(zeros)
    outs = (out1, out2, out3)
    for d in (1, 2, 3):
        first, count = request_for(lengths, assignment, place[0], lax.rem(place[0] + d, 4))
        start_request(first, count, stripes, lambda v, o=outs[d - 1]: o.at[v], zeros, sems.at[d - 1])
    for d in (1, 2, 3):
        pltpu.make_async_copy(outs[d - 1], outs[d - 1], sems.at[d - 1]).wait()


def pack(place, lengths, assignment, stripes):
    rows = stripes.shape[1]
    one = jax.ShapeDtypeStruct((MOST_STRIPES, rows, 128), jnp.bfloat16)
    return pl.pallas_call(
        pack_kernel,
        out_shape=(one, one, one),
        in_specs=[SMEM, SMEM, SMEM, ANY],
        out_specs=(ANY, ANY, ANY),
        scratch_shapes=[pltpu.VMEM((rows, 128), jnp.bfloat16), pltpu.SemaphoreType.DMA((3,))],
        compiler_params=params(),
        cost_estimate=pl.CostEstimate(flops=0, bytes_accessed=4 * 36 * rows * 128, transcendentals=0),
        name="pack",
    )(place, lengths, assignment, stripes)


def place_kernel(start, first_chunk, *refs):
    if first_chunk:
        place, lengths, assignment, stripes, in1, in2, in3, out, zeros, sems = refs
    else:
        place, lengths, assignment, stripes, in1, in2, in3, _, out, zeros, sems = refs
    rows = stripes.shape[1]
    zeros[...] = jnp.zeros_like(zeros)
    here = place[0]

    def slot(d):
        return out.at[lax.rem(here + 4 - d, 4), :, pl.ds(start, rows), :]

    copies = [pltpu.make_async_copy(x, slot(d), sems.at[d]) for d, x in ((1, in1), (2, in2), (3, in3))]
    for copy in copies:
        copy.start()
    first, count = request_for(lengths, assignment, here, here)
    start_request(first, count, stripes, lambda v: out.at[here, v, pl.ds(start, rows), :], zeros, sems.at[0])
    for copy in copies:
        copy.wait()
    pltpu.make_async_copy(slot(0), slot(0), sems.at[0]).wait()


def put(start, place, lengths, assignment, stripes, arrived, cache):
    rows = stripes.shape[1]
    more = () if cache is None else (cache,)
    return pl.pallas_call(
        functools.partial(place_kernel, start, cache is None),
        out_shape=jax.ShapeDtypeStruct((4, MOST_STRIPES, sum(CHUNKS), 128), jnp.bfloat16),
        in_specs=[SMEM, SMEM, SMEM, ANY, ANY, ANY, ANY] + [ANY] * len(more),
        out_specs=ANY,
        input_output_aliases={7: 0} if more else {},
        scratch_shapes=[pltpu.VMEM((rows, 128), jnp.bfloat16), pltpu.SemaphoreType.DMA((4,))],
        compiler_params=params(),
        cost_estimate=pl.CostEstimate(flops=0, bytes_accessed=4 * 48 * rows * 128, transcendentals=0),
        name="put",
    )(place, lengths, assignment, stripes, *arrived, *more)


def pick_kernel(place, lengths, assignment, padding, pieces, out):
    for s in range(32):
        target, _ = request_of(lengths, assignment, padding, place[0], s)
        out[s] = pieces[target]


def pick(place, lengths, assignment, padding, pieces):
    return pl.pallas_call(
        pick_kernel,
        out_shape=jax.ShapeDtypeStruct((32,) + pieces.shape[1:], pieces.dtype),
        in_specs=[SMEM, SMEM, SMEM, SMEM, VMEM],
        out_specs=VMEM,
        compiler_params=params(),
        name="pick",
    )(place, lengths, assignment, padding, pieces)


def in_three(x):
    high = x.astype(jnp.bfloat16)
    rest = x - high.astype(jnp.float32)
    middle = rest.astype(jnp.bfloat16)
    low = (rest - middle.astype(jnp.float32)).astype(jnp.bfloat16)
    return high, middle, low


def attend_kernel(steps, place, lengths, assignment, padding, queries, *refs):
    keys, (out, peak, total, weighted) = refs[: len(CHUNKS)], refs[len(CHUNKS) :]
    step = pl.program_id(0)
    _, empty = request_of(lengths, assignment, padding, place[0], place[1])

    @pl.when(step == 0)
    def _():
        peak[...] = jnp.full_like(peak, NEG_FILL)
        total[...] = jnp.zeros_like(total)
        weighted[...] = jnp.zeros_like(weighted)

    latent = jnp.concatenate(
        [jnp.concatenate([k[b] for k in keys], axis=0) for b in range(KEY_TILE)], axis=1
    )
    scores = jnp.dot(queries[...], latent, preferred_element_type=jnp.float32) * SCORE_SCALE
    columns = lax.broadcasted_iota(jnp.int32, scores.shape, 1)
    limit = jnp.where(step == steps - 1, KEY_TILE * 128 - empty, KEY_TILE * 128)
    scores = jnp.where(columns < limit, scores, NEG_FILL)
    before = peak[...]
    now = jnp.maximum(before, jnp.max(scores, axis=1, keepdims=True))
    shrink = jnp.exp(before - now)
    weights = jnp.exp(scores - now[:, :1]).astype(jnp.bfloat16)
    total[...] = total[...] * shrink + jnp.sum(weights.astype(jnp.float32), axis=1, keepdims=True)
    weighted[...] = weighted[...] * shrink[:, :1] + lax.dot_general(
        weights, latent[:LATENT_CHANNELS], (((1,), (1,)), ((), ())), preferred_element_type=jnp.float32
    )
    peak[...] = now

    @pl.when(step == steps - 1)
    def _():
        out[:, :LATENT_CHANNELS] = weighted[...].astype(jnp.bfloat16)
        lane = lax.broadcasted_iota(jnp.int32, peak.shape, 1)
        note = jnp.zeros(peak.shape, jnp.float32)
        for i, part in enumerate(in_three(peak[...]) + in_three(total[...])):
            note = jnp.where(lane == i, part.astype(jnp.float32), note)
        out[:, LATENT_CHANNELS:] = note.astype(jnp.bfloat16)


def attend(place, lengths, assignment, padding, queries, keys):
    rows = queries.shape[0]
    blocks = keys[0].shape[0]
    steps = blocks // KEY_TILE
    width = LATENT_CHANNELS + NOTE_LANES
    return pl.pallas_call(
        functools.partial(attend_kernel, steps),
        grid=(steps,),
        out_shape=jax.ShapeDtypeStruct((rows, width), jnp.bfloat16),
        in_specs=[SMEM, SMEM, SMEM, SMEM, pl.BlockSpec(queries.shape, lambda i: (0, 0))]
        + [pl.BlockSpec((KEY_TILE,) + k.shape[1:], lambda i: (i, 0, 0)) for k in keys],
        out_specs=pl.BlockSpec((rows, width), lambda i: (0, 0)),
        scratch_shapes=[
            pltpu.VMEM((rows, 128), jnp.float32),
            pltpu.VMEM((rows, 128), jnp.float32),
            pltpu.VMEM((rows, LATENT_CHANNELS), jnp.float32),
        ],
        compiler_params=params(),
        cost_estimate=pl.CostEstimate(
            flops=2 * rows * blocks * 128 * (576 + 512), bytes_accessed=6 << 20, transcendentals=rows * blocks * 128
        ),
        name="attend",
    )(place, lengths, assignment, padding, queries, *keys)


def join_kernel(place, lengths, assignment, padding, partials, out):
    stripes, rows, _ = partials.shape
    note = partials[:, :, LATENT_CHANNELS:].astype(jnp.float32)
    peak = note[:, :, 0:1] + note[:, :, 1:2] + note[:, :, 2:3]
    total = note[:, :, 3:4] + note[:, :, 4:5] + note[:, :, 5:6]
    stripe = lax.broadcasted_iota(jnp.int32, peak.shape, 0)
    lane = lax.broadcasted_iota(jnp.int32, (rows, NOTE_LANES), 1)
    values = partials[:, :, :LATENT_CHANNELS].astype(jnp.float32)
    for target in range(4):
        first, count = request_for(lengths, assignment, place[0], target)
        inside = jnp.logical_and(stripe >= first, stripe < first + count)
        top = jnp.max(jnp.where(inside, peak, NEG_FILL), axis=0)
        factor = jnp.where(inside, jnp.exp(jnp.where(inside, peak, NEG_FILL) - top[None]), 0.0)
        out[target, :, :LATENT_CHANNELS] = jnp.sum(values * factor, axis=0)
        whole = jnp.sum(total * factor, axis=0)
        out[target, :, LATENT_CHANNELS:] = jnp.where(lane == 0, top, jnp.where(lane == 1, whole, 0.0))


def join(place, lengths, assignment, padding, partials):
    return pl.pallas_call(
        join_kernel,
        out_shape=jax.ShapeDtypeStruct((4,) + partials.shape[1:], jnp.float32),
        in_specs=[SMEM, SMEM, SMEM, SMEM, VMEM],
        out_specs=VMEM,
        compiler_params=params(),
        name="join",
    )(place, lengths, assignment, padding, partials)


def finish(joined, queries, fresh, seq_here):
    own = joined.shape[1]
    row_start = seq_here * own
    own_queries = lax.dynamic_slice_in_dim(queries, row_start, own, 1)
    scores = (
        jnp.einsum("yeu,ynu->yen", own_queries, fresh, preferred_element_type=jnp.float32) * SCORE_SCALE
    )
    row_step = (row_start + jnp.arange(own, dtype=jnp.int32)) // HEADS
    col_step = jnp.arange(fresh.shape[1], dtype=jnp.int32)
    scores = jnp.where((col_step[None, :] <= row_step[:, None])[None], scores, NEG_FILL)
    cache_peak = joined[:, :, LATENT_CHANNELS]
    cache_total = joined[:, :, LATENT_CHANNELS + 1]
    peak = jnp.maximum(cache_peak, jnp.max(scores, axis=2))
    shrink = jnp.exp(cache_peak - peak)
    weights = jnp.exp(scores - peak[:, :, None]).astype(jnp.bfloat16)
    weighted = joined[:, :, :LATENT_CHANNELS] * shrink[:, :, None] + jnp.einsum(
        "oep,opf->oef", weights, fresh[:, :, :LATENT_CHANNELS], preferred_element_type=jnp.float32
    )
    total = cache_total * shrink + jnp.sum(weights.astype(jnp.float32), axis=2)
    return (weighted / total[:, :, None]).astype(jnp.bfloat16)


def local(
    compressed,
    block_channel_scale,
    outlier_channels,
    outlier_values,
    lengths,
    assignment,
    padding,
    queries,
    decode_token_latent,
):
    group_here = lax.axis_index("grp")
    seq_here = lax.axis_index("seq")
    place = jnp.stack([group_here, seq_here]).astype(jnp.int32)
    packed = compressed.T
    scale = block_channel_scale.reshape(4, 8, -1).transpose(0, 2, 1)

    turned = queries.transpose(0, 2, 1)
    piece = lax.dynamic_slice(
        turned, (0, (seq_here // 4) * 72, (seq_here % 4) * 128), (4, 72, 128)
    )
    pieces = lax.all_to_all(piece, "grp", split_axis=0, concat_axis=0, tiled=True)
    picked = pick(place, lengths, assignment, padding, pieces)
    gathered = lax.all_to_all(picked, "seq", split_axis=0, concat_axis=0, tiled=True)
    own_queries = gathered.reshape(8, 4, 72, 128).transpose(1, 3, 0, 2).reshape(512, 576)

    starts = [sum(CHUNKS[:i]) for i in range(len(CHUNKS))]
    latent = [
        dequantize(
            start, rows, place, lengths, assignment, padding, packed, scale, outlier_channels, outlier_values
        )
        for start, rows in zip(starts, CHUNKS)
    ]
    cache = None
    for start, chunk in zip(starts, latent):
        stripes = lax.all_to_all(chunk, "seq", split_axis=0, concat_axis=0, tiled=True)
        outgoing = pack(place, lengths, assignment, stripes)
        arrived = [
            lax.ppermute(x, "grp", [(i, (i + d) % 4) for i in range(4)]) for d, x in zip((1, 2, 3), outgoing)
        ]
        cache = put(start, place, lengths, assignment, stripes, arrived, cache)

    partial = attend(place, lengths, assignment, padding, own_queries, latent)
    partials = lax.all_to_all(
        partial.reshape(32, 16, partial.shape[1]), "seq", split_axis=0, concat_axis=0, tiled=True
    )
    joined = lax.all_to_all(
        join(place, lengths, assignment, padding, partials), "grp", split_axis=0, concat_axis=0, tiled=True
    )
    attended = finish(joined, queries, decode_token_latent, seq_here)
    return cache.transpose(0, 1, 3, 2)[None, :, None], attended


def solution(mesh):
    placed = (
        P(("grp", "seq"), None),
        P(("grp", "seq"), None),
        P(("grp", "seq"), None),
        P(("grp", "seq"), None, None),
        P(),
        P(),
        P(),
        P("grp", None, None),
        P("grp", None, None),
    )
    return jax.shard_map(
        local,
        mesh=mesh,
        in_specs=placed,
        out_specs=(P("grp", None, "seq", None, None, None), P("grp", "seq", None)),
        check_vma=False,
    )
```

time: 450 us -> 450 us (level)
  the two profiles are of different devices: /device:TPU:1 before, /device:TPU:14 now
where the time goes in v1:
time: 450 us; the launch traced here: 457 us
  Pallas kernels  286 us (64%)
  starting transfers between devices  80 us (18%)
  local copies, waits for them, and re-layouts  43.7 us (10%)
  waiting for transfers between devices  20.9 us (5%)
  blocking collectives  18.4 us (4%)
    pallas_call x4, Pallas kernels, put(): pl.pallas_call(functools.partial(place_kernel, start, cache is None), out...  208 us
    pallas_call x4, Pallas kernels, pack(): pl.pallas_call(pack_kernel, out_shape=(one, one, one), in_specs=[SMEM, SM...  53 us
    unnamed x96, local copies, waits for them, and re-layouts  36.1 us
    ppermute x12, starting transfers between devices, local(): lax.ppermute(x, 'grp', [(i, (i + d) % 4) for i in range(4)])  34.2 us
    all_to_all x4, starting transfers between devices, local(): lax.all_to_all(chunk, 'seq', split_axis=0, concat_axis=0, tiled=True)  26.7 us
    all_to_all x1, blocking collectives, local(): lax.all_to_all(partial.reshape(32, 16, partial.shape[1]), 'seq', split_ax...  18.4 us
    all_to_all x4, waiting for transfers between devices, local(): lax.all_to_all(chunk, 'seq', split_axis=0, concat_axis=0, tiled=True)  16.7 us
    pallas_call x4, Pallas kernels, dequantize(): pl.pallas_call(functools.partial(dequantize_kernel, start, per_step, step...  11.7 us
  transfers between devices with their start and end apart: 19, of which 4 were waited for; matrix products, arithmetic and copies ran while one was open for 3% of the time, Pallas kernels for 53%

profile of v1, /device:TPU:14, one launch (start us, length us, event | category | flops | bytes accessed | tf_op | source)
XLA Modules:
  0.0 457.4 jit_solution(16075447285647376078)
XLA Ops:
  2.9 4.8 %all-to-all-start.4 = ((bf16[4,72,128]{2,1,0:T(8,128)(2,1)}), bf16[4,72,128]{2,1,0:T(8,128)(2,1)S(1)}, u32[]{:S(2)}, u32[]{:S(2)}) async-start(bf16[4,72,128]{2,1,0:T(8,128)(2,1)} %dynamic-slice_bitcast_fusion), calls=%async_computation.4 | async-start | bytes 147456 | tf_op jit(solution)/shard_map/all_to_all | solution.py:333
  7.8 3.5 all-to-all-done.4.pieces
  15.1 8.6 %all-to-all-start.5 = ((bf16[32,72,128]{2,1,0:T(8,128)(2,1)}), bf16[32,72,128]{2,1,0:T(8,128)(2,1)}, u32[]{:S(2)}, u32[]{:S(2)}) async-start(bf16[32,72,128]{2,1,0:T(8,128)(2,1)} %pick.1), calls=%async_computation.5 | async-start | bytes 1179648 | tf_op jit(solution)/shard_map/all_to_all | solution.py:335
  29.3 2.9 dequantize.7.refs_0_
  33.9 6.8 %all-to-all-start.3 = ((bf16[32,144,128]{2,1,0:T(8,128)(2,1)}), bf16[32,144,128]{2,1,0:T(8,128)(2,1)}, u32[]{:S(2)}, u32[]{:S(2)}) async-start(bf16[32,144,128]{2,1,0:T(8,128)(2,1)} %copy-done.3), calls=%async_computation.3 | async-start | bytes 2359296 | tf_op jit(solution)/shard_map/all_to_all | solution.py:347
  48.3 8.3 %all-to-all-done.3.stripes.refs_3_ = bf16[32,144,128]{2,1,0:T(8,128)(2,1)} async-done(((bf16[32,144,128]{2,1,0:T(8,128)(2,1)}), bf16[32,144,128]{2,1,0:T(8,128)(2,1)}, u32[]{:S(2)}, u32[]{:S(2)}) %all-to-all-start.3) | async-done | bytes 1179680 | tf_op jit(solution)/shard_map/all_to_all | solution.py:347
  56.7 7.1 %all-to-all-start.2 = ((bf16[32,144,128]{2,1,0:T(8,128)(2,1)}), bf16[32,144,128]{2,1,0:T(8,128)(2,1)}, u32[]{:S(2)}, u32[]{:S(2)}) async-start(bf16[32,144,128]{2,1,0:T(8,128)(2,1)} %copy-done.5), calls=%async_computation.2 | async-start | bytes 2359296 | tf_op jit(solution)/shard_map/all_to_all | solution.py:347
  71.3 8.4 %all-to-all-done.2.stripes.refs_3_ = bf16[32,144,128]{2,1,0:T(8,128)(2,1)} async-done(((bf16[32,144,128]{2,1,0:T(8,128)(2,1)}), bf16[32,144,128]{2,1,0:T(8,128)(2,1)}, u32[]{:S(2)}, u32[]{:S(2)}) %all-to-all-start.2) | async-done | bytes 1179680 | tf_op jit(solution)/shard_map/all_to_all | solution.py:347
  79.7 7.0 %all-to-all-start.1 = ((bf16[32,144,128]{2,1,0:T(8,128)(2,1)}), bf16[32,144,128]{2,1,0:T(8,128)(2,1)}, u32[]{:S(2)}, u32[]{:S(2)}) async-start(bf16[32,144,128]{2,1,0:T(8,128)(2,1)} %copy-done.7), calls=%async_computation.1 | async-start | bytes 2359296 | tf_op jit(solution)/shard_map/all_to_all | solution.py:347
  103.8 9.8 %attend.1 = bf16[512,640]{1,0:T(8,128)(2,1)S(1)} custom-call(s32[2]{0:T(128)S(1)} %copy-done.34, s32[4,4]{1,0:T(4,128)S(1)} %copy-done.22, s32[4,4]{1,0:T(4,128)S(1)} %copy-done.28, s32[4,4]{1,0:T(4,128)S(1)} %copy-done.40, bf16[512,576]{1,0:T(8,128)(2,1)S(1)} %copy-done.15, bf16[32,144,128]{2,1,0:T(8,128)(2,1)S(1)} %copy-done.4, ...), custom_call_target="tpu_custom_call" | custom-call | flops 4563402752 | bytes 6291456 | tf_op jit(solution)/shard_map/attend/pallas_call | solution.py:241
  114.5 18.4 %all_to_all.40.partials = bf16[32,16,640]{2,1,0:T(8,128)(2,1)} all-to-all(bf16[32,16,640]{2,1,0:T(8,128)(2,1)} %bitcast.29), channel_id=1, replica_groups=mesh['grp'=4,'seq'=32] {'seq'}, dimensions={0} | all-to-all | bytes 1310720 | tf_op jit(solution)/shard_map/all_to_all | solution.py:355
  132.9 5.8 %all-to-all-start = ((bf16[32,144,128]{2,1,0:T(8,128)(2,1)}), bf16[32,144,128]{2,1,0:T(8,128)(2,1)S(1)}, u32[]{:S(2)}, u32[]{:S(2)}) async-start(bf16[32,144,128]{2,1,0:T(8,128)(2,1)} %copy-done.1), calls=%async_computation | async-start | bytes 2359296 | tf_op jit(solution)/shard_map/all_to_all | solution.py:347
  138.7 20.1 %pack.7 = (bf16[12,144,128]{2,1,0:T(8,128)(2,1)S(1)}, bf16[12,144,128]{2,1,0:T(8,128)(2,1)}, bf16[12,144,128]{2,1,0:T(8,128)(2,1)}) custom-call(s32[2]{0:T(128)S(1)} %copy-done.34, s32[4,4]{1,0:T(4,128)S(1)} %copy-done.22, s32[4,4]{1,0:T(4,128)S(1)} %copy-done.28, bf16[32,144,128]{2,1,0:T(8,128)(2,1)} %all-to-all-done.3.stripes.refs_3_), custom_call_target="tpu_custom_call" | custom-call | bytes 2654208 | tf_op jit(solution)/shard_map/pack/pallas_call | solution.py:123
  166.9 24.1 %pack.6 = (bf16[12,144,128]{2,1,0:T(8,128)(2,1)}, bf16[12,144,128]{2,1,0:T(8,128)(2,1)}, bf16[12,144,128]{2,1,0:T(8,128)(2,1)}) custom-call(s32[2]{0:T(128)S(1)} %copy-done.34, s32[4,4]{1,0:T(4,128)S(1)} %copy-done.22, s32[4,4]{1,0:T(4,128)S(1)} %copy-done.28, bf16[32,144,128]{2,1,0:T(8,128)(2,1)} %all-to-all-done.2.stripes.refs_3_), custom_call_target="tpu_custom_call" | custom-call | bytes 2654208 | tf_op jit(solution)/shard_map/pack/pallas_call | solution.py:123
  191.0 11.0 %collective-permute-start.6 = (bf16[12,144,128]{2,1,0:T(8,128)(2,1)}, bf16[12,144,128]{2,1,0:T(8,128)(2,1)}, u32[]{:S(2)}, u32[]{:S(2)}) collective-permute-start(bf16[12,144,128]{2,1,0:T(8,128)(2,1)} %get-tuple-element.20), channel_id=1, source_target_pairs={{0,32},{32,64},{64,96},{96,0},{1,33},{33,65},{65,97},{97,1},{2,34}... | collective-permute-start | bytes 1327112 | tf_op jit(solution)/shard_map/ppermute | solution.py:350
  202.0 6.2 %pack.5 = (bf16[12,144,128]{2,1,0:T(8,128)(2,1)}, bf16[12,144,128]{2,1,0:T(8,128)(2,1)S(1)}, bf16[12,144,128]{2,1,0:T(8,128)(2,1)S(1)}) custom-call(s32[2]{0:T(128)S(1)} %copy-done.34, s32[4,4]{1,0:T(4,128)S(1)} %copy-done.22, s32[4,4]{1,0:T(4,128)S(1)} %copy-done.28, bf16[32,144,128]{2,1,0:T(8,128)(2,1)} %all-to-all-done.1.stripes.refs_3_), custom_call_target="tpu_custom_call" | custom-call | bytes 2654208 | tf_op jit(solution)/shard_map/pack/pallas_call | solution.py:123
  209.8 5.4 %collective-permute-start.8 = (bf16[12,144,128]{2,1,0:T(8,128)(2,1)}, bf16[12,144,128]{2,1,0:T(8,128)(2,1)}, u32[]{:S(2)}, u32[]{:S(2)}) collective-permute-start(bf16[12,144,128]{2,1,0:T(8,128)(2,1)} %get-tuple-element.22), channel_id=1, source_target_pairs={{0,96},{32,0},{64,32},{96,64},{1,97},{33,1},{65,33},{97,65},{2,98}... | collective-permute-start | bytes 1327112 | tf_op jit(solution)/shard_map/ppermute | solution.py:350
  215.2 3.9 collective-permute-start.3
  223.2 5.7 %all-to-all-start.7 = ((f32[4,16,640]{2,1,0:T(8,128)}), f32[4,16,640]{2,1,0:T(8,128)}, u32[]{:S(2)}, u32[]{:S(2)}) async-start(f32[4,16,640]{2,1,0:T(8,128)} %copy-done.16), calls=%async_computation.7 | async-start | bytes 327680 | tf_op jit(solution)/shard_map/all_to_all | solution.py:358
  238.7 3.2 collective-permute-start
  249.2 55.3 %put.4.refs_7_ = bf16[4,12,576,128]{3,2,1,0:T(8,128)(2,1)} custom-call(s32[2]{0:T(128)S(1)} %copy-done.34, s32[4,4]{1,0:T(4,128)S(1)} %copy-done.22, s32[4,4]{1,0:T(4,128)S(1)} %copy-done.28, bf16[32,144,128]{2,1,0:T(8,128)(2,1)} %all-to-all-done.3.stripes.refs_3_, bf16[12,144,128]{2,1,0:T(8,128)(2,1)} %collective-permute-done.9.refs_4_, ...), custom_call_target="tpu_custom_call" | custom-call | bytes 3538944 | tf_op jit(solution)/shard_map/put/pallas_call | solution.py:160
  304.5 55.4 %put.5.refs_7_ = bf16[4,12,576,128]{3,2,1,0:T(8,128)(2,1)} custom-call(s32[2]{0:T(128)S(1)} %copy-done.34, s32[4,4]{1,0:T(4,128)S(1)} %copy-done.22, s32[4,4]{1,0:T(4,128)S(1)} %copy-done.28, bf16[32,144,128]{2,1,0:T(8,128)(2,1)} %all-to-all-done.2.stripes.refs_3_, ...), custom_call_target="tpu_custom_call", output_to_operand_aliasing={{}: (7, {})} | custom-call | bytes 3538944 | tf_op jit(solution)/shard_map/put/pallas_call | solution.py:160
  359.9 55.4 %put.6.refs_7_ = bf16[4,12,576,128]{3,2,1,0:T(8,128)(2,1)} custom-call(s32[2]{0:T(128)S(1)} %copy-done.34, s32[4,4]{1,0:T(4,128)S(1)} %copy-done.22, s32[4,4]{1,0:T(4,128)S(1)} %copy-done.28, bf16[32,144,128]{2,1,0:T(8,128)(2,1)} %all-to-all-done.1.stripes.refs_3_, ...), custom_call_target="tpu_custom_call", output_to_operand_aliasing={{}: (7, {})} | custom-call | bytes 3538944 | tf_op jit(solution)/shard_map/put/pallas_call | solution.py:160
  415.3 42.0 %put.7 = bf16[4,12,576,128]{3,2,1,0:T(8,128)(2,1)} custom-call(s32[2]{0:T(128)S(1)} %copy-done.34, s32[4,4]{1,0:T(4,128)S(1)} %copy-done.22, s32[4,4]{1,0:T(4,128)S(1)} %copy-done.28, bf16[32,144,128]{2,1,0:T(8,128)(2,1)S(1)} %all-to-all-done.stripes.refs_3_, bf16[12,144,128]{2,1,0:T(8,128)(2,1)} %collective-permute-done.refs_4_, ...), custom_call_target="tpu_custom_call", output_to_operand_aliasing={{}: (7, {})} | custom-call | bytes 3538944 | tf_op jit(solution)/shard_map/put/pallas_call | solution.py:160
  (140 shorter events, 77.2 us)
Async XLA Ops:
  2.9 8.4 %all-to-all-start.4 = ((bf16[4,72,128]{2,1,0:T(8,128)(2,1)}), bf16[4,72,128]{2,1,0:T(8,128)(2,1)S(1)}, u32[]{:S(2)}, u32[]{:S(2)}) async-start(bf16[4,72,128]{2,1,0:T(8,128)(2,1)} %dynamic-slice_bitcast_fusion), calls=%async_computation.4 | async-start | bytes 147456 | tf_op jit(solution)/shard_map/all_to_all | solution.py:333
  7.8 15.9 %copy-start.29 = (s32[2]{0:T(128)}, s32[2]{0:T(128)S(1)}, u32[]{:S(2)}) copy-start(s32[2]{0:T(128)S(1)} %pad_add_fusion.place.refs_0_) | copy-start | bytes 28
  15.1 18.9 %all-to-all-start.5 = ((bf16[32,72,128]{2,1,0:T(8,128)(2,1)}), bf16[32,72,128]{2,1,0:T(8,128)(2,1)}, u32[]{:S(2)}, u32[]{:S(2)}) async-start(bf16[32,72,128]{2,1,0:T(8,128)(2,1)} %pick.1), calls=%async_computation.5 | async-start | bytes 1179648 | tf_op jit(solution)/shard_map/all_to_all | solution.py:335
  33.9 22.7 %all-to-all-start.3 = ((bf16[32,144,128]{2,1,0:T(8,128)(2,1)}), bf16[32,144,128]{2,1,0:T(8,128)(2,1)}, u32[]{:S(2)}, u32[]{:S(2)}) async-start(bf16[32,144,128]{2,1,0:T(8,128)(2,1)} %copy-done.3), calls=%async_computation.3 | async-start | bytes 2359296 | tf_op jit(solution)/shard_map/all_to_all | solution.py:347
  56.7 23.0 %all-to-all-start.2 = ((bf16[32,144,128]{2,1,0:T(8,128)(2,1)}), bf16[32,144,128]{2,1,0:T(8,128)(2,1)}, u32[]{:S(2)}, u32[]{:S(2)}) async-start(bf16[32,144,128]{2,1,0:T(8,128)(2,1)} %copy-done.5), calls=%async_computation.2 | async-start | bytes 2359296 | tf_op jit(solution)/shard_map/all_to_all | solution.py:347
  79.7 34.8 %all-to-all-start.1 = ((bf16[32,144,128]{2,1,0:T(8,128)(2,1)}), bf16[32,144,128]{2,1,0:T(8,128)(2,1)}, u32[]{:S(2)}, u32[]{:S(2)}) async-start(bf16[32,144,128]{2,1,0:T(8,128)(2,1)} %copy-done.7), calls=%async_computation.1 | async-start | bytes 2359296 | tf_op jit(solution)/shard_map/all_to_all | solution.py:347
  94.3 4.6 %copy-start.28 = (s32[4,4]{1,0:T(4,128)S(1)}, s32[4,4]{1,0:T(4,128)}, u32[]{:S(2)}) copy-start(s32[4,4]{1,0:T(4,128)} %assignment.21) | copy-start | bytes 196
  94.3 4.6 %copy-start.34 = (s32[2]{0:T(128)S(1)}, s32[2]{0:T(128)}, u32[]{:S(2)}) copy-start(s32[2]{0:T(128)} %copy-done.29) | copy-start | bytes 28
  94.3 4.6 %copy-start.40 = (s32[4,4]{1,0:T(4,128)S(1)}, s32[4,4]{1,0:T(4,128)}, u32[]{:S(2)}) copy-start(s32[4,4]{1,0:T(4,128)} %padding.13) | copy-start | bytes 196
  94.3 4.6 %copy-start.2 = (bf16[32,144,128]{2,1,0:T(8,128)(2,1)S(1)}, bf16[32,144,128]{2,1,0:T(8,128)(2,1)}, u32[]{:S(2)}) copy-start(bf16[32,144,128]{2,1,0:T(8,128)(2,1)} %copy-done.1) | copy-start | bytes 3538948
  132.9 90.3 %all-to-all-start = ((bf16[32,144,128]{2,1,0:T(8,128)(2,1)}), bf16[32,144,128]{2,1,0:T(8,128)(2,1)S(1)}, u32[]{:S(2)}, u32[]{:S(2)}) async-start(bf16[32,144,128]{2,1,0:T(8,128)(2,1)} %copy-done.1), calls=%async_computation | async-start | bytes 2359296 | tf_op jit(solution)/shard_map/all_to_all | solution.py:347
  159.5 50.3 %collective-permute-start.10 = (bf16[12,144,128]{2,1,0:T(8,128)(2,1)}, bf16[12,144,128]{2,1,0:T(8,128)(2,1)}, u32[]{:S(2)}, u32[]{:S(2)}) collective-permute-start(bf16[12,144,128]{2,1,0:T(8,128)(2,1)} %get-tuple-element.24), channel_id=1, source_target_pairs={{0,64},{32,96},{64,0},{96,32},{1,65},{33,97},{65,1},{97,33},{2,66}... | collective-permute-start | bytes 1327112 | tf_op jit(solution)/shard_map/ppermute | solution.py:350
  161.3 53.9 %collective-permute-start.11 = (bf16[12,144,128]{2,1,0:T(8,128)(2,1)}, bf16[12,144,128]{2,1,0:T(8,128)(2,1)}, u32[]{:S(2)}, u32[]{:S(2)}) collective-permute-start(bf16[12,144,128]{2,1,0:T(8,128)(2,1)} %get-tuple-element.25), channel_id=1, source_target_pairs={{0,96},{32,0},{64,32},{96,64},{1,97},{33,1},{65,33},{97,65},{2,98}... | collective-permute-start | bytes 1327112 | tf_op jit(solution)/shard_map/ppermute | solution.py:350
  164.1 73.0 %collective-permute-start.9 = (bf16[12,144,128]{2,1,0:T(8,128)(2,1)}, bf16[12,144,128]{2,1,0:T(8,128)(2,1)}, u32[]{:S(2)}, u32[]{:S(2)}) collective-permute-start(bf16[12,144,128]{2,1,0:T(8,128)(2,1)} %copy-done.46), channel_id=1, source_target_pairs={{0,32},{32,64},{64,96},{96,0},{1,33},{33,65},{65,97},{97,1},{2,34}... | collective-permute-start | bytes 1327112 | tf_op jit(solution)/shard_map/ppermute | solution.py:350
  191.0 47.8 %collective-permute-start.6 = (bf16[12,144,128]{2,1,0:T(8,128)(2,1)}, bf16[12,144,128]{2,1,0:T(8,128)(2,1)}, u32[]{:S(2)}, u32[]{:S(2)}) collective-permute-start(bf16[12,144,128]{2,1,0:T(8,128)(2,1)} %get-tuple-element.20), channel_id=1, source_target_pairs={{0,32},{32,64},{64,96},{96,0},{1,33},{33,65},{65,97},{97,1},{2,34}... | collective-permute-start | bytes 1327112 | tf_op jit(solution)/shard_map/ppermute | solution.py:350
  202.0 36.7 %collective-permute-start.7 = (bf16[12,144,128]{2,1,0:T(8,128)(2,1)}, bf16[12,144,128]{2,1,0:T(8,128)(2,1)}, u32[]{:S(2)}, u32[]{:S(2)}) collective-permute-start(bf16[12,144,128]{2,1,0:T(8,128)(2,1)} %get-tuple-element.21), channel_id=1, source_target_pairs={{0,64},{32,96},{64,0},{96,32},{1,65},{33,97},{65,1},{97,33},{2,66}... | collective-permute-start | bytes 1327112 | tf_op jit(solution)/shard_map/ppermute | solution.py:350
  209.8 32.2 %collective-permute-start.8 = (bf16[12,144,128]{2,1,0:T(8,128)(2,1)}, bf16[12,144,128]{2,1,0:T(8,128)(2,1)}, u32[]{:S(2)}, u32[]{:S(2)}) collective-permute-start(bf16[12,144,128]{2,1,0:T(8,128)(2,1)} %get-tuple-element.22), channel_id=1, source_target_pairs={{0,96},{32,0},{64,32},{96,64},{1,97},{33,1},{65,33},{97,65},{2,98}... | collective-permute-start | bytes 1327112 | tf_op jit(solution)/shard_map/ppermute | solution.py:350
  215.2 27.6 %collective-permute-start.3 = (bf16[12,144,128]{2,1,0:T(8,128)(2,1)}, bf16[12,144,128]{2,1,0:T(8,128)(2,1)}, u32[]{:S(2)}, u32[]{:S(2)}) collective-permute-start(bf16[12,144,128]{2,1,0:T(8,128)(2,1)} %get-tuple-element.17), channel_id=1, source_target_pairs={{0,32},{32,64},{64,96},{96,0},{1,33},{33,65},{65,97},{97,1},{2,34}... | collective-permute-start | bytes 1327112 | tf_op jit(solution)/shard_map/ppermute | solution.py:350
  223.2 13.1 %all-to-all-start.7 = ((f32[4,16,640]{2,1,0:T(8,128)}), f32[4,16,640]{2,1,0:T(8,128)}, u32[]{:S(2)}, u32[]{:S(2)}) async-start(f32[4,16,640]{2,1,0:T(8,128)} %copy-done.16), calls=%async_computation.7 | async-start | bytes 327680 | tf_op jit(solution)/shard_map/all_to_all | solution.py:358
  237.2 122.7 %collective-permute-start.4 = (bf16[12,144,128]{2,1,0:T(8,128)(2,1)}, bf16[12,144,128]{2,1,0:T(8,128)(2,1)}, u32[]{:S(2)}, u32[]{:S(2)}) collective-permute-start(bf16[12,144,128]{2,1,0:T(8,128)(2,1)} %copy-done.42), channel_id=1, source_target_pairs={{0,64},{32,96},{64,0},{96,32},{1,65},{33,97},{65,1},{97,33},{2,66}... | collective-permute-start | bytes 1327112 | tf_op jit(solution)/shard_map/ppermute | solution.py:350
  238.7 121.2 %collective-permute-start.5 = (bf16[12,144,128]{2,1,0:T(8,128)(2,1)}, bf16[12,144,128]{2,1,0:T(8,128)(2,1)}, u32[]{:S(2)}, u32[]{:S(2)}) collective-permute-start(bf16[12,144,128]{2,1,0:T(8,128)(2,1)} %copy-done.41), channel_id=1, source_target_pairs={{0,96},{32,0},{64,32},{96,64},{1,97},{33,1},{65,33},{97,65},{2,98}... | collective-permute-start | bytes 1327112 | tf_op jit(solution)/shard_map/ppermute | solution.py:350
  238.7 176.5 %collective-permute-start = (bf16[12,144,128]{2,1,0:T(8,128)(2,1)}, bf16[12,144,128]{2,1,0:T(8,128)(2,1)}, u32[]{:S(2)}, u32[]{:S(2)}) collective-permute-start(bf16[12,144,128]{2,1,0:T(8,128)(2,1)} %copy-done.45), channel_id=1, source_target_pairs={{0,32},{32,64},{64,96},{96,0},{1,33},{33,65},{65,97},{97,1},{2,34}... | collective-permute-start | bytes 1327112 | tf_op jit(solution)/shard_map/ppermute | solution.py:350
  242.0 173.3 %collective-permute-start.1 = (bf16[12,144,128]{2,1,0:T(8,128)(2,1)}, bf16[12,144,128]{2,1,0:T(8,128)(2,1)}, u32[]{:S(2)}, u32[]{:S(2)}) collective-permute-start(bf16[12,144,128]{2,1,0:T(8,128)(2,1)} %copy-done.44), channel_id=1, source_target_pairs={{0,64},{32,96},{64,0},{96,32},{1,65},{33,97},{65,1},{97,33},{2,66}... | collective-permute-start | bytes 1327112 | tf_op jit(solution)/shard_map/ppermute | solution.py:350
  242.8 172.4 %collective-permute-start.2 = (bf16[12,144,128]{2,1,0:T(8,128)(2,1)}, bf16[12,144,128]{2,1,0:T(8,128)(2,1)}, u32[]{:S(2)}, u32[]{:S(2)}) collective-permute-start(bf16[12,144,128]{2,1,0:T(8,128)(2,1)} %copy-done.43), channel_id=1, source_target_pairs={{0,96},{32,0},{64,32},{96,64},{1,97},{33,1},{65,33},{97,65},{2,98}... | collective-permute-start | bytes 1327112 | tf_op jit(solution)/shard_map/ppermute | solution.py:350
  (42 other events, 39.1 us)

commit v2 on v1

v2 whole, which is shorter than its diff:
```python
import functools

import jax
import jax.numpy as jnp
from jax import lax
from jax.experimental import pallas as pl
from jax.experimental.pallas import tpu as pltpu
from jax.sharding import PartitionSpec as P

LATENT_CHANNELS = 512
MOST_STRIPES = 12
HEADS = 128
NEG_FILL = -1e30
SCORE_SCALE = 192.0 ** (-0.5)
CHUNKS = (336, 240)
KEY_TILE = 8
NOTE_LANES = 128

SMEM = pl.BlockSpec(memory_space=pltpu.SMEM)
HBM = pl.BlockSpec(memory_space=pltpu.HBM)
VMEM = pl.BlockSpec(memory_space=pltpu.VMEM)


def params(megabytes=16):
    return pltpu.CompilerParams(vmem_limit_bytes=megabytes << 20)


def moved(steps, rows):
    size = 2 * steps * MOST_STRIPES * rows * 128
    return pl.CostEstimate(flops=0, bytes_accessed=2 * size, transcendentals=0)


def request_for(table, target):
    first, count, before = 0, 0, 0
    for r in range(4):
        here = table[2 + r]
        hit = table[6 + r] == target
        first = jnp.where(hit, before, first)
        count = jnp.where(hit, here, count)
        before = before + here
    return first, count


def request_here(table):
    target, empty, before = 0, 0, 0
    for r in range(4):
        after = before + table[2 + r]
        inside = jnp.logical_and(table[1] >= before, table[1] < after)
        target = jnp.where(inside, table[6 + r], target)
        empty = jnp.where(table[1] == after - 1, table[10 + r], empty)
        before = after
    return target, empty


def dequantize_kernel(start, per_step, total, table, packed, scale, channels, values, out, scales, marks):
    rows = packed.shape[0]
    width = per_step * 16
    step = pl.program_id(0)

    @pl.when(step == 0)
    def _():
        mark = channels[...].astype(jnp.float32).T
        ids = lax.broadcasted_iota(jnp.int32, scale.shape, 1).astype(jnp.float32)
        plain = scale[...]
        for k in range(16):
            plain = jnp.where(ids == mark[:, k : k + 1], 0.0, plain)
        turned = plain.T[start : start + rows]
        for i in range(total):
            scales[i] = turned[:, i * per_step : (i + 1) * per_step]
            marks[i] = jnp.concatenate([mark[i * per_step + b : i * per_step + b + 1] for b in range(per_step)], axis=1)

    _, empty = request_here(table)
    ids = (lax.broadcasted_iota(jnp.int32, (rows, width), 0) + start).astype(jnp.float32)
    onehot = (ids == marks[step]).astype(jnp.bfloat16)
    flat = values[...].reshape(width, 128)
    block = lax.broadcasted_iota(jnp.int32, (width, 128), 0) // 16
    spread = jnp.concatenate([jnp.where(block == b, flat, jnp.zeros_like(flat)) for b in range(per_step)], axis=1)
    outliers = jnp.dot(onehot, spread, preferred_element_type=jnp.float32)
    tokens = lax.broadcasted_iota(jnp.int32, (rows, 128), 1)
    here = scales[step]
    for b in range(per_step):
        lanes = slice(b * 128, (b + 1) * 128)
        latent = packed[:, lanes].astype(jnp.float32) * here[:, b : b + 1] + outliers[:, lanes]
        if b == per_step - 1:
            limit = jnp.where(step == total - 1, 128 - empty, 128)
            latent = jnp.where(tokens < limit, latent, 0.0)
        out[b] = latent.astype(jnp.bfloat16)


def dequantize(start, rows, table, packed, scale, channels, values):
    blocks = scale.shape[0]
    per_step = 8
    steps = blocks // per_step
    return pl.pallas_call(
        functools.partial(dequantize_kernel, start, per_step, steps),
        grid=(steps,),
        out_shape=pltpu.HBM((blocks, rows, 128), jnp.bfloat16),
        in_specs=[
            SMEM,
            pl.BlockSpec((pl.Element(rows), pl.Element(per_step * 128)), lambda i: (start, i * per_step * 128)),
            pl.BlockSpec(scale.shape, lambda i: (0, 0)),
            pl.BlockSpec(channels.shape, lambda i: (0, 0)),
            pl.BlockSpec((per_step, 16, 128), lambda i: (i, 0, 0)),
        ],
        out_specs=pl.BlockSpec((per_step, rows, 128), lambda i: (i, 0, 0)),
        scratch_shapes=[
            pltpu.VMEM((steps, rows, per_step), jnp.float32),
            pltpu.VMEM((steps, 1, per_step * 16), jnp.float32),
        ],
        compiler_params=params(60),
        cost_estimate=pl.CostEstimate(
            flops=4 * blocks * rows * 128, bytes_accessed=4 * blocks * rows * 128, transcendentals=0
        ),
        name="dequantize",
    )(table, packed, scale, channels, values)


def collect(table, steps, stripes, targets, zeros, sems):
    zeros[...] = jnp.zeros_like(zeros)
    for i, d in enumerate(steps):
        first, count = request_for(table, lax.rem(table[0] + d, 4))
        for v in range(MOST_STRIPES):

            @pl.when(v < count)
            def _():
                pltpu.make_async_copy(stripes.at[first + v], targets[i].at[v], sems.at[i]).start()

            @pl.when(v >= count)
            def _():
                pltpu.make_async_copy(zeros, targets[i].at[v], sems.at[i]).start()

    for i in range(len(steps)):
        pltpu.make_async_copy(targets[i], targets[i], sems.at[i]).wait()


def collect_scratch(steps, rows):
    return [pltpu.VMEM((rows, 128), jnp.bfloat16), pltpu.SemaphoreType.DMA((steps,))]


def pack_kernel(steps, table, stripes, *refs):
    outs, scratch = refs[: len(steps)], refs[len(steps) :]
    collect(table, steps, stripes, outs, *scratch)


def pack(table, stripes, steps):
    rows = stripes.shape[1]
    one = pltpu.HBM((MOST_STRIPES, rows, 128), jnp.bfloat16)
    return pl.pallas_call(
        functools.partial(pack_kernel, steps),
        out_shape=(one,) * len(steps),
        in_specs=[SMEM, VMEM],
        out_specs=(HBM,) * len(steps),
        scratch_shapes=collect_scratch(len(steps), rows),
        compiler_params=params(),
        cost_estimate=moved(len(steps), rows),
        name="pack",
    )(table, stripes)


def own_kernel(start, table, stripes, *refs):
    out, scratch = refs[-3], refs[-2:]
    rows = stripes.shape[1]
    collect(table, (0,), stripes, [out.at[table[0], :, pl.ds(start, rows), :]], *scratch)


def own(start, table, stripes, cache):
    rows = stripes.shape[1]
    more = () if cache is None else (cache,)
    return pl.pallas_call(
        functools.partial(own_kernel, start),
        out_shape=jax.ShapeDtypeStruct((4, MOST_STRIPES, sum(CHUNKS), 128), jnp.bfloat16),
        in_specs=[SMEM, VMEM] + [HBM] * len(more),
        out_specs=HBM,
        input_output_aliases={2: 0} if more else {},
        scratch_shapes=collect_scratch(1, rows),
        compiler_params=params(),
        cost_estimate=moved(1, rows),
        name="own",
    )(table, stripes, *more)


def put_kernel(start, steps, table, *refs):
    arrived, (_, out, sems) = refs[: len(steps)], refs[len(steps) :]
    rows = arrived[0].shape[1]
    copies = [
        pltpu.make_async_copy(
            arrived[i], out.at[lax.rem(table[0] + 4 - d, 4), :, pl.ds(start, rows), :], sems.at[i]
        )
        for i, d in enumerate(steps)
    ]
    for copy in copies:
        copy.start()
    for copy in copies:
        copy.wait()


def put(start, table, steps, arrived, cache):
    rows = arrived[0].shape[1]
    return pl.pallas_call(
        functools.partial(put_kernel, start, steps),
        out_shape=jax.ShapeDtypeStruct(cache.shape, cache.dtype),
        in_specs=[SMEM] + [VMEM] * len(steps) + [HBM],
        out_specs=HBM,
        input_output_aliases={len(steps) + 1: 0},
        scratch_shapes=[pltpu.SemaphoreType.DMA((len(steps),))],
        compiler_params=params(),
        cost_estimate=moved(len(steps), rows),
        name="put",
    )(table, *arrived, cache)


def split_kernel(table, queries, *refs):
    outs, (held, in_sems, out_sems) = refs[:3], refs[3:]
    come = [
        pltpu.make_async_copy(queries.at[lax.rem(table[0] + d + 1, 4)], held.at[d], in_sems.at[d]) for d in range(3)
    ]
    leave = [pltpu.make_async_copy(held.at[d], outs[d], out_sems.at[d]) for d in range(3)]
    for copy in come:
        copy.start()
    for d in range(3):
        come[d].wait()
        leave[d].start()
    for copy in leave:
        copy.wait()


def split(table, queries):
    one = pltpu.HBM(queries.shape[1:], queries.dtype)
    return pl.pallas_call(
        split_kernel,
        out_shape=(one,) * 3,
        in_specs=[SMEM, HBM],
        out_specs=(HBM,) * 3,
        scratch_shapes=[
            pltpu.VMEM((3,) + queries.shape[1:], queries.dtype),
            pltpu.SemaphoreType.DMA((3,)),
            pltpu.SemaphoreType.DMA((3,)),
        ],
        compiler_params=params(),
        name="split",
    )(table, pltpu.with_memory_space_constraint(queries, pltpu.HBM))


def in_three(x):
    high = x.astype(jnp.bfloat16)
    rest = x - high.astype(jnp.float32)
    middle = rest.astype(jnp.bfloat16)
    low = (rest - middle.astype(jnp.float32)).astype(jnp.bfloat16)
    return high, middle, low


def attend_kernel(steps, table, *refs):
    sources, keys = refs[:4], refs[4 : 4 + len(CHUNKS)]
    out, peak, total, weighted, turned, queries, sem = refs[4 + len(CHUNKS) :]
    step = pl.program_id(0)
    target, empty = request_here(table)

    @pl.when(step == 0)
    def _():
        for d in range(4):
            source = sources[d].at[table[0]] if d == 0 else sources[d]

            @pl.when(target == lax.rem(table[0] + 4 - d, 4))
            def _():
                pltpu.make_async_copy(source, turned, sem).start()

        pltpu.make_async_copy(sources[1], turned, sem).wait()
        queries[...] = turned[...].T
        peak[...] = jnp.full_like(peak, NEG_FILL)
        total[...] = jnp.zeros_like(total)
        weighted[...] = jnp.zeros_like(weighted)

    latent = jnp.concatenate(
        [jnp.concatenate([k[b] for k in keys], axis=0) for b in range(KEY_TILE)], axis=1
    )
    scores = jnp.dot(queries[...], latent, preferred_element_type=jnp.float32) * SCORE_SCALE
    columns = lax.broadcasted_iota(jnp.int32, scores.shape, 1)
    limit = jnp.where(step == steps - 1, KEY_TILE * 128 - empty, KEY_TILE * 128)
    scores = jnp.where(columns < limit, scores, NEG_FILL)
    before = peak[...]
    now = jnp.maximum(before, jnp.max(scores, axis=1, keepdims=True))
    shrink = jnp.exp(before - now)
    weights = jnp.exp(scores - now[:, :1]).astype(jnp.bfloat16)
    total[...] = total[...] * shrink + jnp.sum(weights.astype(jnp.float32), axis=1, keepdims=True)
    weighted[...] = weighted[...] * shrink[:, :1] + lax.dot_general(
        weights, latent[:LATENT_CHANNELS], (((1,), (1,)), ((), ())), preferred_element_type=jnp.float32
    )
    peak[...] = now

    @pl.when(step == steps - 1)
    def _():
        out[:, :LATENT_CHANNELS] = weighted[...].astype(jnp.bfloat16)
        lane = lax.broadcasted_iota(jnp.int32, peak.shape, 1)
        note = jnp.zeros(peak.shape, jnp.float32)
        for i, part in enumerate(in_three(peak[...]) + in_three(total[...])):
            note = jnp.where(lane == i, part.astype(jnp.float32), note)
        out[:, LATENT_CHANNELS:] = note.astype(jnp.bfloat16)


def attend(table, queries, pieces, keys):
    channels, rows = queries.shape[1:]
    queries, *pieces = [pltpu.with_memory_space_constraint(x, pltpu.HBM) for x in (queries, *pieces)]
    keys = [pltpu.with_memory_space_constraint(k, pltpu.HBM) for k in keys]
    blocks = keys[0].shape[0]
    steps = blocks // KEY_TILE
    width = LATENT_CHANNELS + NOTE_LANES
    return pl.pallas_call(
        functools.partial(attend_kernel, steps),
        grid=(steps,),
        out_shape=jax.ShapeDtypeStruct((rows, width), jnp.bfloat16),
        in_specs=[SMEM] + [HBM] * 4
        + [pl.BlockSpec((KEY_TILE,) + k.shape[1:], lambda i: (i, 0, 0)) for k in keys],
        out_specs=pl.BlockSpec((rows, width), lambda i: (0, 0)),
        scratch_shapes=[
            pltpu.VMEM((rows, 128), jnp.float32),
            pltpu.VMEM((rows, 128), jnp.float32),
            pltpu.VMEM((rows, LATENT_CHANNELS), jnp.float32),
            pltpu.VMEM((channels, rows), jnp.bfloat16),
            pltpu.VMEM((rows, channels), jnp.bfloat16),
            pltpu.SemaphoreType.DMA,
        ],
        compiler_params=params(40),
        cost_estimate=pl.CostEstimate(
            flops=16 * rows * blocks * 128 * (576 + 512), bytes_accessed=6 << 20, transcendentals=rows * blocks * 128
        ),
        name="attend",
    )(table, queries, *pieces, *keys)


def join_kernel(table, partials, out):
    stripes, rows, _ = partials.shape
    note = partials[:, :, LATENT_CHANNELS:].astype(jnp.float32)
    peak = note[:, :, 0:1] + note[:, :, 1:2] + note[:, :, 2:3]
    total = note[:, :, 3:4] + note[:, :, 4:5] + note[:, :, 5:6]
    stripe = lax.broadcasted_iota(jnp.int32, peak.shape, 0)
    lane = lax.broadcasted_iota(jnp.int32, (rows, NOTE_LANES), 1)
    values = partials[:, :, :LATENT_CHANNELS].astype(jnp.float32)
    for target in range(4):
        first, count = request_for(table, target)
        inside = jnp.logical_and(stripe >= first, stripe < first + count)
        top = jnp.max(jnp.where(inside, peak, NEG_FILL), axis=0)
        factor = jnp.where(inside, jnp.exp(jnp.where(inside, peak, NEG_FILL) - top[None]), 0.0)
        out[target, :, :LATENT_CHANNELS] = jnp.sum(values * factor, axis=0)
        whole = jnp.sum(total * factor, axis=0)
        out[target, :, LATENT_CHANNELS:] = jnp.where(lane == 0, top, jnp.where(lane == 1, whole, 0.0))


def join(table, partials):
    return pl.pallas_call(
        join_kernel,
        out_shape=jax.ShapeDtypeStruct((4,) + partials.shape[1:], jnp.float32),
        in_specs=[SMEM, VMEM],
        out_specs=VMEM,
        compiler_params=params(),
        name="join",
    )(table, partials)


def finish(joined, queries, fresh, seq_here):
    own = joined.shape[1]
    row_start = seq_here * own
    own_queries = lax.dynamic_slice_in_dim(queries, row_start, own, 1)
    scores = (
        jnp.einsum("yeu,ynu->yen", own_queries, fresh, preferred_element_type=jnp.float32) * SCORE_SCALE
    )
    row_step = (row_start + jnp.arange(own, dtype=jnp.int32)) // HEADS
    col_step = jnp.arange(fresh.shape[1], dtype=jnp.int32)
    scores = jnp.where((col_step[None, :] <= row_step[:, None])[None], scores, NEG_FILL)
    cache_peak = joined[:, :, LATENT_CHANNELS]
    cache_total = joined[:, :, LATENT_CHANNELS + 1]
    peak = jnp.maximum(cache_peak, jnp.max(scores, axis=2))
    shrink = jnp.exp(cache_peak - peak)
    weights = jnp.exp(scores - peak[:, :, None]).astype(jnp.bfloat16)
    weighted = joined[:, :, :LATENT_CHANNELS] * shrink[:, :, None] + jnp.einsum(
        "oep,opf->oef", weights, fresh[:, :, :LATENT_CHANNELS], preferred_element_type=jnp.float32
    )
    total = cache_total * shrink + jnp.sum(weights.astype(jnp.float32), axis=2)
    return (weighted / total[:, :, None]).astype(jnp.bfloat16)


def over_seq(x):
    return lax.all_to_all(x, "seq", split_axis=0, concat_axis=0, tiled=True)


def along(x, d):
    return lax.ppermute(x, "grp", [(i, (i + d) % 4) for i in range(4)])


def local(
    compressed,
    block_channel_scale,
    outlier_channels,
    outlier_values,
    lengths,
    assignment,
    padding,
    queries,
    decode_token_latent,
):
    group_here = lax.axis_index("grp")
    seq_here = lax.axis_index("seq")
    rows_here = [lax.dynamic_index_in_dim(x, group_here, 0, keepdims=False) for x in (lengths, assignment, padding)]
    table = jnp.concatenate([jnp.stack([group_here, seq_here]).astype(jnp.int32)] + rows_here)
    packed = compressed.T
    channels = outlier_channels.T

    starts = [sum(CHUNKS[:i]) for i in range(len(CHUNKS))]
    last = len(CHUNKS) - 1
    latent = [
        dequantize(start, rows, table, packed, block_channel_scale, channels, outlier_values)
        for start, rows in zip(starts, CHUNKS)
    ]
    turned = queries.transpose(0, 2, 1)
    pieces = [along(x, d) for d, x in zip((1, 2, 3), split(table, turned))]

    stripes, *pieces = lax.optimization_barrier((over_seq(latent[0]), *pieces))
    partial = attend(table, turned, pieces, latent)
    cache = None
    for i, start in enumerate(starts):
        (two,) = pack(table, stripes, (2,))
        if i < last:
            stripes, chunk, two = lax.optimization_barrier((stripes, latent[i + 1], two))
        else:
            stripes, two = lax.optimization_barrier((stripes, two))
        one, three = pack(table, stripes, (1, 3))
        two = along(two, 2)
        if i == 0:
            one, two, three, partial = lax.optimization_barrier((one, two, three, partial))
        else:
            one, two, three = lax.optimization_barrier((one, two, three))
        step = [along(one, 1), two, along(three, 3)]
        if i < last:
            cache = own(start, table, stripes, cache)
            cache = put(start, table, (2,), step[1:2], cache)
            stripes = over_seq(chunk)
            if i == last - 1:
                partial, cache = lax.optimization_barrier((partial, cache, stripes))[:2]
                partials = over_seq(partial.reshape(32, 16, -1))
                stripes, partials, *step = lax.optimization_barrier((stripes, partials, *step))
            else:
                stripes, cache, *step = lax.optimization_barrier((stripes, cache, *step))
            before = (start, step)

    joined = lax.all_to_all(join(table, partials), "grp", split_axis=0, concat_axis=0, tiled=True)
    cache = put(before[0], table, (1, 3), before[1][::2], cache)
    cache = own(start, table, stripes, cache)
    cache = put(start, table, (2,), step[1:2], cache)
    joined, cache = lax.optimization_barrier((joined, cache))
    cache = put(start, table, (1, 3), step[::2], cache)
    attended = finish(joined, queries, decode_token_latent, seq_here)
    return cache.transpose(0, 1, 3, 2)[None, :, None], attended


def solution(mesh):
    placed = (
        P(("grp", "seq"), None),
        P(("grp", "seq"), None),
        P(("grp", "seq"), None),
        P(("grp", "seq"), None, None),
        P(),
        P(),
        P(),
        P("grp", None, None),
        P("grp", None, None),
    )
    return jax.shard_map(
        local,
        mesh=mesh,
        in_specs=placed,
        out_specs=(P("grp", None, "seq", None, None, None), P("grp", "seq", None)),
        check_vma=False,
    )
```

time: 450 us -> 152 us (0.34)
  the two profiles are of different devices: /device:TPU:14 before, /device:TPU:1 now
where the time goes in v2:
time: 152 us; the launch traced here: 150 us
  waiting for transfers between devices  58.6 us (39%)
  Pallas kernels  49.1 us (32%)
  starting transfers between devices  36.9 us (24%)
  matrix products  2.27 us (1%)
  local copies, waits for them, and re-layouts  2.23 us (1%)
    ppermute x9, waiting for transfers between devices, along(): return lax.ppermute(x, 'grp', [(i, (i + d) % 4) for i in range(4)])  48.6 us
    all_to_all x3, starting transfers between devices, over_seq(): return lax.all_to_all(x, 'seq', split_axis=0, concat_axis=0, tiled=True)  19.5 us
    ppermute x9, starting transfers between devices, along(): return lax.ppermute(x, 'grp', [(i, (i + d) % 4) for i in range(4)])  13.6 us
    pallas_call x1, Pallas kernels, attend(): pl.pallas_call(functools.partial(attend_kernel, steps), grid=(steps,), ou...  12.6 us
    pallas_call x2, Pallas kernels, dequantize(): pl.pallas_call(functools.partial(dequantize_kernel, start, per_step, step...  10.5 us
    all_to_all x3, waiting for transfers between devices, over_seq(): return lax.all_to_all(x, 'seq', split_axis=0, concat_axis=0, tiled=True)  9.96 us
    pallas_call x4, Pallas kernels, pack(): pl.pallas_call(functools.partial(pack_kernel, steps), out_shape=(one,) *...  8.62 us
    pallas_call x4, Pallas kernels, put(): pl.pallas_call(functools.partial(put_kernel, start, steps), out_shape=jax...  8.17 us
  transfers between devices with their start and end apart: 13, of which 9 were waited for; matrix products, arithmetic and copies ran while one was open for 2% of the time, Pallas kernels for 25%

profile of v2, /device:TPU:1, one launch (start us, length us, event | category | flops | bytes accessed | tf_op | source)
XLA Modules:
  0.0 150.2 jit_solution(869801463942148583)
XLA Ops:
  2.7 5.5 %dequantize.2.refs_4_ = bf16[32,336,128]{2,1,0:T(8,128)(2,1)} custom-call(s32[14]{0:T(128)} %concatenate.3.table, bf16[576,4096]{1,0:T(8,128)(2,1)} %bitcast.21, f32[32,576]{1,0:T(8,128)} %scale.3, s32[16,32]{1,0:T(8,128)} %bitcast.25, bf16[32,16,128]{2,1,0:T(8,128)(2,1)} %values.3), custom_call_target="tpu_custom_call" | custom-call | flops 5505024 | bytes 5505024 | tf_op jit(solution)/shard_map/dequantize/pallas_call | solution.py:94
  8.2 9.6 %all-to-all-start = ((bf16[32,336,128]{2,1,0:T(8,128)(2,1)}), bf16[32,336,128]{2,1,0:T(8,128)(2,1)S(1)}, u32[]{:S(2)}, u32[]{:S(2)}) async-start(bf16[32,336,128]{2,1,0:T(8,128)(2,1)} %dequantize.2.refs_4_), calls=%async_computation | async-start | bytes 5505024 | tf_op jit(solution)/shard_map/all_to_all | solution.py:382
  17.8 2.9 %split.1 = (bf16[576,512]{1,0:T(8,128)(2,1)}, bf16[576,512]{1,0:T(8,128)(2,1)}, bf16[576,512]{1,0:T(8,128)(2,1)}) custom-call(s32[14]{0:T(128)S(1)} %copy-done.1, bf16[4,576,512]{2,1,0:T(8,128)(2,1)} %bitcast.23), custom_call_target="tpu_custom_call" | custom-call | tf_op jit(solution)/shard_map/split/pallas_call | solution.py:229
  21.9 2.4 %collective-permute-start.1 = (bf16[576,512]{1,0:T(8,128)(2,1)}, bf16[576,512]{1,0:T(8,128)(2,1)}, u32[]{:S(2)}, u32[]{:S(2)}) collective-permute-start(bf16[576,512]{1,0:T(8,128)(2,1)} %get-tuple-element.34), channel_id=1, source_target_pairs={{0,64},{32,96},{64,0},{96,32},{1,65},{33,97},{65,1},{97,33},{2,66}... | collective-permute-start | bytes 1769480 | tf_op jit(solution)/shard_map/ppermute | solution.py:386
  25.6 5.0 %dequantize.3.refs_5_ = bf16[32,240,128]{2,1,0:T(8,128)(2,1)} custom-call(s32[14]{0:T(128)} %concatenate.3.table, bf16[576,4096]{1,0:T(8,128)(2,1)} %bitcast.22, f32[32,576]{1,0:T(8,128)} %scale.3, s32[16,32]{1,0:T(8,128)} %bitcast.26, bf16[32,16,128]{2,1,0:T(8,128)(2,1)} %values.3), custom_call_target="tpu_custom_call" | custom-call | flops 3932160 | bytes 3932160 | tf_op jit(solution)/shard_map/dequantize/pallas_call | solution.py:94
  30.5 6.3 %collective-permute-done.refs_1_ = bf16[576,512]{1,0:T(8,128)(2,1)S(1)} collective-permute-done((bf16[576,512]{1,0:T(8,128)(2,1)}, bf16[576,512]{1,0:T(8,128)(2,1)S(1)}, u32[]{:S(2)}, u32[]{:S(2)}) %collective-permute-start) | collective-permute-done | bytes 589856 | tf_op jit(solution)/shard_map/ppermute | solution.py:386
  36.9 13.7 %collective-permute-done.1.refs_2_ = bf16[576,512]{1,0:T(8,128)(2,1)} collective-permute-done((bf16[576,512]{1,0:T(8,128)(2,1)}, bf16[576,512]{1,0:T(8,128)(2,1)}, u32[]{:S(2)}, u32[]{:S(2)}) %collective-permute-start.1) | collective-permute-done | bytes 589856 | tf_op jit(solution)/shard_map/ppermute | solution.py:386
  50.6 2.5 %all-to-all-done.stripes = bf16[32,336,128]{2,1,0:T(8,128)(2,1)S(1)} async-done(((bf16[32,336,128]{2,1,0:T(8,128)(2,1)}), bf16[32,336,128]{2,1,0:T(8,128)(2,1)S(1)}, u32[]{:S(2)}, u32[]{:S(2)}) %all-to-all-start) | async-done | bytes 2752544 | tf_op jit(solution)/shard_map/all_to_all | solution.py:382
  54.6 2.8 %collective-permute-start.3 = (bf16[12,336,128]{2,1,0:T(8,128)(2,1)}, bf16[12,336,128]{2,1,0:T(8,128)(2,1)}, u32[]{:S(2)}, u32[]{:S(2)}) collective-permute-start(bf16[12,336,128]{2,1,0:T(8,128)(2,1)} %pack.4), channel_id=1, source_target_pairs={{0,64},{32,96},{64,0},{96,32},{1,65},{33,97},{65,1},{97,33},{2,66}... | collective-permute-start | bytes 3096584 | tf_op jit(solution)/shard_map/ppermute | solution.py:386
  57.4 5.6 %all-to-all-start.1 = ((bf16[32,240,128]{2,1,0:T(8,128)(2,1)}), bf16[32,240,128]{2,1,0:T(8,128)(2,1)}, u32[]{:S(2)}, u32[]{:S(2)}) async-start(bf16[32,240,128]{2,1,0:T(8,128)(2,1)} %dequantize.3.refs_5_), calls=%async_computation.1 | async-start | bytes 3932160 | tf_op jit(solution)/shard_map/all_to_all | solution.py:382
  63.0 12.6 %attend.1 = bf16[512,640]{1,0:T(8,128)(2,1)} custom-call(s32[14]{0:T(128)S(1)} %copy-done.2, bf16[4,576,512]{2,1,0:T(8,128)(2,1)} %bitcast.24, bf16[576,512]{1,0:T(8,128)(2,1)} %copy-done.4, bf16[576,512]{1,0:T(8,128)(2,1)} %collective-permute-done.1.refs_2_, bf16[576,512]{1,0:T(8,128)(2,1)} %collective-permute-done.2.refs_3_, ...), custom_call_target="tpu_custom_call" | custom-call | flops 36507222016 | bytes 6291456 | tf_op jit(solution)/shard_map/attend/pallas_call | solution.py:307
  86.3 3.8 %all-to-all-done.1.stripes = bf16[32,240,128]{2,1,0:T(8,128)(2,1)} async-done(((bf16[32,240,128]{2,1,0:T(8,128)(2,1)}), bf16[32,240,128]{2,1,0:T(8,128)(2,1)}, u32[]{:S(2)}, u32[]{:S(2)}) %all-to-all-start.1) | async-done | bytes 1966112 | tf_op jit(solution)/shard_map/all_to_all | solution.py:382
  90.1 4.4 %all-to-all-start.2 = ((bf16[32,16,640]{2,1,0:T(8,128)(2,1)}), bf16[32,16,640]{2,1,0:T(8,128)(2,1)S(1)}, u32[]{:S(2)}, u32[]{:S(2)}) async-start(bf16[32,16,640]{2,1,0:T(8,128)(2,1)} %bitcast.8), calls=%async_computation.2 | async-start | bytes 1310720 | tf_op jit(solution)/shard_map/all_to_all | solution.py:382
  94.4 9.4 %collective-permute-done.4.refs_0_ = bf16[12,336,128]{2,1,0:T(8,128)(2,1)} collective-permute-done((bf16[12,336,128]{2,1,0:T(8,128)(2,1)}, bf16[12,336,128]{2,1,0:T(8,128)(2,1)}, u32[]{:S(2)}, u32[]{:S(2)}) %collective-permute-start.4) | collective-permute-done | bytes 1032224 | tf_op jit(solution)/shard_map/ppermute | solution.py:386
  103.8 3.7 %all-to-all-done.2.partials = bf16[32,16,640]{2,1,0:T(8,128)(2,1)S(1)} async-done(((bf16[32,16,640]{2,1,0:T(8,128)(2,1)}), bf16[32,16,640]{2,1,0:T(8,128)(2,1)S(1)}, u32[]{:S(2)}, u32[]{:S(2)}) %all-to-all-start.2) | async-done | bytes 655392 | tf_op jit(solution)/shard_map/all_to_all | solution.py:382
  107.5 2.4 %pack.6 = bf16[12,240,128]{2,1,0:T(8,128)(2,1)} custom-call(s32[14]{0:T(128)S(1)} %copy-done.2, bf16[32,240,128]{2,1,0:T(8,128)(2,1)} %all-to-all-done.1.stripes), custom_call_target="tpu_custom_call" | custom-call | bytes 1474560 | tf_op jit(solution)/shard_map/pack/pallas_call | solution.py:148
  110.5 2.7 %pack.7 = (bf16[12,240,128]{2,1,0:T(8,128)(2,1)}, bf16[12,240,128]{2,1,0:T(8,128)(2,1)}) custom-call(s32[14]{0:T(128)S(1)} %copy-done.2, bf16[32,240,128]{2,1,0:T(8,128)(2,1)} %all-to-all-done.1.stripes), custom_call_target="tpu_custom_call" | custom-call | bytes 2949120 | tf_op jit(solution)/shard_map/pack/pallas_call | solution.py:148
  113.2 2.4 %join.1 = f32[4,16,640]{2,1,0:T(8,128)} custom-call(s32[14]{0:T(128)S(1)} %copy-done.2, bf16[32,16,640]{2,1,0:T(8,128)(2,1)S(1)} %all-to-all-done.2.partials), custom_call_target="tpu_custom_call" | custom-call | tf_op jit(solution)/shard_map/join/pallas_call | solution.py:349
  115.6 3.8 %all-to-all-start.3 = ((f32[4,16,640]{2,1,0:T(8,128)}), f32[4,16,640]{2,1,0:T(8,128)S(1)}, u32[]{:S(2)}, u32[]{:S(2)}) async-start(f32[4,16,640]{2,1,0:T(8,128)} %join.1), calls=%async_computation.3 | async-start | bytes 327680 | tf_op jit(solution)/shard_map/all_to_all | solution.py:444
  119.4 10.7 %collective-permute-done.6.refs_0_ = bf16[12,240,128]{2,1,0:T(8,128)(2,1)S(1)} collective-permute-done((bf16[12,240,128]{2,1,0:T(8,128)(2,1)}, bf16[12,240,128]{2,1,0:T(8,128)(2,1)S(1)}, u32[]{:S(2)}, u32[]{:S(2)}) %collective-permute-start.6) | collective-permute-done | bytes 737312 | tf_op jit(solution)/shard_map/ppermute | solution.py:386
  130.2 2.5 %collective-permute-start.8 = (bf16[12,240,128]{2,1,0:T(8,128)(2,1)}, bf16[12,240,128]{2,1,0:T(8,128)(2,1)S(1)}, u32[]{:S(2)}, u32[]{:S(2)}) collective-permute-start(bf16[12,240,128]{2,1,0:T(8,128)(2,1)} %get-tuple-element.56), channel_id=1, source_target_pairs={{0,96},{32,0},{64,32},{96,64},{1,97},{33,1},{65,33},{97,65},{2,98}... | collective-permute-start | bytes 2211848 | tf_op jit(solution)/shard_map/ppermute | solution.py:386
  134.2 2.9 %put.5.refs_0_ = bf16[4,12,576,128]{3,2,1,0:T(8,128)(2,1)} custom-call(s32[14]{0:T(128)S(1)} %copy-done.2, bf16[12,336,128]{2,1,0:T(8,128)(2,1)} %collective-permute-done.4.refs_0_, bf16[12,336,128]{2,1,0:T(8,128)(2,1)} %collective-permute-done.5.refs_1_, bf16[4,12,576,128]{3,2,1,0:T(8,128)(2,1)} %put.4.refs_2_), custom_call_target="tpu_custom_call", output_to_operand_aliasing={{}: (3, {})} | custom-call | bytes 4128768 | tf_op jit(solution)/shard_map/put/pallas_call | solution.py:199
  137.1 2.4 %own.3.refs_1_ = bf16[4,12,576,128]{3,2,1,0:T(8,128)(2,1)} custom-call(s32[14]{0:T(128)S(1)} %copy-done.2, bf16[32,240,128]{2,1,0:T(8,128)(2,1)} %all-to-all-done.1.stripes, bf16[4,12,576,128]{3,2,1,0:T(8,128)(2,1)} %put.5.refs_0_), custom_call_target="tpu_custom_call", output_to_operand_aliasing={{}: (2, {})} | custom-call | bytes 1474560 | tf_op jit(solution)/shard_map/own/pallas_call | solution.py:169
  142.2 6.3 %collective-permute-done.7.refs_0_ = bf16[12,240,128]{2,1,0:T(8,128)(2,1)S(1)} collective-permute-done((bf16[12,240,128]{2,1,0:T(8,128)(2,1)}, bf16[12,240,128]{2,1,0:T(8,128)(2,1)S(1)}, u32[]{:S(2)}, u32[]{:S(2)}) %collective-permute-start.7) | collective-permute-done | bytes 737312 | tf_op jit(solution)/shard_map/ppermute | solution.py:386
  (39 shorter events, 23.2 us)
Async XLA Ops:
  0.6 0.7 copy-start
  2.7 15.1 %copy-start.1 = (s32[14]{0:T(128)S(1)}, s32[14]{0:T(128)}, u32[]{:S(2)}) copy-start(s32[14]{0:T(128)} %concatenate.3.table) | copy-start | bytes 172
  8.2 44.9 %all-to-all-start = ((bf16[32,336,128]{2,1,0:T(8,128)(2,1)}), bf16[32,336,128]{2,1,0:T(8,128)(2,1)S(1)}, u32[]{:S(2)}, u32[]{:S(2)}) async-start(bf16[32,336,128]{2,1,0:T(8,128)(2,1)} %dequantize.2.refs_4_), calls=%async_computation | async-start | bytes 5505024 | tf_op jit(solution)/shard_map/all_to_all | solution.py:382
  17.8 35.3 %copy-start.2 = (s32[14]{0:T(128)S(1)}, s32[14]{0:T(128)}, u32[]{:S(2)}) copy-start(s32[14]{0:T(128)} %concatenate.3.table) | copy-start | bytes 172
  20.7 16.2 %collective-permute-start = (bf16[576,512]{1,0:T(8,128)(2,1)}, bf16[576,512]{1,0:T(8,128)(2,1)S(1)}, u32[]{:S(2)}, u32[]{:S(2)}) collective-permute-start(bf16[576,512]{1,0:T(8,128)(2,1)} %get-tuple-element.33), channel_id=1, source_target_pairs={{0,32},{32,64},{64,96},{96,0},{1,33},{33,65},{65,97},{97,1},{2,34}... | collective-permute-start | bytes 1769480 | tf_op jit(solution)/shard_map/ppermute | solution.py:386
  21.9 28.6 %collective-permute-start.1 = (bf16[576,512]{1,0:T(8,128)(2,1)}, bf16[576,512]{1,0:T(8,128)(2,1)}, u32[]{:S(2)}, u32[]{:S(2)}) collective-permute-start(bf16[576,512]{1,0:T(8,128)(2,1)} %get-tuple-element.34), channel_id=1, source_target_pairs={{0,64},{32,96},{64,0},{96,32},{1,65},{33,97},{65,1},{97,33},{2,66}... | collective-permute-start | bytes 1769480 | tf_op jit(solution)/shard_map/ppermute | solution.py:386
  24.4 26.2 %collective-permute-start.2 = (bf16[576,512]{1,0:T(8,128)(2,1)}, bf16[576,512]{1,0:T(8,128)(2,1)}, u32[]{:S(2)}, u32[]{:S(2)}) collective-permute-start(bf16[576,512]{1,0:T(8,128)(2,1)} %get-tuple-element.35), channel_id=1, source_target_pairs={{0,96},{32,0},{64,32},{96,64},{1,97},{33,1},{65,33},{97,65},{2,98}... | collective-permute-start | bytes 1769480 | tf_op jit(solution)/shard_map/ppermute | solution.py:386
  36.9 26.2 %copy-start.4 = (bf16[576,512]{1,0:T(8,128)(2,1)}, bf16[576,512]{1,0:T(8,128)(2,1)S(1)}, u32[]{:S(2)}) copy-start(bf16[576,512]{1,0:T(8,128)(2,1)S(1)} %collective-permute-done.refs_1_) | copy-start | bytes 1769476
  54.6 25.2 %collective-permute-start.3 = (bf16[12,336,128]{2,1,0:T(8,128)(2,1)}, bf16[12,336,128]{2,1,0:T(8,128)(2,1)}, u32[]{:S(2)}, u32[]{:S(2)}) collective-permute-start(bf16[12,336,128]{2,1,0:T(8,128)(2,1)} %pack.4), channel_id=1, source_target_pairs={{0,64},{32,96},{64,0},{96,32},{1,65},{33,97},{65,1},{97,33},{2,66}... | collective-permute-start | bytes 3096584 | tf_op jit(solution)/shard_map/ppermute | solution.py:386
  57.4 32.6 %all-to-all-start.1 = ((bf16[32,240,128]{2,1,0:T(8,128)(2,1)}), bf16[32,240,128]{2,1,0:T(8,128)(2,1)}, u32[]{:S(2)}, u32[]{:S(2)}) async-start(bf16[32,240,128]{2,1,0:T(8,128)(2,1)} %dequantize.3.refs_5_), calls=%async_computation.1 | async-start | bytes 3932160 | tf_op jit(solution)/shard_map/all_to_all | solution.py:382
  79.9 23.9 %collective-permute-start.4 = (bf16[12,336,128]{2,1,0:T(8,128)(2,1)}, bf16[12,336,128]{2,1,0:T(8,128)(2,1)}, u32[]{:S(2)}, u32[]{:S(2)}) collective-permute-start(bf16[12,336,128]{2,1,0:T(8,128)(2,1)} %get-tuple-element.48), channel_id=1, source_target_pairs={{0,32},{32,64},{64,96},{96,0},{1,33},{33,65},{65,97},{97,1},{2,34}... | collective-permute-start | bytes 3096584 | tf_op jit(solution)/shard_map/ppermute | solution.py:386
  81.1 22.7 %collective-permute-start.5 = (bf16[12,336,128]{2,1,0:T(8,128)(2,1)}, bf16[12,336,128]{2,1,0:T(8,128)(2,1)}, u32[]{:S(2)}, u32[]{:S(2)}) collective-permute-start(bf16[12,336,128]{2,1,0:T(8,128)(2,1)} %get-tuple-element.49), channel_id=1, source_target_pairs={{0,96},{32,0},{64,32},{96,64},{1,97},{33,1},{65,33},{97,65},{2,98}... | collective-permute-start | bytes 3096584 | tf_op jit(solution)/shard_map/ppermute | solution.py:386
  86.3 46.5 %copy-start.3 = (bf16[4,4,576]{2,1,0:T(4,128)(2,1)S(1)}, bf16[4,4,576]{2,1,0:T(4,128)(2,1)}, u32[]{:S(2)}) copy-start(bf16[4,4,576]{2,1,0:T(4,128)(2,1)} %param.17) | copy-start | bytes 55300
  90.1 17.4 %all-to-all-start.2 = ((bf16[32,16,640]{2,1,0:T(8,128)(2,1)}), bf16[32,16,640]{2,1,0:T(8,128)(2,1)S(1)}, u32[]{:S(2)}, u32[]{:S(2)}) async-start(bf16[32,16,640]{2,1,0:T(8,128)(2,1)} %bitcast.8), calls=%async_computation.2 | async-start | bytes 1310720 | tf_op jit(solution)/shard_map/all_to_all | solution.py:382
  109.9 20.1 %collective-permute-start.6 = (bf16[12,240,128]{2,1,0:T(8,128)(2,1)}, bf16[12,240,128]{2,1,0:T(8,128)(2,1)S(1)}, u32[]{:S(2)}, u32[]{:S(2)}) collective-permute-start(bf16[12,240,128]{2,1,0:T(8,128)(2,1)} %pack.6), channel_id=1, source_target_pairs={{0,64},{32,96},{64,0},{96,32},{1,65},{33,97},{65,1},{97,33},{2,66}... | collective-permute-start | bytes 2211848 | tf_op jit(solution)/shard_map/ppermute | solution.py:386
  115.6 25.3 %all-to-all-start.3 = ((f32[4,16,640]{2,1,0:T(8,128)}), f32[4,16,640]{2,1,0:T(8,128)S(1)}, u32[]{:S(2)}, u32[]{:S(2)}) async-start(f32[4,16,640]{2,1,0:T(8,128)} %join.1), calls=%async_computation.3 | async-start | bytes 327680 | tf_op jit(solution)/shard_map/all_to_all | solution.py:444
  130.0 18.5 %collective-permute-start.7 = (bf16[12,240,128]{2,1,0:T(8,128)(2,1)}, bf16[12,240,128]{2,1,0:T(8,128)(2,1)S(1)}, u32[]{:S(2)}, u32[]{:S(2)}) collective-permute-start(bf16[12,240,128]{2,1,0:T(8,128)(2,1)} %get-tuple-element.55), channel_id=1, source_target_pairs={{0,32},{32,64},{64,96},{96,0},{1,33},{33,65},{65,97},{97,1},{2,34}... | collective-permute-start | bytes 2211848 | tf_op jit(solution)/shard_map/ppermute | solution.py:386
  130.2 18.4 %collective-permute-start.8 = (bf16[12,240,128]{2,1,0:T(8,128)(2,1)}, bf16[12,240,128]{2,1,0:T(8,128)(2,1)S(1)}, u32[]{:S(2)}, u32[]{:S(2)}) collective-permute-start(bf16[12,240,128]{2,1,0:T(8,128)(2,1)} %get-tuple-element.56), channel_id=1, source_target_pairs={{0,96},{32,0},{64,32},{96,64},{1,97},{33,1},{65,33},{97,65},{2,98}... | collective-permute-start | bytes 2211848 | tf_op jit(solution)/shard_map/ppermute | solution.py:386

commit v3 on v2

v3 whole, which is shorter than its diff:
```python
import functools

import jax
import jax.numpy as jnp
from jax import lax
from jax.experimental import pallas as pl
from jax.experimental.pallas import tpu as pltpu
from jax.sharding import PartitionSpec as P

LATENT_CHANNELS = 512
MOST_STRIPES = 12
HEADS = 128
NEG_FILL = -1e30
SCORE_SCALE = 192.0 ** (-0.5)
CHUNKS = (256, 320)
KEY_TILE = 16
KEY_PART = 4
NOTE_LANES = 128

SMEM = pl.BlockSpec(memory_space=pltpu.SMEM)
HBM = pl.BlockSpec(memory_space=pltpu.HBM)
VMEM = pl.BlockSpec(memory_space=pltpu.VMEM)


LONG = pl.CostEstimate(flops=40 << 30, bytes_accessed=0, transcendentals=0)


def params(megabytes=16):
    return pltpu.CompilerParams(vmem_limit_bytes=megabytes << 20)


def moved(steps, rows):
    size = 2 * steps * MOST_STRIPES * rows * 128
    return pl.CostEstimate(flops=0, bytes_accessed=2 * size, transcendentals=0)


def request_for(table, target):
    first, count, before = 0, 0, 0
    for r in range(4):
        here = table[2 + r]
        hit = table[6 + r] == target
        first = jnp.where(hit, before, first)
        count = jnp.where(hit, here, count)
        before = before + here
    return first, count


def request_of(table, stripe):
    target, empty, before = 0, 0, 0
    for r in range(4):
        after = before + table[2 + r]
        inside = jnp.logical_and(stripe >= before, stripe < after)
        target = jnp.where(inside, table[6 + r], target)
        empty = jnp.where(stripe == after - 1, table[10 + r], empty)
        before = after
    return target, empty


def dequantize_kernel(start, per_step, total, table, packed, scale, channels, values, out, scales, marks):
    rows = packed.shape[0]
    width = per_step * 16
    step = pl.program_id(0)

    @pl.when(step == 0)
    def _():
        mark = channels[...].astype(jnp.float32).T
        low, high = start // 128 * 128, min(-(-(start + rows) // 128) * 128, scale.shape[1])
        plain = scale[:, low:high]
        ids = (lax.broadcasted_iota(jnp.int32, plain.shape, 1) + low).astype(jnp.float32)
        for k in range(16):
            plain = jnp.where(ids == mark[:, k : k + 1], 0.0, plain)
        turned = plain.T[start - low : start - low + rows]
        for i in range(total):
            scales[i] = turned[:, i * per_step : (i + 1) * per_step]
            marks[i] = jnp.concatenate([mark[i * per_step + b : i * per_step + b + 1] for b in range(per_step)], axis=1)

    _, empty = request_of(table, table[1])
    ids = (lax.broadcasted_iota(jnp.int32, (rows, width), 0) + start).astype(jnp.float32)
    onehot = (ids == marks[step]).astype(jnp.bfloat16)
    flat = values[...].reshape(width, 128)
    block = lax.broadcasted_iota(jnp.int32, (width, 128), 0) // 16
    spread = jnp.concatenate([jnp.where(block == b, flat, jnp.zeros_like(flat)) for b in range(per_step)], axis=1)
    outliers = jnp.dot(onehot, spread, preferred_element_type=jnp.float32)
    tokens = lax.broadcasted_iota(jnp.int32, (rows, 128), 1)
    here = scales[step]
    for b in range(per_step):
        lanes = slice(b * 128, (b + 1) * 128)
        latent = packed[:, lanes].astype(jnp.float32) * here[:, b : b + 1] + outliers[:, lanes]
        if b == per_step - 1:
            limit = jnp.where(step == total - 1, 128 - empty, 128)
            latent = jnp.where(tokens < limit, latent, 0.0)
        out[b] = latent.astype(jnp.bfloat16)


def dequantize(start, rows, table, packed, scale, channels, values, cost):
    packed, values = [pltpu.with_memory_space_constraint(x, pltpu.HBM) for x in (packed, values)]
    blocks = scale.shape[0]
    per_step = 16
    steps = blocks // per_step
    return pl.pallas_call(
        functools.partial(dequantize_kernel, start, per_step, steps),
        grid=(steps,),
        out_shape=pltpu.HBM((blocks, rows, 128), jnp.bfloat16),
        in_specs=[
            SMEM,
            pl.BlockSpec((pl.Element(rows), pl.Element(per_step * 128)), lambda i: (start, i * per_step * 128)),
            pl.BlockSpec(scale.shape, lambda i: (0, 0)),
            pl.BlockSpec(channels.shape, lambda i: (0, 0)),
            pl.BlockSpec((per_step, 16, 128), lambda i: (i, 0, 0)),
        ],
        out_specs=pl.BlockSpec((per_step, rows, 128), lambda i: (i, 0, 0)),
        scratch_shapes=[
            pltpu.VMEM((steps, rows, per_step), jnp.float32),
            pltpu.VMEM((steps, 1, per_step * 16), jnp.float32),
        ],
        compiler_params=params(60),
        cost_estimate=pl.CostEstimate(flops=0, bytes_accessed=4 * blocks * rows * 128, transcendentals=0),
        name="dequantize",
    )(table, packed, scale, channels, values)


def collect(table, steps, stripes, targets, zeros, sems):
    zeros[...] = jnp.zeros_like(zeros)
    for i, d in enumerate(steps):
        first, count = request_for(table, lax.rem(table[0] + d, 4))
        for v in range(MOST_STRIPES):

            @pl.when(v < count)
            def _():
                pltpu.make_async_copy(stripes.at[first + v], targets[i].at[v], sems.at[i]).start()

            @pl.when(v >= count)
            def _():
                pltpu.make_async_copy(zeros, targets[i].at[v], sems.at[i]).start()

    for i in range(len(steps)):
        pltpu.make_async_copy(targets[i], targets[i], sems.at[i]).wait()


def collect_scratch(steps, rows):
    return [pltpu.VMEM((rows, 128), jnp.bfloat16), pltpu.SemaphoreType.DMA((steps,))]


def pack_kernel(steps, table, stripes, *refs):
    outs, scratch = refs[: len(steps)], refs[len(steps) :]
    collect(table, steps, stripes, outs, *scratch)


def pack(table, stripes, steps):
    rows = stripes.shape[1]
    one = pltpu.HBM((MOST_STRIPES, rows, 128), jnp.bfloat16)
    return pl.pallas_call(
        functools.partial(pack_kernel, steps),
        out_shape=(one,) * len(steps),
        in_specs=[SMEM, VMEM],
        out_specs=(HBM,) * len(steps),
        scratch_shapes=collect_scratch(len(steps), rows),
        compiler_params=params(),
        cost_estimate=moved(len(steps), rows),
        name="pack",
    )(table, stripes)


def own_kernel(start, table, stripes, *refs):
    out, scratch = refs[-3], refs[-2:]
    rows = stripes.shape[1]
    collect(table, (0,), stripes, [out.at[table[0], :, pl.ds(start, rows), :]], *scratch)


def own(start, table, stripes, cache, cost=None):
    rows = stripes.shape[1]
    more = () if cache is None else (cache,)
    return pl.pallas_call(
        functools.partial(own_kernel, start),
        out_shape=jax.ShapeDtypeStruct((4, MOST_STRIPES, sum(CHUNKS), 128), jnp.bfloat16),
        in_specs=[SMEM, VMEM] + [HBM] * len(more),
        out_specs=HBM,
        input_output_aliases={2: 0} if more else {},
        scratch_shapes=collect_scratch(1, rows),
        compiler_params=params(),
        cost_estimate=cost or moved(1, rows),
        name="own",
    )(table, stripes, *more)


PIECES = 3


def put_copies(start, steps, table, arrived, out, sems):
    rows, size = arrived[0].shape[1], MOST_STRIPES // PIECES
    copies = []
    for i, d in enumerate(steps):
        slot = out.at[lax.rem(table[0] + 4 - d, 4)]
        for h in range(PIECES):
            part = pl.ds(h * size, size)
            copies.append(
                pltpu.make_async_copy(arrived[i].at[part], slot.at[part, pl.ds(start, rows), :], sems.at[i, h])
            )
    return copies


def put_kernel(start, steps, table, *refs):
    arrived, (out, sems) = refs[: len(steps)], refs[-2:]
    copies = put_copies(start, steps, table, arrived, out, sems)
    for copy in copies:
        copy.start()
    for copy in copies:
        copy.wait()


def put_later_kernel(start, steps, table, *refs):
    arrived, (out, sems, held, in_sems) = refs[: len(steps)], refs[-4:]
    come = [pltpu.make_async_copy(arrived[i], held.at[i], in_sems.at[i]) for i in range(len(steps))]
    leave = put_copies(start, steps, table, [held.at[i] for i in range(len(steps))], out, sems)
    for copy in come:
        copy.start()
    for i, copy in enumerate(come):
        copy.wait()
        for part in leave[i * PIECES : (i + 1) * PIECES]:
            part.start()
    for part in leave:
        part.wait()


def put(start, table, steps, arrived, cache, later=False):
    rows = arrived[0].shape[1]
    scratch = [pltpu.SemaphoreType.DMA((len(steps), PIECES))]
    if later:
        scratch += [
            pltpu.VMEM((len(steps), MOST_STRIPES, rows, 128), jnp.bfloat16),
            pltpu.SemaphoreType.DMA((len(steps),)),
        ]
    return pl.pallas_call(
        functools.partial(put_later_kernel if later else put_kernel, start, steps),
        out_shape=jax.ShapeDtypeStruct((4, MOST_STRIPES, sum(CHUNKS), 128), jnp.bfloat16),
        in_specs=[SMEM] + [pl.BlockSpec(memory_space=pl.ANY) if later else VMEM] * len(steps) + [HBM],
        out_specs=HBM,
        input_output_aliases={len(steps) + 1: 0},
        scratch_shapes=scratch,
        compiler_params=params(),
        cost_estimate=moved(len(steps), rows),
        name="put",
    )(table, *arrived, cache)


def partner(table):
    return table[1] + 1 - 2 * lax.rem(table[1], 2)


def half_of(table, rows):
    return pl.ds(pl.multiple_of(lax.rem(table[1], 2) * rows, rows), rows)


def split_kernel(table, queries, *refs):
    outs, (held, in_sems, out_sems) = refs[:3], refs[3:]
    half = half_of(table, held.shape[1])
    come = [
        pltpu.make_async_copy(queries.at[lax.rem(table[0] + d + 1, 4), half], held.at[d], in_sems.at[d])
        for d in range(3)
    ]
    leave = [pltpu.make_async_copy(held.at[d], outs[d], out_sems.at[d]) for d in range(3)]
    for copy in come:
        copy.start()
    for d in range(3):
        come[d].wait()
        leave[d].start()
    for copy in leave:
        copy.wait()


def split(table, queries):
    shape = (queries.shape[1] // 2, queries.shape[2])
    return pl.pallas_call(
        split_kernel,
        out_shape=(pltpu.HBM(shape, queries.dtype),) * 3,
        in_specs=[SMEM, HBM],
        out_specs=(HBM,) * 3,
        scratch_shapes=[
            pltpu.VMEM((3,) + shape, queries.dtype),
            pltpu.SemaphoreType.DMA((3,)),
            pltpu.SemaphoreType.DMA((3,)),
        ],
        compiler_params=params(),
        cost_estimate=pl.CostEstimate(flops=0, bytes_accessed=1 << 20, transcendentals=0),
        name="split",
    )(table, pltpu.with_memory_space_constraint(queries, pltpu.HBM))


def start_half(table, target, queries, pieces, out, sem):
    for d in range(4):
        source = queries.at[table[0], half_of(table, out.shape[0])] if d == 0 else pieces[d - 1]

        @pl.when(target == lax.rem(table[0] + 4 - d, 4))
        def _():
            pltpu.make_async_copy(source, out, sem).start()


def hand_kernel(table, queries, in1, in2, in3, out, sem):
    target, _ = request_of(table, partner(table))
    start_half(table, target, queries, (in1, in2, in3), out, sem)
    pltpu.make_async_copy(in1, out, sem).wait()


def hand(table, queries, pieces):
    queries = pltpu.with_memory_space_constraint(queries, pltpu.HBM)
    return pl.pallas_call(
        hand_kernel,
        out_shape=jax.ShapeDtypeStruct(pieces[0].shape, pieces[0].dtype),
        in_specs=[SMEM, HBM] + [VMEM] * 3,
        out_specs=VMEM,
        scratch_shapes=[pltpu.SemaphoreType.DMA],
        compiler_params=params(),
        cost_estimate=pl.CostEstimate(flops=0, bytes_accessed=1 << 20, transcendentals=0),
        name="hand",
    )(table, queries, *pieces)


def in_three(x):
    high = x.astype(jnp.bfloat16)
    rest = x - high.astype(jnp.float32)
    middle = rest.astype(jnp.bfloat16)
    low = (rest - middle.astype(jnp.float32)).astype(jnp.bfloat16)
    return high, middle, low


def attend_kernel(steps, table, *refs):
    sources, handed, keys = refs[:4], refs[4], refs[5 : 5 + len(CHUNKS)]
    out, peak, total, weighted, turned, queries, sems = refs[5 + len(CHUNKS) :]
    step = pl.program_id(0)
    target, empty = request_of(table, table[1])

    @pl.when(step == 0)
    def _():
        rows = handed.shape[0]
        mine, other = turned.at[half_of(table, rows)], turned.at[half_of((0, partner(table)), rows)]
        start_half(table, target, sources[0], sources[1:], mine, sems.at[0])
        copy = pltpu.make_async_copy(handed, other, sems.at[1])
        copy.start()
        copy.wait()
        pltpu.make_async_copy(sources[1], mine, sems.at[0]).wait()
        queries[...] = turned[...].T
        peak[...] = jnp.full_like(peak, NEG_FILL)
        total[...] = jnp.zeros_like(total)
        weighted[...] = jnp.zeros_like(weighted)

    parts = [
        jnp.concatenate(
            [jnp.concatenate([k[b] for k in keys], axis=0) for b in range(i, i + KEY_PART)], axis=1
        )
        for i in range(0, KEY_TILE, KEY_PART)
    ]
    scores = [jnp.dot(queries[...], part, preferred_element_type=jnp.float32) for part in parts]
    limit = jnp.where(step == steps - 1, KEY_PART * 128 - empty, KEY_PART * 128)
    columns = lax.broadcasted_iota(jnp.int32, (1, KEY_PART * 128), 1)
    scores[-1] = scores[-1] + jnp.where(columns < limit, 0.0, NEG_FILL)
    before = peak[...]
    now = before
    for score in scores:
        now = jnp.maximum(now, jnp.max(score, axis=1, keepdims=True))
    shrink = jnp.exp((before - now) * SCORE_SCALE)
    whole, sums = total[...] * shrink, weighted[...] * shrink[:, :1]
    for score, part in zip(scores, parts):
        weights = jnp.exp((score - now[:, :1]) * SCORE_SCALE).astype(jnp.bfloat16)
        whole = whole + jnp.sum(weights.astype(jnp.float32), axis=1, keepdims=True)
        sums = sums + lax.dot_general(
            weights, part[:LATENT_CHANNELS], (((1,), (1,)), ((), ())), preferred_element_type=jnp.float32
        )
    total[...], weighted[...], peak[...] = whole, sums, now

    @pl.when(step == steps - 1)
    def _():
        out[:, :LATENT_CHANNELS] = weighted[...].astype(jnp.bfloat16)
        lane = lax.broadcasted_iota(jnp.int32, peak.shape, 1)
        note = jnp.zeros(peak.shape, jnp.float32)
        for i, part in enumerate(in_three(peak[...] * SCORE_SCALE) + in_three(total[...])):
            note = jnp.where(lane == i, part.astype(jnp.float32), note)
        out[:, LATENT_CHANNELS:] = note.astype(jnp.bfloat16)


def attend(table, queries, pieces, handed, keys):
    channels, rows = queries.shape[1:]
    queries = pltpu.with_memory_space_constraint(queries, pltpu.HBM)
    keys = [pltpu.with_memory_space_constraint(k, pltpu.HBM) for k in keys]
    blocks = keys[0].shape[0]
    steps = blocks // KEY_TILE
    width = LATENT_CHANNELS + NOTE_LANES
    return pl.pallas_call(
        functools.partial(attend_kernel, steps),
        grid=(steps,),
        out_shape=jax.ShapeDtypeStruct((rows, width), jnp.bfloat16),
        in_specs=[SMEM, HBM] + [VMEM] * 4
        + [pl.BlockSpec((KEY_TILE,) + k.shape[1:], lambda i: (i, 0, 0)) for k in keys],
        out_specs=pl.BlockSpec((rows, width), lambda i: (0, 0)),
        scratch_shapes=[
            pltpu.VMEM((rows, 128), jnp.float32),
            pltpu.VMEM((rows, 128), jnp.float32),
            pltpu.VMEM((rows, LATENT_CHANNELS), jnp.float32),
            pltpu.VMEM((channels, rows), jnp.bfloat16),
            pltpu.VMEM((rows, channels), jnp.bfloat16),
            pltpu.SemaphoreType.DMA((2,)),
        ],
        compiler_params=params(60),
        cost_estimate=LONG,
        name="attend",
    )(table, queries, *pieces, handed, *keys)


def join_kernel(table, partials, out):
    stripes, rows, _ = partials.shape
    note = partials[:, :, LATENT_CHANNELS:].astype(jnp.float32)
    peak = note[:, :, 0:1] + note[:, :, 1:2] + note[:, :, 2:3]
    total = note[:, :, 3:4] + note[:, :, 4:5] + note[:, :, 5:6]
    stripe = lax.broadcasted_iota(jnp.int32, peak.shape, 0)
    lane = lax.broadcasted_iota(jnp.int32, (rows, NOTE_LANES), 1)
    values = partials[:, :, :LATENT_CHANNELS].astype(jnp.float32)
    for d in range(4):
        first, count = request_for(table, d)
        inside = jnp.logical_and(stripe >= first, stripe < first + count)
        top = jnp.max(jnp.where(inside, peak, NEG_FILL), axis=0)
        factor = jnp.where(inside, jnp.exp(jnp.where(inside, peak, NEG_FILL) - top[None]), 0.0)
        out[d, :, :LATENT_CHANNELS] = jnp.sum(values * factor, axis=0)
        whole = jnp.sum(total * factor, axis=0)
        out[d, :, LATENT_CHANNELS:] = jnp.where(lane == 0, top, jnp.where(lane == 1, whole, 0.0))


def join(table, partials):
    return pl.pallas_call(
        join_kernel,
        out_shape=jax.ShapeDtypeStruct((4,) + partials.shape[1:], jnp.float32),
        in_specs=[SMEM, VMEM],
        out_specs=VMEM,
        compiler_params=params(),
        cost_estimate=pl.CostEstimate(flops=0, bytes_accessed=1 << 20, transcendentals=0),
        name="join",
    )(table, partials)


def finish_kernel(scores, fresh, joined, out):
    for slot in range(4):
        cache_peak = joined[slot, :, LATENT_CHANNELS : LATENT_CHANNELS + 1]
        cache_total = joined[slot, :, LATENT_CHANNELS + 1 : LATENT_CHANNELS + 2]
        peak = jnp.maximum(cache_peak, jnp.max(scores[slot], axis=1, keepdims=True))
        shrink = jnp.exp(cache_peak - peak)
        weights = jnp.exp(scores[slot] - peak).astype(jnp.bfloat16)
        weighted = joined[slot, :, :LATENT_CHANNELS] * shrink + jnp.dot(
            weights, fresh[slot][:, :LATENT_CHANNELS], preferred_element_type=jnp.float32
        )
        total = cache_total * shrink + jnp.sum(weights.astype(jnp.float32), axis=1, keepdims=True)
        out[slot] = (weighted / total).astype(jnp.bfloat16)


def finish(joined, queries, fresh, seq_here):
    own = joined.shape[1]
    row_start = seq_here * own
    own_queries = lax.dynamic_slice_in_dim(queries, row_start, own, 1)
    scores = (
        jnp.einsum("yeu,ynu->yen", own_queries, fresh, preferred_element_type=jnp.float32) * SCORE_SCALE
    )
    row_step = (row_start + jnp.arange(own, dtype=jnp.int32)) // HEADS
    col_step = jnp.arange(fresh.shape[1], dtype=jnp.int32)
    scores = jnp.where((col_step[None, :] <= row_step[:, None])[None], scores, NEG_FILL)
    return pl.pallas_call(
        finish_kernel,
        out_shape=jax.ShapeDtypeStruct((4, own, LATENT_CHANNELS), jnp.bfloat16),
        in_specs=[VMEM] * 3,
        out_specs=VMEM,
        compiler_params=params(),
        cost_estimate=pl.CostEstimate(flops=0, bytes_accessed=1 << 20, transcendentals=0),
        name="finish",
    )(scores, fresh, joined)


def tie(*xs):
    return lax.optimization_barrier(xs)


def over_seq(x):
    return lax.all_to_all(x, "seq", split_axis=0, concat_axis=0, tiled=True)


def all_along(x):
    return lax.all_to_all(x, "grp", split_axis=0, concat_axis=0, tiled=True)


def along(x, d):
    return lax.ppermute(x, "grp", [(i, (i + d) % 4) for i in range(4)])


def local(
    compressed,
    block_channel_scale,
    outlier_channels,
    outlier_values,
    lengths,
    assignment,
    padding,
    queries,
    decode_token_latent,
):
    group_here = lax.axis_index("grp")
    seq_here = lax.axis_index("seq")
    rows_here = [lax.dynamic_index_in_dim(x, group_here, 0, keepdims=False) for x in (lengths, assignment, padding)]
    table = jnp.concatenate([jnp.stack([group_here, seq_here]).astype(jnp.int32)] + rows_here)
    packed = compressed.T
    channels = outlier_channels.T

    starts = [sum(CHUNKS[:i]) for i in range(len(CHUNKS))]
    last = len(CHUNKS) - 1
    latent = [
        dequantize(
            start, rows, table, packed, block_channel_scale, channels, outlier_values, LONG if start == starts[-1] else None
        )
        for start, rows in zip(starts, CHUNKS)
    ]
    turned = queries.transpose(0, 2, 1)
    latent[0], turned = tie(latent[0], turned)
    pieces = [along(x, d) for d, x in zip((1, 2, 3), split(table, turned))]
    handed = hand(table, turned, pieces)

    stripes, latent[1], handed, *pieces = tie(over_seq(latent[0]), latent[1], handed, *pieces)

    one, two, three = pack(table, stripes, (1, 2, 3))
    stripes, following, one, two, three = tie(stripes, latent[1], one, two, three)
    two = along(two, 2)
    handed = lax.ppermute(handed, "seq", [(j, j ^ 1) for j in range(32)])
    partial = attend(table, turned, pieces, handed, latent)
    one, two, three, partial = tie(one, two, three, partial)
    first = [along(one, 1), along(three, 3)]
    cache = put(starts[0], table, (2,), (two,), own(starts[0], table, stripes, None))
    stripes, cache, partial, *first = tie(over_seq(following), cache, partial, *first)

    one, two, three = pack(table, stripes, (1, 2, 3))
    stripes, cache, one, two, three = tie(stripes, cache, one, two, three)
    cache = own(starts[1], table, stripes, cache, LONG)
    following, cache = tie(partial.reshape(32, 16, -1), cache)
    second = [along(one, 1), along(three, 3)]
    two = along(two, 2)
    joined = all_along(join(table, over_seq(following)))
    cache = put(starts[0], table, (1, 3), first, cache, later=True)
    cache = put(starts[1], table, (2,), (two,), cache)
    joined, cache = tie(joined, cache)
    attended = finish(joined, queries, decode_token_latent, seq_here)
    attended, cache = tie(attended, cache)
    cache = put(starts[1], table, (1, 3), second, cache)
    return cache.transpose(0, 1, 3, 2)[None, :, None], attended


def solution(mesh):
    placed = (
        P(("grp", "seq"), None),
        P(("grp", "seq"), None),
        P(("grp", "seq"), None),
        P(("grp", "seq"), None, None),
        P(),
        P(),
        P(),
        P("grp", None, None),
        P("grp", None, None),
    )
    return jax.shard_map(
        local,
        mesh=mesh,
        in_specs=placed,
        out_specs=(P("grp", None, "seq", None, None, None), P("grp", "seq", None)),
        check_vma=False,
    )
```

time: 152 us -> 145 us (0.954)
  waiting for transfers between devices: 58.6 us -> 52.2 us
  Pallas kernels: 49.1 us -> 42.8 us
  local copies, waits for them, and re-layouts: 2.23 us -> 6.39 us
  starting transfers between devices: 36.9 us -> 40.5 us
    ppermute x9, waiting for transfers between devices: 48.6 us -> 24.8 us  [along(): return lax.ppermute(x, 'grp', [(i, (i + d) % 4) for i in range(4)])]
    all_to_all x3, waiting for transfers between devices: 9.96 us -> 19.4 us  [over_seq(): return lax.all_to_all(x, 'seq', split_axis=0, concat_axis=0, tiled=True)]
    all_to_all x1, waiting for transfers between devices: 0.01 us -> 7.98 us  [all_along(): return lax.all_to_all(x, 'grp', split_axis=0, concat_axis=0, tiled=True)]
    unnamed x10 -> x26, local copies, waits for them, and re-layouts: 0.69 us -> 5.1 us
    pallas_call x4 -> x2, Pallas kernels: 8.62 us -> 5.39 us  [pack(): pl.pallas_call(functools.partial(pack_kernel, steps), out_shape=(one,) *...]
    pallas_call x1, Pallas kernels: 12.6 us -> 10.6 us  [attend(): pl.pallas_call(functools.partial(attend_kernel, steps), grid=(steps,), ou...]
    pallas_call x2, Pallas kernels: 10.5 us -> 8.75 us  [dequantize(): pl.pallas_call(functools.partial(dequantize_kernel, start, per_step, step...]
    ppermute x9, starting transfers between devices: 13.6 us -> 15.3 us  [along(): return lax.ppermute(x, 'grp', [(i, (i + d) % 4) for i in range(4)])]
  transfers between devices with their start and end apart: 13 -> 14, of which waited for: 9 -> 7; matrix products, arithmetic and copies ran while one was open for 2% -> 1% of each run, Pallas kernels for 25% -> 23%
where the time goes in v3:
time: 145 us; the launch traced here: 144 us
  waiting for transfers between devices  52.2 us (36%)
  Pallas kernels  42.8 us (30%)
  starting transfers between devices  40.5 us (28%)
  local copies, waits for them, and re-layouts  6.39 us (4%)
  matrix products  1.66 us (1%)
    ppermute x9, waiting for transfers between devices, along(): return lax.ppermute(x, 'grp', [(i, (i + d) % 4) for i in range(4)])  24.8 us
    all_to_all x3, starting transfers between devices, over_seq(): return lax.all_to_all(x, 'seq', split_axis=0, concat_axis=0, tiled=True)  21 us
    all_to_all x3, waiting for transfers between devices, over_seq(): return lax.all_to_all(x, 'seq', split_axis=0, concat_axis=0, tiled=True)  19.4 us
    ppermute x9, starting transfers between devices, along(): return lax.ppermute(x, 'grp', [(i, (i + d) % 4) for i in range(4)])  15.3 us
    pallas_call x1, Pallas kernels, attend(): pl.pallas_call(functools.partial(attend_kernel, steps), grid=(steps,), ou...  10.6 us
    pallas_call x2, Pallas kernels, dequantize(): pl.pallas_call(functools.partial(dequantize_kernel, start, per_step, step...  8.75 us
    all_to_all x1, waiting for transfers between devices, all_along(): return lax.all_to_all(x, 'grp', split_axis=0, concat_axis=0, tiled=True)  7.98 us
    pallas_call x4, Pallas kernels, put(): pl.pallas_call(functools.partial(put_later_kernel if later else put_kerne...  7.36 us
  transfers between devices with their start and end apart: 14, of which 7 were waited for; matrix products, arithmetic and copies ran while one was open for 1% of the time, Pallas kernels for 23%

profile of v3, /device:TPU:1, one launch (start us, length us, event | category | flops | bytes accessed | tf_op | source)
XLA Modules:
  0.0 144.4 jit_solution(10244549537989006891)
XLA Ops:
  2.6 4.1 %dequantize.2.refs_5_ = bf16[32,256,128]{2,1,0:T(8,128)(2,1)} custom-call(s32[14]{0:T(128)} %concatenate.3.table, bf16[576,4096]{1,0:T(8,128)(2,1)} %bitcast.19, f32[32,576]{1,0:T(8,128)} %scale.3, s32[16,32]{1,0:T(8,128)} %bitcast.25, bf16[32,16,128]{2,1,0:T(8,128)(2,1)} %values.3), custom_call_target="tpu_custom_call" | custom-call | bytes 4194304 | tf_op jit(solution)/shard_map/dequantize/pallas_call | solution.py:100
  6.7 9.6 %all-to-all-start = ((bf16[32,256,128]{2,1,0:T(8,128)(2,1)}), bf16[32,256,128]{2,1,0:T(8,128)(2,1)S(1)}, u32[]{:S(2)}, u32[]{:S(2)}) async-start(bf16[32,256,128]{2,1,0:T(8,128)(2,1)} %dequantize.2.refs_5_), calls=%async_computation | async-start | bytes 4194304 | tf_op jit(solution)/shard_map/all_to_all | solution.py:478
  16.3 2.5 %split.1 = (bf16[288,512]{1,0:T(8,128)(2,1)}, bf16[288,512]{1,0:T(8,128)(2,1)}, bf16[288,512]{1,0:T(8,128)(2,1)}) custom-call(s32[14]{0:T(128)S(1)} %copy-done.9, bf16[4,576,512]{2,1,0:T(8,128)(2,1)} %bitcast.21), custom_call_target="tpu_custom_call" | custom-call | bytes 1048576 | tf_op jit(solution)/shard_map/split/pallas_call | solution.py:273
  20.1 2.4 %collective-permute-start.1 = (bf16[288,512]{1,0:T(8,128)(2,1)}, bf16[288,512]{1,0:T(8,128)(2,1)S(1)}, u32[]{:S(2)}, u32[]{:S(2)}) collective-permute-start(bf16[288,512]{1,0:T(8,128)(2,1)} %get-tuple-element.47), channel_id=1, source_target_pairs={{0,64},{32,96},{64,0},{96,32},{1,65},{33,97},{65,1},{97,33},{2,66}... | collective-permute-start | bytes 884744 | tf_op jit(solution)/shard_map/ppermute | solution.py:486
  23.7 4.6 %dequantize.3.refs_6_ = bf16[32,320,128]{2,1,0:T(8,128)(2,1)} custom-call(s32[14]{0:T(128)} %concatenate.3.table, bf16[576,4096]{1,0:T(8,128)(2,1)} %bitcast.20, f32[32,576]{1,0:T(8,128)} %scale.3, s32[16,32]{1,0:T(8,128)} %bitcast.26, bf16[32,16,128]{2,1,0:T(8,128)(2,1)} %values.3), custom_call_target="tpu_custom_call" | custom-call | bytes 5242880 | tf_op jit(solution)/shard_map/dequantize/pallas_call | solution.py:100
  28.7 7.3 %collective-permute-done.1.in2.refs_2_ = bf16[288,512]{1,0:T(8,128)(2,1)S(1)} collective-permute-done((bf16[288,512]{1,0:T(8,128)(2,1)}, bf16[288,512]{1,0:T(8,128)(2,1)S(1)}, u32[]{:S(2)}, u32[]{:S(2)}) %collective-permute-start.1) | collective-permute-done | bytes 294944 | tf_op jit(solution)/shard_map/ppermute | solution.py:486
  38.1 6.5 %all-to-all-done.stripes = bf16[32,256,128]{2,1,0:T(8,128)(2,1)S(1)} async-done(((bf16[32,256,128]{2,1,0:T(8,128)(2,1)}), bf16[32,256,128]{2,1,0:T(8,128)(2,1)S(1)}, u32[]{:S(2)}, u32[]{:S(2)}) %all-to-all-start) | async-done | bytes 2097184 | tf_op jit(solution)/shard_map/all_to_all | solution.py:478
  45.5 2.0 %pack.2 = (bf16[12,256,128]{2,1,0:T(8,128)(2,1)}, bf16[12,256,128]{2,1,0:T(8,128)(2,1)}, bf16[12,256,128]{2,1,0:T(8,128)(2,1)}) custom-call(s32[14]{0:T(128)S(1)} %copy-done.10, bf16[32,256,128]{2,1,0:T(8,128)(2,1)S(1)} %all-to-all-done.stripes), custom_call_target="tpu_custom_call" | custom-call | bytes 4718592 | tf_op jit(solution)/shard_map/pack/pallas_call | solution.py:152
  47.5 2.8 %collective-permute-start.3 = (bf16[12,256,128]{2,1,0:T(8,128)(2,1)}, bf16[12,256,128]{2,1,0:T(8,128)(2,1)S(1)}, u32[]{:S(2)}, u32[]{:S(2)}) collective-permute-start(bf16[12,256,128]{2,1,0:T(8,128)(2,1)} %get-tuple-element.56), channel_id=1, source_target_pairs={{0,64},{32,96},{64,0},{96,32},{1,65},{33,97},{65,1},{97,33},{2,66}... | collective-permute-start | bytes 2359304 | tf_op jit(solution)/shard_map/ppermute | solution.py:486
  50.3 4.7 %all-to-all-start.1 = ((bf16[32,320,128]{2,1,0:T(8,128)(2,1)}), bf16[32,320,128]{2,1,0:T(8,128)(2,1)}, u32[]{:S(2)}, u32[]{:S(2)}) async-start(bf16[32,320,128]{2,1,0:T(8,128)(2,1)} %dequantize.3.refs_6_), calls=%async_computation.1 | async-start | bytes 5242880 | tf_op jit(solution)/shard_map/all_to_all | solution.py:478
  55.0 10.6 %attend.1 = bf16[512,640]{1,0:T(8,128)(2,1)} custom-call(s32[14]{0:T(128)} %concatenate.3.table, bf16[4,576,512]{2,1,0:T(8,128)(2,1)} %bitcast.23, bf16[288,512]{1,0:T(8,128)(2,1)} %copy-done.6, bf16[288,512]{1,0:T(8,128)(2,1)} %copy-done.7, bf16[288,512]{1,0:T(8,128)(2,1)} %copy-done.8, bf16[288,512]{1,0:T(8,128)(2,1)} %collective-permute-done.4.refs_4_, ...), custom_call_target="tpu_custom_call" | custom-call | flops 42949672960 | tf_op jit(solution)/shard_map/attend/pallas_call | solution.py:387
  65.6 2.9 %collective-permute-done.3.refs_0_ = bf16[12,256,128]{2,1,0:T(8,128)(2,1)S(1)} collective-permute-done((bf16[12,256,128]{2,1,0:T(8,128)(2,1)}, bf16[12,256,128]{2,1,0:T(8,128)(2,1)S(1)}, u32[]{:S(2)}, u32[]{:S(2)}) %collective-permute-start.3) | collective-permute-done | bytes 786464 | tf_op jit(solution)/shard_map/ppermute | solution.py:486
  75.1 14.2 %collective-permute-done.5.refs_0_ = bf16[12,256,128]{2,1,0:T(8,128)(2,1)S(1)} collective-permute-done((bf16[12,256,128]{2,1,0:T(8,128)(2,1)}, bf16[12,256,128]{2,1,0:T(8,128)(2,1)S(1)}, u32[]{:S(2)}, u32[]{:S(2)}) %collective-permute-start.5) | collective-permute-done | bytes 786464 | tf_op jit(solution)/shard_map/ppermute | solution.py:486
  90.3 3.4 %pack.3 = (bf16[12,320,128]{2,1,0:T(8,128)(2,1)}, bf16[12,320,128]{2,1,0:T(8,128)(2,1)}, bf16[12,320,128]{2,1,0:T(8,128)(2,1)}) custom-call(s32[14]{0:T(128)S(1)} %copy-done.11, bf16[32,320,128]{2,1,0:T(8,128)(2,1)} %all-to-all-done.1.stripes), custom_call_target="tpu_custom_call" | custom-call | bytes 5898240 | tf_op jit(solution)/shard_map/pack/pallas_call | solution.py:152
  93.7 2.2 %collective-permute-start.9 = (bf16[12,320,128]{2,1,0:T(8,128)(2,1)}, bf16[12,320,128]{2,1,0:T(8,128)(2,1)}, u32[]{:S(2)}, u32[]{:S(2)}) collective-permute-start(bf16[12,320,128]{2,1,0:T(8,128)(2,1)} %get-tuple-element.78), channel_id=1, source_target_pairs={{0,64},{32,96},{64,0},{96,32},{1,65},{33,97},{65,1},{97,33},{2,66}... | collective-permute-start | bytes 2949128 | tf_op jit(solution)/shard_map/ppermute | solution.py:486
  96.7 1.9 %collective-permute-start.8 = (bf16[12,320,128]{2,1,0:T(8,128)(2,1)}, bf16[12,320,128]{2,1,0:T(8,128)(2,1)S(1)}, u32[]{:S(2)}, u32[]{:S(2)}) collective-permute-start(bf16[12,320,128]{2,1,0:T(8,128)(2,1)} %get-tuple-element.73), channel_id=1, source_target_pairs={{0,96},{32,0},{64,32},{96,64},{1,97},{33,1},{65,33},{97,65},{2,98}... | collective-permute-start | bytes 2949128 | tf_op jit(solution)/shard_map/ppermute | solution.py:486
  98.6 2.7 %own.3.refs_2_ = bf16[4,12,576,128]{3,2,1,0:T(8,128)(2,1)} custom-call(s32[14]{0:T(128)S(1)} %copy-done.11, bf16[32,320,128]{2,1,0:T(8,128)(2,1)} %all-to-all-done.1.stripes, bf16[4,12,576,128]{3,2,1,0:T(8,128)(2,1)} %put.4.refs_0_), custom_call_target="tpu_custom_call", output_to_operand_aliasing={{}: (2, {})} | custom-call | flops 42949672960 | tf_op jit(solution)/shard_map/own/pallas_call | solution.py:173
  101.3 6.7 %all-to-all-start.2 = ((bf16[32,16,640]{2,1,0:T(8,128)(2,1)}), bf16[32,16,640]{2,1,0:T(8,128)(2,1)S(1)}, u32[]{:S(2)}, u32[]{:S(2)}) async-start(bf16[32,16,640]{2,1,0:T(8,128)(2,1)} %bitcast.24), calls=%async_computation.2 | async-start | bytes 1310720 | tf_op jit(solution)/shard_map/all_to_all | solution.py:478
  108.1 12.8 %all-to-all-done.2.partials = bf16[32,16,640]{2,1,0:T(8,128)(2,1)S(1)} async-done(((bf16[32,16,640]{2,1,0:T(8,128)(2,1)}), bf16[32,16,640]{2,1,0:T(8,128)(2,1)S(1)}, u32[]{:S(2)}, u32[]{:S(2)}) %all-to-all-start.2) | async-done | bytes 655392 | tf_op jit(solution)/shard_map/all_to_all | solution.py:478
  123.3 3.3 %all-to-all-start.3 = ((f32[4,16,640]{2,1,0:T(8,128)}), f32[4,16,640]{2,1,0:T(8,128)S(1)}, u32[]{:S(2)}, u32[]{:S(2)}) async-start(f32[4,16,640]{2,1,0:T(8,128)} %copy-done.5), calls=%async_computation.3 | async-start | bytes 327680 | tf_op jit(solution)/shard_map/all_to_all | solution.py:482
  129.5 1.9 %put.5.refs_1_ = bf16[4,12,576,128]{3,2,1,0:T(8,128)(2,1)} custom-call(s32[14]{0:T(128)S(1)} %copy-done.11, bf16[12,256,128]{2,1,0:T(8,128)(2,1)S(1)} %collective-permute-done.5.refs_0_, bf16[12,256,128]{2,1,0:T(8,128)(2,1)S(1)} %copy-done.2, bf16[4,12,576,128]{3,2,1,0:T(8,128)(2,1)} %own.3.refs_2_), custom_call_target="tpu_custom_call", output_to_operand_aliasing={{}: (3, {})} | custom-call | bytes 3145728 | tf_op jit(solution)/shard_map/put/pallas_call | solution.py:233
  131.4 2.2 %put.6.refs_2_ = bf16[4,12,576,128]{3,2,1,0:T(8,128)(2,1)} custom-call(s32[14]{0:T(128)S(1)} %copy-done.11, bf16[12,320,128]{2,1,0:T(8,128)(2,1)} %collective-permute-done.9.refs_0_, bf16[4,12,576,128]{3,2,1,0:T(8,128)(2,1)} %put.5.refs_1_), custom_call_target="tpu_custom_call", output_to_operand_aliasing={{}: (2, {})} | custom-call | bytes 1966080 | tf_op jit(solution)/shard_map/put/pallas_call | solution.py:233
  133.6 8.0 %all-to-all-done.3.joined = f32[4,16,640]{2,1,0:T(8,128)S(1)} async-done(((f32[4,16,640]{2,1,0:T(8,128)}), f32[4,16,640]{2,1,0:T(8,128)S(1)}, u32[]{:S(2)}, u32[]{:S(2)}) %all-to-all-start.3) | async-done | bytes 163872 | tf_op jit(solution)/shard_map/all_to_all | solution.py:482
  142.6 1.9 %put.7 = bf16[4,12,576,128]{3,2,1,0:T(8,128)(2,1)} custom-call(s32[14]{0:T(128)S(1)} %copy-done.11, bf16[12,320,128]{2,1,0:T(8,128)(2,1)S(1)} %collective-permute-done.7.refs_0_, bf16[12,320,128]{2,1,0:T(8,128)(2,1)S(1)} %collective-permute-done.8.refs_1_, bf16[4,12,576,128]{3,2,1,0:T(8,128)(2,1)} %put.6.refs_2_), custom_call_target="tpu_custom_call", output_to_operand_aliasing={{}: (3, {})} | custom-call | bytes 3932160 | tf_op jit(solution)/shard_map/put/pallas_call | solution.py:233
  (51 shorter events, 22.2 us)
Async XLA Ops:
  2.6 13.7 %copy-start.9 = (s32[14]{0:T(128)S(1)}, s32[14]{0:T(128)}, u32[]{:S(2)}) copy-start(s32[14]{0:T(128)} %concatenate.3.table) | copy-start | bytes 172
  6.7 37.9 %all-to-all-start = ((bf16[32,256,128]{2,1,0:T(8,128)(2,1)}), bf16[32,256,128]{2,1,0:T(8,128)(2,1)S(1)}, u32[]{:S(2)}, u32[]{:S(2)}) async-start(bf16[32,256,128]{2,1,0:T(8,128)(2,1)} %dequantize.2.refs_5_), calls=%async_computation | async-start | bytes 4194304 | tf_op jit(solution)/shard_map/all_to_all | solution.py:478
  16.3 19.7 %copy-start.10 = (s32[14]{0:T(128)S(1)}, s32[14]{0:T(128)}, u32[]{:S(2)}) copy-start(s32[14]{0:T(128)} %concatenate.3.table) | copy-start | bytes 172
  18.8 9.9 %collective-permute-start = (bf16[288,512]{1,0:T(8,128)(2,1)}, bf16[288,512]{1,0:T(8,128)(2,1)S(1)}, u32[]{:S(2)}, u32[]{:S(2)}) collective-permute-start(bf16[288,512]{1,0:T(8,128)(2,1)} %get-tuple-element.46), channel_id=1, source_target_pairs={{0,32},{32,64},{64,96},{96,0},{1,33},{33,65},{65,97},{97,1},{2,34}... | collective-permute-start | bytes 884744 | tf_op jit(solution)/shard_map/ppermute | solution.py:486
  20.1 15.9 %collective-permute-start.1 = (bf16[288,512]{1,0:T(8,128)(2,1)}, bf16[288,512]{1,0:T(8,128)(2,1)S(1)}, u32[]{:S(2)}, u32[]{:S(2)}) collective-permute-start(bf16[288,512]{1,0:T(8,128)(2,1)} %get-tuple-element.47), channel_id=1, source_target_pairs={{0,64},{32,96},{64,0},{96,32},{1,65},{33,97},{65,1},{97,33},{2,66}... | collective-permute-start | bytes 884744 | tf_op jit(solution)/shard_map/ppermute | solution.py:486
  22.5 13.4 %collective-permute-start.2 = (bf16[288,512]{1,0:T(8,128)(2,1)}, bf16[288,512]{1,0:T(8,128)(2,1)S(1)}, u32[]{:S(2)}, u32[]{:S(2)}) collective-permute-start(bf16[288,512]{1,0:T(8,128)(2,1)} %get-tuple-element.48), channel_id=1, source_target_pairs={{0,96},{32,0},{64,32},{96,64},{1,97},{33,1},{65,33},{97,65},{2,98}... | collective-permute-start | bytes 884744 | tf_op jit(solution)/shard_map/ppermute | solution.py:486
  28.7 21.6 %copy-start.6 = (bf16[288,512]{1,0:T(8,128)(2,1)}, bf16[288,512]{1,0:T(8,128)(2,1)S(1)}, u32[]{:S(2)}) copy-start(bf16[288,512]{1,0:T(8,128)(2,1)S(1)} %collective-permute-done.in1.refs_1_) | copy-start | bytes 884740
  36.0 14.3 %copy-start.7 = (bf16[288,512]{1,0:T(8,128)(2,1)}, bf16[288,512]{1,0:T(8,128)(2,1)S(1)}, u32[]{:S(2)}) copy-start(bf16[288,512]{1,0:T(8,128)(2,1)S(1)} %collective-permute-done.1.in2.refs_2_) | copy-start | bytes 884740
  44.6 10.4 %collective-permute-start.4 = (bf16[288,512]{1,0:T(8,128)(2,1)}, bf16[288,512]{1,0:T(8,128)(2,1)}, u32[]{:S(2)}, u32[]{:S(2)}) collective-permute-start(bf16[288,512]{1,0:T(8,128)(2,1)} %hand.1), channel_id=1, source_target_pairs={{0,1},{1,0},{2,3},{3,2},{4,5},{5,4},{6,7},{7,6},{8,9},{9,8},{10,11... | collective-permute-start | bytes 884744 | tf_op jit(solution)/shard_map/ppermute | solution.py:525
  47.5 21.1 %collective-permute-start.3 = (bf16[12,256,128]{2,1,0:T(8,128)(2,1)}, bf16[12,256,128]{2,1,0:T(8,128)(2,1)S(1)}, u32[]{:S(2)}, u32[]{:S(2)}) collective-permute-start(bf16[12,256,128]{2,1,0:T(8,128)(2,1)} %get-tuple-element.56), channel_id=1, source_target_pairs={{0,64},{32,96},{64,0},{96,32},{1,65},{33,97},{65,1},{97,33},{2,66}... | collective-permute-start | bytes 2359304 | tf_op jit(solution)/shard_map/ppermute | solution.py:486
  50.3 40.0 %all-to-all-start.1 = ((bf16[32,320,128]{2,1,0:T(8,128)(2,1)}), bf16[32,320,128]{2,1,0:T(8,128)(2,1)}, u32[]{:S(2)}, u32[]{:S(2)}) async-start(bf16[32,320,128]{2,1,0:T(8,128)(2,1)} %dequantize.3.refs_6_), calls=%async_computation.1 | async-start | bytes 5242880 | tf_op jit(solution)/shard_map/all_to_all | solution.py:478
  55.0 17.2 %copy-start.11 = (s32[14]{0:T(128)S(1)}, s32[14]{0:T(128)}, u32[]{:S(2)}) copy-start(s32[14]{0:T(128)} %concatenate.3.table) | copy-start | bytes 172
  68.5 1.0 copy-start.3
  69.5 19.8 %collective-permute-start.5 = (bf16[12,256,128]{2,1,0:T(8,128)(2,1)}, bf16[12,256,128]{2,1,0:T(8,128)(2,1)S(1)}, u32[]{:S(2)}, u32[]{:S(2)}) collective-permute-start(bf16[12,256,128]{2,1,0:T(8,128)(2,1)} %get-tuple-element.65), channel_id=1, source_target_pairs={{0,32},{32,64},{64,96},{96,0},{1,33},{33,65},{65,97},{97,1},{2,34}... | collective-permute-start | bytes 2359304 | tf_op jit(solution)/shard_map/ppermute | solution.py:486
  70.7 2.9 %copy-start.4 = (bf16[12,256,128]{2,1,0:T(8,128)(2,1)S(1)}, bf16[12,256,128]{2,1,0:T(8,128)(2,1)}, u32[]{:S(2)}) copy-start(bf16[12,256,128]{2,1,0:T(8,128)(2,1)} %copy-done.3) | copy-start | bytes 2359300
  70.7 18.6 %collective-permute-start.6 = (bf16[12,256,128]{2,1,0:T(8,128)(2,1)}, bf16[12,256,128]{2,1,0:T(8,128)(2,1)S(1)}, u32[]{:S(2)}, u32[]{:S(2)}) collective-permute-start(bf16[12,256,128]{2,1,0:T(8,128)(2,1)} %get-tuple-element.66), channel_id=1, source_target_pairs={{0,96},{32,0},{64,32},{96,64},{1,97},{33,1},{65,33},{97,65},{2,98}... | collective-permute-start | bytes 2359304 | tf_op jit(solution)/shard_map/ppermute | solution.py:486
  89.3 0.9 copy-start.1
  93.7 33.0 %copy-start.12 = (bf16[4,4,576]{2,1,0:T(4,128)(2,1)S(1)}, bf16[4,4,576]{2,1,0:T(4,128)(2,1)}, u32[]{:S(2)}) copy-start(bf16[4,4,576]{2,1,0:T(4,128)(2,1)} %fresh.1) | copy-start | bytes 55300
  93.7 37.7 %collective-permute-start.9 = (bf16[12,320,128]{2,1,0:T(8,128)(2,1)}, bf16[12,320,128]{2,1,0:T(8,128)(2,1)}, u32[]{:S(2)}, u32[]{:S(2)}) collective-permute-start(bf16[12,320,128]{2,1,0:T(8,128)(2,1)} %get-tuple-element.78), channel_id=1, source_target_pairs={{0,64},{32,96},{64,0},{96,32},{1,65},{33,97},{65,1},{97,33},{2,66}... | collective-permute-start | bytes 2949128 | tf_op jit(solution)/shard_map/ppermute | solution.py:486
  95.9 46.6 %collective-permute-start.7 = (bf16[12,320,128]{2,1,0:T(8,128)(2,1)}, bf16[12,320,128]{2,1,0:T(8,128)(2,1)S(1)}, u32[]{:S(2)}, u32[]{:S(2)}) collective-permute-start(bf16[12,320,128]{2,1,0:T(8,128)(2,1)} %get-tuple-element.72), channel_id=1, source_target_pairs={{0,32},{32,64},{64,96},{96,0},{1,33},{33,65},{65,97},{97,1},{2,34}... | collective-permute-start | bytes 2949128 | tf_op jit(solution)/shard_map/ppermute | solution.py:486
  96.7 45.8 %collective-permute-start.8 = (bf16[12,320,128]{2,1,0:T(8,128)(2,1)}, bf16[12,320,128]{2,1,0:T(8,128)(2,1)S(1)}, u32[]{:S(2)}, u32[]{:S(2)}) collective-permute-start(bf16[12,320,128]{2,1,0:T(8,128)(2,1)} %get-tuple-element.73), channel_id=1, source_target_pairs={{0,96},{32,0},{64,32},{96,64},{1,97},{33,1},{65,33},{97,65},{2,98}... | collective-permute-start | bytes 2949128 | tf_op jit(solution)/shard_map/ppermute | solution.py:486
  101.3 19.6 %all-to-all-start.2 = ((bf16[32,16,640]{2,1,0:T(8,128)(2,1)}), bf16[32,16,640]{2,1,0:T(8,128)(2,1)S(1)}, u32[]{:S(2)}, u32[]{:S(2)}) async-start(bf16[32,16,640]{2,1,0:T(8,128)(2,1)} %bitcast.24), calls=%async_computation.2 | async-start | bytes 1310720 | tf_op jit(solution)/shard_map/all_to_all | solution.py:478
  123.3 18.2 %all-to-all-start.3 = ((f32[4,16,640]{2,1,0:T(8,128)}), f32[4,16,640]{2,1,0:T(8,128)S(1)}, u32[]{:S(2)}, u32[]{:S(2)}) async-start(f32[4,16,640]{2,1,0:T(8,128)} %copy-done.5), calls=%async_computation.3 | async-start | bytes 327680 | tf_op jit(solution)/shard_map/all_to_all | solution.py:482
  128.3 1.2 copy-start.2
  (3 other events, 2.1 us)

commit v4 on v3

--- a/solution.py
+++ b/solution.py
@@ -12,7 +12,7 @@
 HEADS = 128
 NEG_FILL = -1e30
 SCORE_SCALE = 192.0 ** (-0.5)
-CHUNKS = (256, 320)
+CHUNKS = (272, 304)
 KEY_TILE = 16
 KEY_PART = 4
 NOTE_LANES = 128
@@ -56,7 +56,7 @@
     return target, empty
 
 
-def dequantize_kernel(start, per_step, total, table, packed, scale, channels, values, out, scales, marks):
+def dequantize_kernel(start, per_step, total, place, lengths, padding, packed, scale, channels, values, out, scales, marks):
     rows = packed.shape[0]
     width = per_step * 16
     step = pl.program_id(0)
@@ -74,7 +74,10 @@
             scales[i] = turned[:, i * per_step : (i + 1) * per_step]
             marks[i] = jnp.concatenate([mark[i * per_step + b : i * per_step + b + 1] for b in range(per_step)], axis=1)
 
-    _, empty = request_of(table, table[1])
+    group, empty, before = place[0], 0, 0
+    for r in range(4):
+        before = before + lengths[group, r]
+        empty = jnp.where(place[1] == before - 1, padding[group, r], empty)
     ids = (lax.broadcasted_iota(jnp.int32, (rows, width), 0) + start).astype(jnp.float32)
     onehot = (ids == marks[step]).astype(jnp.bfloat16)
     flat = values[...].reshape(width, 128)
@@ -92,7 +95,7 @@
         out[b] = latent.astype(jnp.bfloat16)
 
 
-def dequantize(start, rows, table, packed, scale, channels, values, cost):
+def dequantize(start, rows, place, lengths, padding, packed, scale, channels, values):
     packed, values = [pltpu.with_memory_space_constraint(x, pltpu.HBM) for x in (packed, values)]
     blocks = scale.shape[0]
     per_step = 16
@@ -102,6 +105,8 @@
         grid=(steps,),
         out_shape=pltpu.HBM((blocks, rows, 128), jnp.bfloat16),
         in_specs=[
+            SMEM,
+            SMEM,
             SMEM,
             pl.BlockSpec((pl.Element(rows), pl.Element(per_step * 128)), lambda i: (start, i * per_step * 128)),
             pl.BlockSpec(scale.shape, lambda i: (0, 0)),
@@ -116,70 +121,46 @@
         compiler_params=params(60),
         cost_estimate=pl.CostEstimate(flops=0, bytes_accessed=4 * blocks * rows * 128, transcendentals=0),
         name="dequantize",
-    )(table, packed, scale, channels, values)
-
-
-def collect(table, steps, stripes, targets, zeros, sems):
+    )(place, lengths, padding, packed, scale, channels, values)
+
+
+def collect(table, d, stripes, target, zeros, sem):
+    first, count = request_for(table, lax.rem(table[0] + d, 4))
+    for v in range(MOST_STRIPES):
+
+        @pl.when(v < count)
+        def _():
+            pltpu.make_async_copy(stripes.at[first + v], target.at[v], sem).start()
+
+        @pl.when(v >= count)
+        def _():
+            pltpu.make_async_copy(zeros, target.at[v], sem).start()
+
+
+def pack_kernel(start, table, stripes, *refs):
+    *outs, cache, zeros, sems = refs[-6:]
     zeros[...] = jnp.zeros_like(zeros)
-    for i, d in enumerate(steps):
-        first, count = request_for(table, lax.rem(table[0] + d, 4))
-        for v in range(MOST_STRIPES):
-
-            @pl.when(v < count)
-            def _():
-                pltpu.make_async_copy(stripes.at[first + v], targets[i].at[v], sems.at[i]).start()
-
-            @pl.when(v >= count)
-            def _():
-                pltpu.make_async_copy(zeros, targets[i].at[v], sems.at[i]).start()
-
-    for i in range(len(steps)):
-        pltpu.make_async_copy(targets[i], targets[i], sems.at[i]).wait()
-
-
-def collect_scratch(steps, rows):
-    return [pltpu.VMEM((rows, 128), jnp.bfloat16), pltpu.SemaphoreType.DMA((steps,))]
-
-
-def pack_kernel(steps, table, stripes, *refs):
-    outs, scratch = refs[: len(steps)], refs[len(steps) :]
-    collect(table, steps, stripes, outs, *scratch)
-
-
-def pack(table, stripes, steps):
-    rows = stripes.shape[1]
-    one = pltpu.HBM((MOST_STRIPES, rows, 128), jnp.bfloat16)
-    return pl.pallas_call(
-        functools.partial(pack_kernel, steps),
-        out_shape=(one,) * len(steps),
-        in_specs=[SMEM, VMEM],
-        out_specs=(HBM,) * len(steps),
-        scratch_shapes=collect_scratch(len(steps), rows),
-        compiler_params=params(),
-        cost_estimate=moved(len(steps), rows),
-        name="pack",
-    )(table, stripes)
-
-
-def own_kernel(start, table, stripes, *refs):
-    out, scratch = refs[-3], refs[-2:]
-    rows = stripes.shape[1]
-    collect(table, (0,), stripes, [out.at[table[0], :, pl.ds(start, rows), :]], *scratch)
-
-
-def own(start, table, stripes, cache, cost=None):
+    targets = [cache.at[table[0], :, pl.ds(start, stripes.shape[1]), :], *outs]
+    for d in (2, 1, 3, 0):
+        collect(table, d, stripes, targets[d], zeros, sems.at[d])
+    for d, target in enumerate(targets):
+        pltpu.make_async_copy(target, target, sems.at[d]).wait()
+
+
+def pack(start, table, stripes, cache):
     rows = stripes.shape[1]
     more = () if cache is None else (cache,)
-    return pl.pallas_call(
-        functools.partial(own_kernel, start),
-        out_shape=jax.ShapeDtypeStruct((4, MOST_STRIPES, sum(CHUNKS), 128), jnp.bfloat16),
+    one = pltpu.HBM((MOST_STRIPES, rows, 128), jnp.bfloat16)
+    return pl.pallas_call(
+        functools.partial(pack_kernel, start),
+        out_shape=(one, one, one, jax.ShapeDtypeStruct((4, MOST_STRIPES, sum(CHUNKS), 128), jnp.bfloat16)),
         in_specs=[SMEM, VMEM] + [HBM] * len(more),
-        out_specs=HBM,
-        input_output_aliases={2: 0} if more else {},
-        scratch_shapes=collect_scratch(1, rows),
+        out_specs=(HBM,) * 4,
+        input_output_aliases={2: 3} if more else {},
+        scratch_shapes=[pltpu.VMEM((rows, 128), jnp.bfloat16), pltpu.SemaphoreType.DMA((4,))],
         compiler_params=params(),
-        cost_estimate=cost or moved(1, rows),
-        name="own",
+        cost_estimate=moved(4, rows),
+        name="pack",
     )(table, stripes, *more)
 
 
@@ -222,7 +203,7 @@
         part.wait()
 
 
-def put(start, table, steps, arrived, cache, later=False):
+def put(start, table, steps, arrived, cache, later=False, cost=None):
     rows = arrived[0].shape[1]
     scratch = [pltpu.SemaphoreType.DMA((len(steps), PIECES))]
     if later:
@@ -238,7 +219,7 @@
         input_output_aliases={len(steps) + 1: 0},
         scratch_shapes=scratch,
         compiler_params=params(),
-        cost_estimate=moved(len(steps), rows),
+        cost_estimate=cost or moved(len(steps), rows),
         name="put",
     )(table, *arrived, cache)
 
@@ -387,7 +368,7 @@
     return pl.pallas_call(
         functools.partial(attend_kernel, steps),
         grid=(steps,),
-        out_shape=jax.ShapeDtypeStruct((rows, width), jnp.bfloat16),
+        out_shape=pltpu.HBM((rows, width), jnp.bfloat16),
         in_specs=[SMEM, HBM] + [VMEM] * 4
         + [pl.BlockSpec((KEY_TILE,) + k.shape[1:], lambda i: (i, 0, 0)) for k in keys],
         out_specs=pl.BlockSpec((rows, width), lambda i: (0, 0)),
@@ -399,7 +380,7 @@
             pltpu.VMEM((rows, channels), jnp.bfloat16),
             pltpu.SemaphoreType.DMA((2,)),
         ],
-        compiler_params=params(60),
+        compiler_params=params(44),
         cost_estimate=LONG,
         name="attend",
     )(table, queries, *pieces, handed, *keys)
@@ -500,16 +481,15 @@
     group_here = lax.axis_index("grp")
     seq_here = lax.axis_index("seq")
     rows_here = [lax.dynamic_index_in_dim(x, group_here, 0, keepdims=False) for x in (lengths, assignment, padding)]
-    table = jnp.concatenate([jnp.stack([group_here, seq_here]).astype(jnp.int32)] + rows_here)
+    place = jnp.stack([group_here, seq_here]).astype(jnp.int32)
+    table = jnp.concatenate([place] + rows_here)
     packed = compressed.T
     channels = outlier_channels.T
 
     starts = [sum(CHUNKS[:i]) for i in range(len(CHUNKS))]
     last = len(CHUNKS) - 1
     latent = [
-        dequantize(
-            start, rows, table, packed, block_channel_scale, channels, outlier_values, LONG if start == starts[-1] else None
-        )
+        dequantize(start, rows, place, lengths, padding, packed, block_channel_scale, channels, outlier_values)
         for start, rows in zip(starts, CHUNKS)
     ]
     turned = queries.transpose(0, 2, 1)
@@ -519,29 +499,23 @@
 
     stripes, latent[1], handed, *pieces = tie(over_seq(latent[0]), latent[1], handed, *pieces)
 
-    one, two, three = pack(table, stripes, (1, 2, 3))
-    stripes, following, one, two, three = tie(stripes, latent[1], one, two, three)
-    two = along(two, 2)
+    one, two, three, cache = pack(starts[0], table, stripes, None)
+    following, one, two, three = tie(latent[1], one, two, three)
+    one, two, three = along(one, 1), along(two, 2), along(three, 3)
     handed = lax.ppermute(handed, "seq", [(j, j ^ 1) for j in range(32)])
     partial = attend(table, turned, pieces, handed, latent)
-    one, two, three, partial = tie(one, two, three, partial)
-    first = [along(one, 1), along(three, 3)]
-    cache = put(starts[0], table, (2,), (two,), own(starts[0], table, stripes, None))
-    stripes, cache, partial, *first = tie(over_seq(following), cache, partial, *first)
-
-    one, two, three = pack(table, stripes, (1, 2, 3))
-    stripes, cache, one, two, three = tie(stripes, cache, one, two, three)
-    cache = own(starts[1], table, stripes, cache, LONG)
+    stripes, partial, *first = tie(over_seq(following), partial, one, two, three)
+
+    one, two, three, cache = pack(starts[1], table, stripes, cache)
+    partial, cache, one, two, three = tie(partial, cache, one, two, three)
+    one, two, three = along(one, 1), along(two, 2), along(three, 3)
+    cache = put(starts[0], table, (1, 2, 3), first, cache, later=True, cost=LONG)
     following, cache = tie(partial.reshape(32, 16, -1), cache)
-    second = [along(one, 1), along(three, 3)]
-    two = along(two, 2)
     joined = all_along(join(table, over_seq(following)))
-    cache = put(starts[0], table, (1, 3), first, cache, later=True)
     cache = put(starts[1], table, (2,), (two,), cache)
+    cache = put(starts[1], table, (1, 3), (one, three), cache)
     joined, cache = tie(joined, cache)
     attended = finish(joined, queries, decode_token_latent, seq_here)
-    attended, cache = tie(attended, cache)
-    cache = put(starts[1], table, (1, 3), second, cache)
     return cache.transpose(0, 1, 3, 2)[None, :, None], attended
 
 

time: 145 us -> 141 us (0.972)
  waiting for transfers between devices: 52.2 us -> 60.8 us
  Pallas kernels: 42.8 us -> 36.3 us
  local copies, waits for them, and re-layouts: 6.39 us -> 2.85 us
  starting transfers between devices: 40.5 us -> 37.2 us
    ppermute x9, waiting for transfers between devices: 24.8 us -> 39.3 us  [along(): return lax.ppermute(x, 'grp', [(i, (i + d) % 4) for i in range(4)])]
    all_to_all x1, waiting for transfers between devices: 7.98 us -> 0.01 us  [all_along(): return lax.all_to_all(x, 'grp', split_axis=0, concat_axis=0, tiled=True)]
    pallas_call x4 -> x2, Pallas kernels: 9.51 us -> 4.7 us  [pack(): pl.pallas_call(functools.partial(pack_kernel, start), out_shape=(one, one...]
    unnamed x26 -> x6, local copies, waits for them, and re-layouts: 5.1 us -> 1.38 us
    all_to_all x3, waiting for transfers between devices: 19.4 us -> 21.5 us  [over_seq(): return lax.all_to_all(x, 'seq', split_axis=0, concat_axis=0, tiled=True)]
    ppermute x9, starting transfers between devices: 15.3 us -> 13.3 us  [along(): return lax.ppermute(x, 'grp', [(i, (i + d) % 4) for i in range(4)])]
    pallas_call x4 -> x3, Pallas kernels: 7.36 us -> 6.58 us  [put(): pl.pallas_call(functools.partial(put_later_kernel if later else put_kerne...]
  transfers between devices with their start and end apart: 14 -> 14, of which waited for: 7 -> 8; matrix products, arithmetic and copies ran while one was open for 1% -> 2% of each run, Pallas kernels for 23% -> 20%
where the time goes in v4:
time: 141 us; the launch traced here: 140 us
  waiting for transfers between devices  60.8 us (43%)
  starting transfers between devices  37.2 us (26%)
  Pallas kernels  36.3 us (26%)
  local copies, waits for them, and re-layouts  2.85 us (2%)
  matrix products  1.66 us (1%)
    ppermute x9, waiting for transfers between devices, along(): return lax.ppermute(x, 'grp', [(i, (i + d) % 4) for i in range(4)])  39.3 us
    all_to_all x3, waiting for transfers between devices, over_seq(): return lax.all_to_all(x, 'seq', split_axis=0, concat_axis=0, tiled=True)  21.5 us
    all_to_all x3, starting transfers between devices, over_seq(): return lax.all_to_all(x, 'seq', split_axis=0, concat_axis=0, tiled=True)  19.7 us
    ppermute x9, starting transfers between devices, along(): return lax.ppermute(x, 'grp', [(i, (i + d) % 4) for i in range(4)])  13.3 us
    pallas_call x1, Pallas kernels, attend(): pl.pallas_call(functools.partial(attend_kernel, steps), grid=(steps,), ou...  10.4 us
    pallas_call x2, Pallas kernels, dequantize(): pl.pallas_call(functools.partial(dequantize_kernel, start, per_step, step...  8.75 us
    pallas_call x3, Pallas kernels, put(): pl.pallas_call(functools.partial(put_later_kernel if later else put_kerne...  6.58 us
    pallas_call x2, Pallas kernels, pack(): pl.pallas_call(functools.partial(pack_kernel, start), out_shape=(one, one...  4.7 us
  transfers between devices with their start and end apart: 14, of which 8 were waited for; matrix products, arithmetic and copies ran while one was open for 2% of the time, Pallas kernels for 20%

profile of v4, /device:TPU:1, one launch (start us, length us, event | category | flops | bytes accessed | tf_op | source)
XLA Modules:
  0.0 140.3 jit_solution(14679867840503667064)
XLA Ops:
  1.3 4.3 %dequantize.2.refs_5_ = bf16[32,272,128]{2,1,0:T(8,128)(2,1)} custom-call(s32[2]{0:T(128)} %pad_add_fusion.place, s32[4,4]{1,0:T(4,128)} %lengths.3, s32[4,4]{1,0:T(4,128)} %padding.3, bf16[576,4096]{1,0:T(8,128)(2,1)} %bitcast.19, f32[32,576]{1,0:T(8,128)} %scale.3, s32[16,32]{1,0:T(8,128)} %bitcast.25, bf16[32,16,128]{2,1,0:T(8,128)(2,1)} %values.3), custom_call_target="tpu_custom_call" | custom-call | bytes 4456448 | tf_op jit(solution)/shard_map/dequantize/pallas_call | solution.py:103
  5.5 9.6 %all-to-all-start = ((bf16[32,272,128]{2,1,0:T(8,128)(2,1)}), bf16[32,272,128]{2,1,0:T(8,128)(2,1)S(1)}, u32[]{:S(2)}, u32[]{:S(2)}) async-start(bf16[32,272,128]{2,1,0:T(8,128)(2,1)} %dequantize.2.refs_5_), calls=%async_computation | async-start | bytes 4456448 | tf_op jit(solution)/shard_map/all_to_all | solution.py:459
  16.6 2.5 %split.1 = (bf16[288,512]{1,0:T(8,128)(2,1)}, bf16[288,512]{1,0:T(8,128)(2,1)}, bf16[288,512]{1,0:T(8,128)(2,1)}) custom-call(s32[14]{0:T(128)S(1)} %concatenate.4.table, bf16[4,576,512]{2,1,0:T(8,128)(2,1)} %bitcast.21), custom_call_target="tpu_custom_call" | custom-call | bytes 1048576 | tf_op jit(solution)/shard_map/split/pallas_call | solution.py:254
  20.4 2.4 %collective-permute-start.1 = (bf16[288,512]{1,0:T(8,128)(2,1)}, bf16[288,512]{1,0:T(8,128)(2,1)S(1)}, u32[]{:S(2)}, u32[]{:S(2)}) collective-permute-start(bf16[288,512]{1,0:T(8,128)(2,1)} %get-tuple-element.42), channel_id=1, source_target_pairs={{0,64},{32,96},{64,0},{96,32},{1,65},{33,97},{65,1},{97,33},{2,66}... | collective-permute-start | bytes 884744 | tf_op jit(solution)/shard_map/ppermute | solution.py:467
  24.0 4.5 %dequantize.3.refs_6_ = bf16[32,304,128]{2,1,0:T(8,128)(2,1)} custom-call(s32[2]{0:T(128)} %pad_add_fusion.place, s32[4,4]{1,0:T(4,128)} %lengths.3, s32[4,4]{1,0:T(4,128)} %padding.3, bf16[576,4096]{1,0:T(8,128)(2,1)} %bitcast.20, f32[32,576]{1,0:T(8,128)} %scale.3, s32[16,32]{1,0:T(8,128)} %bitcast.26, bf16[32,16,128]{2,1,0:T(8,128)(2,1)} %values.3), custom_call_target="tpu_custom_call" | custom-call | bytes 4980736 | tf_op jit(solution)/shard_map/dequantize/pallas_call | solution.py:103
  29.0 7.3 %collective-permute-done.1.in2.refs_2_ = bf16[288,512]{1,0:T(8,128)(2,1)S(1)} collective-permute-done((bf16[288,512]{1,0:T(8,128)(2,1)}, bf16[288,512]{1,0:T(8,128)(2,1)S(1)}, u32[]{:S(2)}, u32[]{:S(2)}) %collective-permute-start.1) | collective-permute-done | bytes 294944 | tf_op jit(solution)/shard_map/ppermute | solution.py:467
  37.7 7.2 %all-to-all-done.stripes = bf16[32,272,128]{2,1,0:T(8,128)(2,1)S(1)} async-done(((bf16[32,272,128]{2,1,0:T(8,128)(2,1)}), bf16[32,272,128]{2,1,0:T(8,128)(2,1)S(1)}, u32[]{:S(2)}, u32[]{:S(2)}) %all-to-all-start) | async-done | bytes 2228256 | tf_op jit(solution)/shard_map/all_to_all | solution.py:459
  45.8 2.3 %pack.2 = (bf16[12,272,128]{2,1,0:T(8,128)(2,1)}, bf16[12,272,128]{2,1,0:T(8,128)(2,1)}, bf16[12,272,128]{2,1,0:T(8,128)(2,1)}, bf16[4,12,576,128]{3,2,1,0:T(8,128)(2,1)}) custom-call(s32[14]{0:T(128)S(1)} %concatenate.4.table, bf16[32,272,128]{2,1,0:T(8,128)(2,1)S(1)} %all-to-all-done.stripes), custom_call_target="tpu_custom_call" | custom-call | bytes 6684672 | tf_op jit(solution)/shard_map/pack/pallas_call | solution.py:154
  49.3 2.4 %collective-permute-start.5 = (bf16[12,272,128]{2,1,0:T(8,128)(2,1)}, bf16[12,272,128]{2,1,0:T(8,128)(2,1)}, u32[]{:S(2)}, u32[]{:S(2)}) collective-permute-start(bf16[12,272,128]{2,1,0:T(8,128)(2,1)} %get-tuple-element.55), channel_id=1, source_target_pairs={{0,64},{32,96},{64,0},{96,32},{1,65},{33,97},{65,1},{97,33},{2,66}... | collective-permute-start | bytes 2506760 | tf_op jit(solution)/shard_map/ppermute | solution.py:467
  52.9 4.6 %all-to-all-start.1 = ((bf16[32,304,128]{2,1,0:T(8,128)(2,1)}), bf16[32,304,128]{2,1,0:T(8,128)(2,1)S(1)}, u32[]{:S(2)}, u32[]{:S(2)}) async-start(bf16[32,304,128]{2,1,0:T(8,128)(2,1)} %dequantize.3.refs_6_), calls=%async_computation.1 | async-start | bytes 4980736 | tf_op jit(solution)/shard_map/all_to_all | solution.py:459
  57.5 10.4 %attend.1 = bf16[512,640]{1,0:T(8,128)(2,1)} custom-call(s32[14]{0:T(128)S(1)} %concatenate.4.table, bf16[4,576,512]{2,1,0:T(8,128)(2,1)} %bitcast.23, bf16[288,512]{1,0:T(8,128)(2,1)S(1)} %collective-permute-done.in1.refs_1_, bf16[288,512]{1,0:T(8,128)(2,1)S(1)} %collective-permute-done.1.in2.refs_2_, ...), custom_call_target="tpu_custom_call" | custom-call | flops 42949672960 | tf_op jit(solution)/shard_map/attend/pallas_call | solution.py:368
  67.9 2.0 %collective-permute-done.4.refs_0_ = bf16[12,272,128]{2,1,0:T(8,128)(2,1)} collective-permute-done((bf16[12,272,128]{2,1,0:T(8,128)(2,1)}, bf16[12,272,128]{2,1,0:T(8,128)(2,1)}, u32[]{:S(2)}, u32[]{:S(2)}) %collective-permute-start.4) | collective-permute-done | bytes 835616 | tf_op jit(solution)/shard_map/ppermute | solution.py:467
  69.9 18.9 %collective-permute-done.5.refs_1_ = bf16[12,272,128]{2,1,0:T(8,128)(2,1)} collective-permute-done((bf16[12,272,128]{2,1,0:T(8,128)(2,1)}, bf16[12,272,128]{2,1,0:T(8,128)(2,1)}, u32[]{:S(2)}, u32[]{:S(2)}) %collective-permute-start.5) | collective-permute-done | bytes 835616 | tf_op jit(solution)/shard_map/ppermute | solution.py:467
  90.1 2.4 %pack.3 = (bf16[12,304,128]{2,1,0:T(8,128)(2,1)}, bf16[12,304,128]{2,1,0:T(8,128)(2,1)}, bf16[12,304,128]{2,1,0:T(8,128)(2,1)}, bf16[4,12,576,128]{3,2,1,0:T(8,128)(2,1)}) custom-call(s32[14]{0:T(128)S(1)} %concatenate.4.table, bf16[32,304,128]{2,1,0:T(8,128)(2,1)S(1)} %all-to-all-done.1.stripes, ...), custom_call_target="tpu_custom_call", output_to_operand_aliasing={{3}: (2, {})} | custom-call | bytes 7471104 | tf_op jit(solution)/shard_map/pack/pallas_call | solution.py:154
  94.2 1.9 %collective-permute-start.8 = (bf16[12,304,128]{2,1,0:T(8,128)(2,1)}, bf16[12,304,128]{2,1,0:T(8,128)(2,1)S(1)}, u32[]{:S(2)}, u32[]{:S(2)}) collective-permute-start(bf16[12,304,128]{2,1,0:T(8,128)(2,1)} %get-tuple-element.71), channel_id=1, source_target_pairs={{0,96},{32,0},{64,32},{96,64},{1,97},{33,1},{65,33},{97,65},{2,98}... | collective-permute-start | bytes 2801672 | tf_op jit(solution)/shard_map/ppermute | solution.py:467
  96.0 3.2 %put.3.refs_1_ = bf16[4,12,576,128]{3,2,1,0:T(8,128)(2,1)} custom-call(s32[14]{0:T(128)S(1)} %concatenate.4.table, bf16[12,272,128]{2,1,0:T(8,128)(2,1)} %collective-permute-done.4.refs_0_, bf16[12,272,128]{2,1,0:T(8,128)(2,1)} %collective-permute-done.5.refs_1_, ...), custom_call_target="tpu_custom_call", output_to_operand_aliasing={{}: (4, {})} | custom-call | flops 42949672960 | tf_op jit(solution)/shard_map/put/pallas_call | solution.py:214
  99.3 5.5 %all-to-all-start.2 = ((bf16[32,16,640]{2,1,0:T(8,128)(2,1)}), bf16[32,16,640]{2,1,0:T(8,128)(2,1)S(1)}, u32[]{:S(2)}, u32[]{:S(2)}) async-start(bf16[32,16,640]{2,1,0:T(8,128)(2,1)} %bitcast.24), calls=%async_computation.2 | async-start | bytes 1310720 | tf_op jit(solution)/shard_map/all_to_all | solution.py:459
  104.9 13.0 %all-to-all-done.2.partials = bf16[32,16,640]{2,1,0:T(8,128)(2,1)S(1)} async-done(((bf16[32,16,640]{2,1,0:T(8,128)(2,1)}), bf16[32,16,640]{2,1,0:T(8,128)(2,1)S(1)}, u32[]{:S(2)}, u32[]{:S(2)}) %all-to-all-start.2) | async-done | bytes 655392 | tf_op jit(solution)/shard_map/all_to_all | solution.py:459
  117.8 1.7 %join.1 = f32[4,16,640]{2,1,0:T(8,128)S(1)} custom-call(s32[14]{0:T(128)S(1)} %concatenate.4.table, bf16[32,16,640]{2,1,0:T(8,128)(2,1)S(1)} %all-to-all-done.2.partials), custom_call_target="tpu_custom_call" | custom-call | bytes 1048576 | tf_op jit(solution)/shard_map/join/pallas_call | solution.py:408
  120.2 3.3 %all-to-all-start.3 = ((f32[4,16,640]{2,1,0:T(8,128)}), f32[4,16,640]{2,1,0:T(8,128)S(1)}, u32[]{:S(2)}, u32[]{:S(2)}) async-start(f32[4,16,640]{2,1,0:T(8,128)} %copy-done), calls=%async_computation.3 | async-start | bytes 327680 | tf_op jit(solution)/shard_map/all_to_all | solution.py:463
  123.6 1.7 %fusion.scores = f32[4,16,4]{2,1,0:T(8,128)S(1)} fusion(bf16[4,4,576]{2,1,0:T(4,128)(2,1)S(1)} %copy-done.2, bf16[4,512,576]{1,2,0:T(8,128)(2,1)} %param.16, s32[]{:T(128)S(6)} %select_n.24, pred[16,4]{1,0:T(8,128)(4,1)S(1)} %iota_compare_fusion), kind=kOutput, calls=%fused_computation.1 | convolution fusion | flops 295424 | bytes 609348 | tf_op jit(solution)/shard_map/yeu,ynu->yen/dot_general | solution.py:438
  125.3 1.5 %put.4.refs_2_ = bf16[4,12,576,128]{3,2,1,0:T(8,128)(2,1)} custom-call(s32[14]{0:T(128)S(1)} %concatenate.4.table, bf16[12,304,128]{2,1,0:T(8,128)(2,1)S(1)} %collective-permute-done.9.refs_0_, bf16[4,12,576,128]{3,2,1,0:T(8,128)(2,1)} %put.3.refs_1_), custom_call_target="tpu_custom_call", output_to_operand_aliasing={{}: (2, {})} | custom-call | bytes 1867776 | tf_op jit(solution)/shard_map/put/pallas_call | solution.py:214
  126.8 10.6 %collective-permute-done.7.refs_0_ = bf16[12,304,128]{2,1,0:T(8,128)(2,1)S(1)} collective-permute-done((bf16[12,304,128]{2,1,0:T(8,128)(2,1)}, bf16[12,304,128]{2,1,0:T(8,128)(2,1)S(1)}, u32[]{:S(2)}, u32[]{:S(2)}) %collective-permute-start.7) | collective-permute-done | bytes 933920 | tf_op jit(solution)/shard_map/ppermute | solution.py:467
  137.4 1.8 %put.5 = bf16[4,12,576,128]{3,2,1,0:T(8,128)(2,1)} custom-call(s32[14]{0:T(128)S(1)} %concatenate.4.table, bf16[12,304,128]{2,1,0:T(8,128)(2,1)S(1)} %collective-permute-done.7.refs_0_, bf16[12,304,128]{2,1,0:T(8,128)(2,1)S(1)} %collective-permute-done.8.refs_1_, bf16[4,12,576,128]{3,2,1,0:T(8,128)(2,1)} %put.4.refs_2_), custom_call_target="tpu_custom_call", output_to_operand_aliasing={{}: (3, {})} | custom-call | bytes 3735552 | tf_op jit(solution)/shard_map/put/pallas_call | solution.py:214
  (29 shorter events, 14.5 us)
Async XLA Ops:
  5.5 39.3 %all-to-all-start = ((bf16[32,272,128]{2,1,0:T(8,128)(2,1)}), bf16[32,272,128]{2,1,0:T(8,128)(2,1)S(1)}, u32[]{:S(2)}, u32[]{:S(2)}) async-start(bf16[32,272,128]{2,1,0:T(8,128)(2,1)} %dequantize.2.refs_5_), calls=%async_computation | async-start | bytes 4456448 | tf_op jit(solution)/shard_map/all_to_all | solution.py:459
  19.1 9.9 %collective-permute-start = (bf16[288,512]{1,0:T(8,128)(2,1)}, bf16[288,512]{1,0:T(8,128)(2,1)S(1)}, u32[]{:S(2)}, u32[]{:S(2)}) collective-permute-start(bf16[288,512]{1,0:T(8,128)(2,1)} %get-tuple-element.41), channel_id=1, source_target_pairs={{0,32},{32,64},{64,96},{96,0},{1,33},{33,65},{65,97},{97,1},{2,34}... | collective-permute-start | bytes 884744 | tf_op jit(solution)/shard_map/ppermute | solution.py:467
  20.4 15.9 %collective-permute-start.1 = (bf16[288,512]{1,0:T(8,128)(2,1)}, bf16[288,512]{1,0:T(8,128)(2,1)S(1)}, u32[]{:S(2)}, u32[]{:S(2)}) collective-permute-start(bf16[288,512]{1,0:T(8,128)(2,1)} %get-tuple-element.42), channel_id=1, source_target_pairs={{0,64},{32,96},{64,0},{96,32},{1,65},{33,97},{65,1},{97,33},{2,66}... | collective-permute-start | bytes 884744 | tf_op jit(solution)/shard_map/ppermute | solution.py:467
  22.9 13.4 %collective-permute-start.2 = (bf16[288,512]{1,0:T(8,128)(2,1)}, bf16[288,512]{1,0:T(8,128)(2,1)S(1)}, u32[]{:S(2)}, u32[]{:S(2)}) collective-permute-start(bf16[288,512]{1,0:T(8,128)(2,1)} %get-tuple-element.43), channel_id=1, source_target_pairs={{0,96},{32,0},{64,32},{96,64},{1,97},{33,1},{65,33},{97,65},{2,98}... | collective-permute-start | bytes 884744 | tf_op jit(solution)/shard_map/ppermute | solution.py:467
  37.0 0.7 copy-start.1
  44.9 12.6 %collective-permute-start.3 = (bf16[288,512]{1,0:T(8,128)(2,1)}, bf16[288,512]{1,0:T(8,128)(2,1)}, u32[]{:S(2)}, u32[]{:S(2)}) collective-permute-start(bf16[288,512]{1,0:T(8,128)(2,1)} %copy-done.1), channel_id=1, source_target_pairs={{0,1},{1,0},{2,3},{3,2},{4,5},{5,4},{6,7},{7,6},{8,9},{9,8},{10,11... | collective-permute-start | bytes 884744 | tf_op jit(solution)/shard_map/ppermute | solution.py:505
  48.1 21.8 %collective-permute-start.4 = (bf16[12,272,128]{2,1,0:T(8,128)(2,1)}, bf16[12,272,128]{2,1,0:T(8,128)(2,1)}, u32[]{:S(2)}, u32[]{:S(2)}) collective-permute-start(bf16[12,272,128]{2,1,0:T(8,128)(2,1)} %get-tuple-element.54), channel_id=1, source_target_pairs={{0,32},{32,64},{64,96},{96,0},{1,33},{33,65},{65,97},{97,1},{2,34}... | collective-permute-start | bytes 2506760 | tf_op jit(solution)/shard_map/ppermute | solution.py:467
  49.3 39.4 %collective-permute-start.5 = (bf16[12,272,128]{2,1,0:T(8,128)(2,1)}, bf16[12,272,128]{2,1,0:T(8,128)(2,1)}, u32[]{:S(2)}, u32[]{:S(2)}) collective-permute-start(bf16[12,272,128]{2,1,0:T(8,128)(2,1)} %get-tuple-element.55), channel_id=1, source_target_pairs={{0,64},{32,96},{64,0},{96,32},{1,65},{33,97},{65,1},{97,33},{2,66}... | collective-permute-start | bytes 2506760 | tf_op jit(solution)/shard_map/ppermute | solution.py:467
  51.8 37.0 %collective-permute-start.6 = (bf16[12,272,128]{2,1,0:T(8,128)(2,1)}, bf16[12,272,128]{2,1,0:T(8,128)(2,1)}, u32[]{:S(2)}, u32[]{:S(2)}) collective-permute-start(bf16[12,272,128]{2,1,0:T(8,128)(2,1)} %get-tuple-element.56), channel_id=1, source_target_pairs={{0,96},{32,0},{64,32},{96,64},{1,97},{33,1},{65,33},{97,65},{2,98}... | collective-permute-start | bytes 2506760 | tf_op jit(solution)/shard_map/ppermute | solution.py:467
  52.9 37.1 %all-to-all-start.1 = ((bf16[32,304,128]{2,1,0:T(8,128)(2,1)}), bf16[32,304,128]{2,1,0:T(8,128)(2,1)S(1)}, u32[]{:S(2)}, u32[]{:S(2)}) async-start(bf16[32,304,128]{2,1,0:T(8,128)(2,1)} %dequantize.3.refs_6_), calls=%async_computation.1 | async-start | bytes 4980736 | tf_op jit(solution)/shard_map/all_to_all | solution.py:459
  92.5 31.1 %copy-start.2 = (bf16[4,4,576]{2,1,0:T(4,128)(2,1)S(1)}, bf16[4,4,576]{2,1,0:T(4,128)(2,1)}, u32[]{:S(2)}) copy-start(bf16[4,4,576]{2,1,0:T(4,128)(2,1)} %fresh.1) | copy-start | bytes 55300
  92.5 32.7 %collective-permute-start.9 = (bf16[12,304,128]{2,1,0:T(8,128)(2,1)}, bf16[12,304,128]{2,1,0:T(8,128)(2,1)S(1)}, u32[]{:S(2)}, u32[]{:S(2)}) collective-permute-start(bf16[12,304,128]{2,1,0:T(8,128)(2,1)} %get-tuple-element.72), channel_id=1, source_target_pairs={{0,64},{32,96},{64,0},{96,32},{1,65},{33,97},{65,1},{97,33},{2,66}... | collective-permute-start | bytes 2801672 | tf_op jit(solution)/shard_map/ppermute | solution.py:467
  93.4 44.0 %collective-permute-start.7 = (bf16[12,304,128]{2,1,0:T(8,128)(2,1)}, bf16[12,304,128]{2,1,0:T(8,128)(2,1)S(1)}, u32[]{:S(2)}, u32[]{:S(2)}) collective-permute-start(bf16[12,304,128]{2,1,0:T(8,128)(2,1)} %get-tuple-element.70), channel_id=1, source_target_pairs={{0,32},{32,64},{64,96},{96,0},{1,33},{33,65},{65,97},{97,1},{2,34}... | collective-permute-start | bytes 2801672 | tf_op jit(solution)/shard_map/ppermute | solution.py:467
  94.2 43.3 %collective-permute-start.8 = (bf16[12,304,128]{2,1,0:T(8,128)(2,1)}, bf16[12,304,128]{2,1,0:T(8,128)(2,1)S(1)}, u32[]{:S(2)}, u32[]{:S(2)}) collective-permute-start(bf16[12,304,128]{2,1,0:T(8,128)(2,1)} %get-tuple-element.71), channel_id=1, source_target_pairs={{0,96},{32,0},{64,32},{96,64},{1,97},{33,1},{65,33},{97,65},{2,98}... | collective-permute-start | bytes 2801672 | tf_op jit(solution)/shard_map/ppermute | solution.py:467
  99.3 18.6 %all-to-all-start.2 = ((bf16[32,16,640]{2,1,0:T(8,128)(2,1)}), bf16[32,16,640]{2,1,0:T(8,128)(2,1)S(1)}, u32[]{:S(2)}, u32[]{:S(2)}) async-start(bf16[32,16,640]{2,1,0:T(8,128)(2,1)} %bitcast.24), calls=%async_computation.2 | async-start | bytes 1310720 | tf_op jit(solution)/shard_map/all_to_all | solution.py:459
  119.6 0.7 copy-start
  120.2 19.0 %all-to-all-start.3 = ((f32[4,16,640]{2,1,0:T(8,128)}), f32[4,16,640]{2,1,0:T(8,128)S(1)}, u32[]{:S(2)}, u32[]{:S(2)}) async-start(f32[4,16,640]{2,1,0:T(8,128)} %copy-done), calls=%async_computation.3 | async-start | bytes 327680 | tf_op jit(solution)/shard_map/all_to_all | solution.py:463

commit v5 on v4

--- a/solution.py
+++ b/solution.py
@@ -56,7 +56,7 @@
     return target, empty
 
 
-def dequantize_kernel(start, per_step, total, place, lengths, padding, packed, scale, channels, values, out, scales, marks):
+def dequantize_kernel(start, per_step, total, lengths, padding, packed, scale, channels, values, out, scales, marks):
     rows = packed.shape[0]
     width = per_step * 16
     step = pl.program_id(0)
@@ -74,10 +74,11 @@
             scales[i] = turned[:, i * per_step : (i + 1) * per_step]
             marks[i] = jnp.concatenate([mark[i * per_step + b : i * per_step + b + 1] for b in range(per_step)], axis=1)
 
-    group, empty, before = place[0], 0, 0
+    group, stripe = lax.axis_index("grp"), lax.axis_index("seq")
+    empty, before = 0, 0
     for r in range(4):
         before = before + lengths[group, r]
-        empty = jnp.where(place[1] == before - 1, padding[group, r], empty)
+        empty = jnp.where(stripe == before - 1, padding[group, r], empty)
     ids = (lax.broadcasted_iota(jnp.int32, (rows, width), 0) + start).astype(jnp.float32)
     onehot = (ids == marks[step]).astype(jnp.bfloat16)
     flat = values[...].reshape(width, 128)
@@ -95,7 +96,7 @@
         out[b] = latent.astype(jnp.bfloat16)
 
 
-def dequantize(start, rows, place, lengths, padding, packed, scale, channels, values):
+def dequantize(start, rows, lengths, padding, packed, scale, channels, values):
     packed, values = [pltpu.with_memory_space_constraint(x, pltpu.HBM) for x in (packed, values)]
     blocks = scale.shape[0]
     per_step = 16
@@ -105,7 +106,6 @@
         grid=(steps,),
         out_shape=pltpu.HBM((blocks, rows, 128), jnp.bfloat16),
         in_specs=[
-            SMEM,
             SMEM,
             SMEM,
             pl.BlockSpec((pl.Element(rows), pl.Element(per_step * 128)), lambda i: (start, i * per_step * 128)),
@@ -121,7 +121,7 @@
         compiler_params=params(60),
         cost_estimate=pl.CostEstimate(flops=0, bytes_accessed=4 * blocks * rows * 128, transcendentals=0),
         name="dequantize",
-    )(place, lengths, padding, packed, scale, channels, values)
+    )(lengths, padding, packed, scale, channels, values)
 
 
 def collect(table, d, stripes, target, zeros, sem):
@@ -489,7 +489,7 @@
     starts = [sum(CHUNKS[:i]) for i in range(len(CHUNKS))]
     last = len(CHUNKS) - 1
     latent = [
-        dequantize(start, rows, place, lengths, padding, packed, block_channel_scale, channels, outlier_values)
+        dequantize(start, rows, lengths, padding, packed, block_channel_scale, channels, outlier_values)
         for start, rows in zip(starts, CHUNKS)
     ]
     turned = queries.transpose(0, 2, 1)

time: 141 us -> 140 us (level)
  no operation moved by 1% of the time
where the time goes in v5:
time: 140 us
  waiting for transfers between devices  60.7 us (43%)
  starting transfers between devices  37.2 us (27%)
  Pallas kernels  36.3 us (26%)
  local copies, waits for them, and re-layouts  2.85 us (2%)
  matrix products  1.66 us (1%)
    ppermute x9, waiting for transfers between devices, along(): return lax.ppermute(x, 'grp', [(i, (i + d) % 4) for i in range(4)])  39.3 us
    all_to_all x3, waiting for transfers between devices, over_seq(): return lax.all_to_all(x, 'seq', split_axis=0, concat_axis=0, tiled=True)  21.4 us
    all_to_all x3, starting transfers between devices, over_seq(): return lax.all_to_all(x, 'seq', split_axis=0, concat_axis=0, tiled=True)  19.7 us
    ppermute x9, starting transfers between devices, along(): return lax.ppermute(x, 'grp', [(i, (i + d) % 4) for i in range(4)])  13.3 us
    pallas_call x1, Pallas kernels, attend(): pl.pallas_call(functools.partial(attend_kernel, steps), grid=(steps,), ou...  10.4 us
    pallas_call x2, Pallas kernels, dequantize(): pl.pallas_call(functools.partial(dequantize_kernel, start, per_step, step...  8.77 us
    pallas_call x3, Pallas kernels, put(): pl.pallas_call(functools.partial(put_later_kernel if later else put_kerne...  6.58 us
    pallas_call x2, Pallas kernels, pack(): pl.pallas_call(functools.partial(pack_kernel, start), out_shape=(one, one...  4.7 us
  transfers between devices with their start and end apart: 14, of which 8 were waited for; matrix products, arithmetic and copies ran while one was open for 2% of the time, Pallas kernels for 20%

profile of v5, /device:TPU:1, one launch (start us, length us, event | category | flops | bytes accessed | tf_op | source)
XLA Modules:
  0.0 139.6 jit_solution(977014090969442510)
XLA Ops:
  0.6 4.3 %dequantize.2.refs_5_ = bf16[32,272,128]{2,1,0:T(8,128)(2,1)} custom-call(s32[4,4]{1,0:T(4,128)} %lengths.3, s32[4,4]{1,0:T(4,128)} %padding.3, bf16[576,4096]{1,0:T(8,128)(2,1)} %bitcast.19, f32[32,576]{1,0:T(8,128)} %scale.3, s32[16,32]{1,0:T(8,128)} %bitcast.25, bf16[32,16,128]{2,1,0:T(8,128)(2,1)} %values.3), custom_call_target="tpu_custom_call" | custom-call | bytes 4456448 | tf_op jit(solution)/shard_map/dequantize/pallas_call | solution.py:104
  4.9 9.6 %all-to-all-start = ((bf16[32,272,128]{2,1,0:T(8,128)(2,1)}), bf16[32,272,128]{2,1,0:T(8,128)(2,1)S(1)}, u32[]{:S(2)}, u32[]{:S(2)}) async-start(bf16[32,272,128]{2,1,0:T(8,128)(2,1)} %dequantize.2.refs_5_), calls=%async_computation | async-start | bytes 4456448 | tf_op jit(solution)/shard_map/all_to_all | solution.py:459
  16.0 2.5 %split.1 = (bf16[288,512]{1,0:T(8,128)(2,1)}, bf16[288,512]{1,0:T(8,128)(2,1)}, bf16[288,512]{1,0:T(8,128)(2,1)}) custom-call(s32[14]{0:T(128)S(1)} %concatenate.3.table, bf16[4,576,512]{2,1,0:T(8,128)(2,1)} %bitcast.21), custom_call_target="tpu_custom_call" | custom-call | bytes 1048576 | tf_op jit(solution)/shard_map/split/pallas_call | solution.py:254
  19.8 2.5 %collective-permute-start.1 = (bf16[288,512]{1,0:T(8,128)(2,1)}, bf16[288,512]{1,0:T(8,128)(2,1)S(1)}, u32[]{:S(2)}, u32[]{:S(2)}) collective-permute-start(bf16[288,512]{1,0:T(8,128)(2,1)} %get-tuple-element.42), channel_id=1, source_target_pairs={{0,64},{32,96},{64,0},{96,32},{1,65},{33,97},{65,1},{97,33},{2,66}... | collective-permute-start | bytes 884744 | tf_op jit(solution)/shard_map/ppermute | solution.py:467
  23.4 4.5 %dequantize.3.refs_6_ = bf16[32,304,128]{2,1,0:T(8,128)(2,1)} custom-call(s32[4,4]{1,0:T(4,128)} %lengths.3, s32[4,4]{1,0:T(4,128)} %padding.3, bf16[576,4096]{1,0:T(8,128)(2,1)} %bitcast.20, f32[32,576]{1,0:T(8,128)} %scale.3, s32[16,32]{1,0:T(8,128)} %bitcast.26, bf16[32,16,128]{2,1,0:T(8,128)(2,1)} %values.3), custom_call_target="tpu_custom_call" | custom-call | bytes 4980736 | tf_op jit(solution)/shard_map/dequantize/pallas_call | solution.py:104
  28.4 7.3 %collective-permute-done.1.in2.refs_2_ = bf16[288,512]{1,0:T(8,128)(2,1)S(1)} collective-permute-done((bf16[288,512]{1,0:T(8,128)(2,1)}, bf16[288,512]{1,0:T(8,128)(2,1)S(1)}, u32[]{:S(2)}, u32[]{:S(2)}) %collective-permute-start.1) | collective-permute-done | bytes 294944 | tf_op jit(solution)/shard_map/ppermute | solution.py:467
  37.1 7.2 %all-to-all-done.stripes = bf16[32,272,128]{2,1,0:T(8,128)(2,1)S(1)} async-done(((bf16[32,272,128]{2,1,0:T(8,128)(2,1)}), bf16[32,272,128]{2,1,0:T(8,128)(2,1)S(1)}, u32[]{:S(2)}, u32[]{:S(2)}) %all-to-all-start) | async-done | bytes 2228256 | tf_op jit(solution)/shard_map/all_to_all | solution.py:459
  45.1 2.3 %pack.2 = (bf16[12,272,128]{2,1,0:T(8,128)(2,1)}, bf16[12,272,128]{2,1,0:T(8,128)(2,1)}, bf16[12,272,128]{2,1,0:T(8,128)(2,1)}, bf16[4,12,576,128]{3,2,1,0:T(8,128)(2,1)}) custom-call(s32[14]{0:T(128)S(1)} %concatenate.3.table, bf16[32,272,128]{2,1,0:T(8,128)(2,1)S(1)} %all-to-all-done.stripes), custom_call_target="tpu_custom_call" | custom-call | bytes 6684672 | tf_op jit(solution)/shard_map/pack/pallas_call | solution.py:154
  48.7 2.5 %collective-permute-start.5 = (bf16[12,272,128]{2,1,0:T(8,128)(2,1)}, bf16[12,272,128]{2,1,0:T(8,128)(2,1)}, u32[]{:S(2)}, u32[]{:S(2)}) collective-permute-start(bf16[12,272,128]{2,1,0:T(8,128)(2,1)} %get-tuple-element.55), channel_id=1, source_target_pairs={{0,64},{32,96},{64,0},{96,32},{1,65},{33,97},{65,1},{97,33},{2,66}... | collective-permute-start | bytes 2506760 | tf_op jit(solution)/shard_map/ppermute | solution.py:467
  52.3 4.6 %all-to-all-start.1 = ((bf16[32,304,128]{2,1,0:T(8,128)(2,1)}), bf16[32,304,128]{2,1,0:T(8,128)(2,1)S(1)}, u32[]{:S(2)}, u32[]{:S(2)}) async-start(bf16[32,304,128]{2,1,0:T(8,128)(2,1)} %dequantize.3.refs_6_), calls=%async_computation.1 | async-start | bytes 4980736 | tf_op jit(solution)/shard_map/all_to_all | solution.py:459
  56.9 10.4 %attend.1 = bf16[512,640]{1,0:T(8,128)(2,1)} custom-call(s32[14]{0:T(128)S(1)} %concatenate.3.table, bf16[4,576,512]{2,1,0:T(8,128)(2,1)} %bitcast.23, bf16[288,512]{1,0:T(8,128)(2,1)S(1)} %collective-permute-done.in1.refs_1_, bf16[288,512]{1,0:T(8,128)(2,1)S(1)} %collective-permute-done.1.in2.refs_2_, ...), custom_call_target="tpu_custom_call" | custom-call | flops 42949672960 | tf_op jit(solution)/shard_map/attend/pallas_call | solution.py:368
  67.3 2.0 %collective-permute-done.4.refs_0_ = bf16[12,272,128]{2,1,0:T(8,128)(2,1)} collective-permute-done((bf16[12,272,128]{2,1,0:T(8,128)(2,1)}, bf16[12,272,128]{2,1,0:T(8,128)(2,1)}, u32[]{:S(2)}, u32[]{:S(2)}) %collective-permute-start.4) | collective-permute-done | bytes 835616 | tf_op jit(solution)/shard_map/ppermute | solution.py:467
  69.2 18.9 %collective-permute-done.5.refs_1_ = bf16[12,272,128]{2,1,0:T(8,128)(2,1)} collective-permute-done((bf16[12,272,128]{2,1,0:T(8,128)(2,1)}, bf16[12,272,128]{2,1,0:T(8,128)(2,1)}, u32[]{:S(2)}, u32[]{:S(2)}) %collective-permute-start.5) | collective-permute-done | bytes 835616 | tf_op jit(solution)/shard_map/ppermute | solution.py:467
  89.5 2.4 %pack.3 = (bf16[12,304,128]{2,1,0:T(8,128)(2,1)}, bf16[12,304,128]{2,1,0:T(8,128)(2,1)}, bf16[12,304,128]{2,1,0:T(8,128)(2,1)}, bf16[4,12,576,128]{3,2,1,0:T(8,128)(2,1)}) custom-call(s32[14]{0:T(128)S(1)} %concatenate.3.table, bf16[32,304,128]{2,1,0:T(8,128)(2,1)S(1)} %all-to-all-done.1.stripes, ...), custom_call_target="tpu_custom_call", output_to_operand_aliasing={{3}: (2, {})} | custom-call | bytes 7471104 | tf_op jit(solution)/shard_map/pack/pallas_call | solution.py:154
  93.5 1.9 %collective-permute-start.8 = (bf16[12,304,128]{2,1,0:T(8,128)(2,1)}, bf16[12,304,128]{2,1,0:T(8,128)(2,1)S(1)}, u32[]{:S(2)}, u32[]{:S(2)}) collective-permute-start(bf16[12,304,128]{2,1,0:T(8,128)(2,1)} %get-tuple-element.71), channel_id=1, source_target_pairs={{0,96},{32,0},{64,32},{96,64},{1,97},{33,1},{65,33},{97,65},{2,98}... | collective-permute-start | bytes 2801672 | tf_op jit(solution)/shard_map/ppermute | solution.py:467
  95.4 3.2 %put.3.refs_1_ = bf16[4,12,576,128]{3,2,1,0:T(8,128)(2,1)} custom-call(s32[14]{0:T(128)S(1)} %concatenate.3.table, bf16[12,272,128]{2,1,0:T(8,128)(2,1)} %collective-permute-done.4.refs_0_, bf16[12,272,128]{2,1,0:T(8,128)(2,1)} %collective-permute-done.5.refs_1_, ...), custom_call_target="tpu_custom_call", output_to_operand_aliasing={{}: (4, {})} | custom-call | flops 42949672960 | tf_op jit(solution)/shard_map/put/pallas_call | solution.py:214
  98.6 5.5 %all-to-all-start.2 = ((bf16[32,16,640]{2,1,0:T(8,128)(2,1)}), bf16[32,16,640]{2,1,0:T(8,128)(2,1)S(1)}, u32[]{:S(2)}, u32[]{:S(2)}) async-start(bf16[32,16,640]{2,1,0:T(8,128)(2,1)} %bitcast.24), calls=%async_computation.2 | async-start | bytes 1310720 | tf_op jit(solution)/shard_map/all_to_all | solution.py:459
  104.2 13.0 %all-to-all-done.2.partials = bf16[32,16,640]{2,1,0:T(8,128)(2,1)S(1)} async-done(((bf16[32,16,640]{2,1,0:T(8,128)(2,1)}), bf16[32,16,640]{2,1,0:T(8,128)(2,1)S(1)}, u32[]{:S(2)}, u32[]{:S(2)}) %all-to-all-start.2) | async-done | bytes 655392 | tf_op jit(solution)/shard_map/all_to_all | solution.py:459
  117.2 1.7 %join.1 = f32[4,16,640]{2,1,0:T(8,128)S(1)} custom-call(s32[14]{0:T(128)S(1)} %concatenate.3.table, bf16[32,16,640]{2,1,0:T(8,128)(2,1)S(1)} %all-to-all-done.2.partials), custom_call_target="tpu_custom_call" | custom-call | bytes 1048576 | tf_op jit(solution)/shard_map/join/pallas_call | solution.py:408
  119.6 3.3 %all-to-all-start.3 = ((f32[4,16,640]{2,1,0:T(8,128)}), f32[4,16,640]{2,1,0:T(8,128)S(1)}, u32[]{:S(2)}, u32[]{:S(2)}) async-start(f32[4,16,640]{2,1,0:T(8,128)} %copy-done), calls=%async_computation.3 | async-start | bytes 327680 | tf_op jit(solution)/shard_map/all_to_all | solution.py:463
  123.0 1.7 %fusion.scores = f32[4,16,4]{2,1,0:T(8,128)S(1)} fusion(bf16[4,4,576]{2,1,0:T(4,128)(2,1)S(1)} %copy-done.2, bf16[4,512,576]{1,2,0:T(8,128)(2,1)} %param.16, s32[]{:T(128)S(6)} %select_n.24, pred[16,4]{1,0:T(8,128)(4,1)S(1)} %iota_compare_fusion), kind=kOutput, calls=%fused_computation.1 | convolution fusion | flops 295424 | bytes 609348 | tf_op jit(solution)/shard_map/yeu,ynu->yen/dot_general | solution.py:438
  124.6 1.5 %put.4.refs_2_ = bf16[4,12,576,128]{3,2,1,0:T(8,128)(2,1)} custom-call(s32[14]{0:T(128)S(1)} %concatenate.3.table, bf16[12,304,128]{2,1,0:T(8,128)(2,1)S(1)} %collective-permute-done.9.refs_0_, bf16[4,12,576,128]{3,2,1,0:T(8,128)(2,1)} %put.3.refs_1_), custom_call_target="tpu_custom_call", output_to_operand_aliasing={{}: (2, {})} | custom-call | bytes 1867776 | tf_op jit(solution)/shard_map/put/pallas_call | solution.py:214
  126.2 10.6 %collective-permute-done.7.refs_0_ = bf16[12,304,128]{2,1,0:T(8,128)(2,1)S(1)} collective-permute-done((bf16[12,304,128]{2,1,0:T(8,128)(2,1)}, bf16[12,304,128]{2,1,0:T(8,128)(2,1)S(1)}, u32[]{:S(2)}, u32[]{:S(2)}) %collective-permute-start.7) | collective-permute-done | bytes 933920 | tf_op jit(solution)/shard_map/ppermute | solution.py:467
  136.8 1.8 %put.5 = bf16[4,12,576,128]{3,2,1,0:T(8,128)(2,1)} custom-call(s32[14]{0:T(128)S(1)} %concatenate.3.table, bf16[12,304,128]{2,1,0:T(8,128)(2,1)S(1)} %collective-permute-done.7.refs_0_, bf16[12,304,128]{2,1,0:T(8,128)(2,1)S(1)} %collective-permute-done.8.refs_1_, bf16[4,12,576,128]{3,2,1,0:T(8,128)(2,1)} %put.4.refs_2_), custom_call_target="tpu_custom_call", output_to_operand_aliasing={{}: (3, {})} | custom-call | bytes 3735552 | tf_op jit(solution)/shard_map/put/pallas_call | solution.py:214
  (28 shorter events, 13.8 us)
Async XLA Ops:
  4.9 39.3 %all-to-all-start = ((bf16[32,272,128]{2,1,0:T(8,128)(2,1)}), bf16[32,272,128]{2,1,0:T(8,128)(2,1)S(1)}, u32[]{:S(2)}, u32[]{:S(2)}) async-start(bf16[32,272,128]{2,1,0:T(8,128)(2,1)} %dequantize.2.refs_5_), calls=%async_computation | async-start | bytes 4456448 | tf_op jit(solution)/shard_map/all_to_all | solution.py:459
  18.5 9.9 %collective-permute-start = (bf16[288,512]{1,0:T(8,128)(2,1)}, bf16[288,512]{1,0:T(8,128)(2,1)S(1)}, u32[]{:S(2)}, u32[]{:S(2)}) collective-permute-start(bf16[288,512]{1,0:T(8,128)(2,1)} %get-tuple-element.41), channel_id=1, source_target_pairs={{0,32},{32,64},{64,96},{96,0},{1,33},{33,65},{65,97},{97,1},{2,34}... | collective-permute-start | bytes 884744 | tf_op jit(solution)/shard_map/ppermute | solution.py:467
  19.8 15.9 %collective-permute-start.1 = (bf16[288,512]{1,0:T(8,128)(2,1)}, bf16[288,512]{1,0:T(8,128)(2,1)S(1)}, u32[]{:S(2)}, u32[]{:S(2)}) collective-permute-start(bf16[288,512]{1,0:T(8,128)(2,1)} %get-tuple-element.42), channel_id=1, source_target_pairs={{0,64},{32,96},{64,0},{96,32},{1,65},{33,97},{65,1},{97,33},{2,66}... | collective-permute-start | bytes 884744 | tf_op jit(solution)/shard_map/ppermute | solution.py:467
  22.2 13.4 %collective-permute-start.2 = (bf16[288,512]{1,0:T(8,128)(2,1)}, bf16[288,512]{1,0:T(8,128)(2,1)S(1)}, u32[]{:S(2)}, u32[]{:S(2)}) collective-permute-start(bf16[288,512]{1,0:T(8,128)(2,1)} %get-tuple-element.43), channel_id=1, source_target_pairs={{0,96},{32,0},{64,32},{96,64},{1,97},{33,1},{65,33},{97,65},{2,98}... | collective-permute-start | bytes 884744 | tf_op jit(solution)/shard_map/ppermute | solution.py:467
  36.3 0.7 copy-start.1
  44.2 12.6 %collective-permute-start.3 = (bf16[288,512]{1,0:T(8,128)(2,1)}, bf16[288,512]{1,0:T(8,128)(2,1)}, u32[]{:S(2)}, u32[]{:S(2)}) collective-permute-start(bf16[288,512]{1,0:T(8,128)(2,1)} %copy-done.1), channel_id=1, source_target_pairs={{0,1},{1,0},{2,3},{3,2},{4,5},{5,4},{6,7},{7,6},{8,9},{9,8},{10,11... | collective-permute-start | bytes 884744 | tf_op jit(solution)/shard_map/ppermute | solution.py:505
  47.4 21.8 %collective-permute-start.4 = (bf16[12,272,128]{2,1,0:T(8,128)(2,1)}, bf16[12,272,128]{2,1,0:T(8,128)(2,1)}, u32[]{:S(2)}, u32[]{:S(2)}) collective-permute-start(bf16[12,272,128]{2,1,0:T(8,128)(2,1)} %get-tuple-element.54), channel_id=1, source_target_pairs={{0,32},{32,64},{64,96},{96,0},{1,33},{33,65},{65,97},{97,1},{2,34}... | collective-permute-start | bytes 2506760 | tf_op jit(solution)/shard_map/ppermute | solution.py:467
  48.7 39.4 %collective-permute-start.5 = (bf16[12,272,128]{2,1,0:T(8,128)(2,1)}, bf16[12,272,128]{2,1,0:T(8,128)(2,1)}, u32[]{:S(2)}, u32[]{:S(2)}) collective-permute-start(bf16[12,272,128]{2,1,0:T(8,128)(2,1)} %get-tuple-element.55), channel_id=1, source_target_pairs={{0,64},{32,96},{64,0},{96,32},{1,65},{33,97},{65,1},{97,33},{2,66}... | collective-permute-start | bytes 2506760 | tf_op jit(solution)/shard_map/ppermute | solution.py:467
  51.2 37.0 %collective-permute-start.6 = (bf16[12,272,128]{2,1,0:T(8,128)(2,1)}, bf16[12,272,128]{2,1,0:T(8,128)(2,1)}, u32[]{:S(2)}, u32[]{:S(2)}) collective-permute-start(bf16[12,272,128]{2,1,0:T(8,128)(2,1)} %get-tuple-element.56), channel_id=1, source_target_pairs={{0,96},{32,0},{64,32},{96,64},{1,97},{33,1},{65,33},{97,65},{2,98}... | collective-permute-start | bytes 2506760 | tf_op jit(solution)/shard_map/ppermute | solution.py:467
  52.3 37.2 %all-to-all-start.1 = ((bf16[32,304,128]{2,1,0:T(8,128)(2,1)}), bf16[32,304,128]{2,1,0:T(8,128)(2,1)S(1)}, u32[]{:S(2)}, u32[]{:S(2)}) async-start(bf16[32,304,128]{2,1,0:T(8,128)(2,1)} %dequantize.3.refs_6_), calls=%async_computation.1 | async-start | bytes 4980736 | tf_op jit(solution)/shard_map/all_to_all | solution.py:459
  91.9 31.1 %copy-start.2 = (bf16[4,4,576]{2,1,0:T(4,128)(2,1)S(1)}, bf16[4,4,576]{2,1,0:T(4,128)(2,1)}, u32[]{:S(2)}) copy-start(bf16[4,4,576]{2,1,0:T(4,128)(2,1)} %fresh.1) | copy-start | bytes 55300
  91.9 32.7 %collective-permute-start.9 = (bf16[12,304,128]{2,1,0:T(8,128)(2,1)}, bf16[12,304,128]{2,1,0:T(8,128)(2,1)S(1)}, u32[]{:S(2)}, u32[]{:S(2)}) collective-permute-start(bf16[12,304,128]{2,1,0:T(8,128)(2,1)} %get-tuple-element.72), channel_id=1, source_target_pairs={{0,64},{32,96},{64,0},{96,32},{1,65},{33,97},{65,1},{97,33},{2,66}... | collective-permute-start | bytes 2801672 | tf_op jit(solution)/shard_map/ppermute | solution.py:467
  92.7 44.0 %collective-permute-start.7 = (bf16[12,304,128]{2,1,0:T(8,128)(2,1)}, bf16[12,304,128]{2,1,0:T(8,128)(2,1)S(1)}, u32[]{:S(2)}, u32[]{:S(2)}) collective-permute-start(bf16[12,304,128]{2,1,0:T(8,128)(2,1)} %get-tuple-element.70), channel_id=1, source_target_pairs={{0,32},{32,64},{64,96},{96,0},{1,33},{33,65},{65,97},{97,1},{2,34}... | collective-permute-start | bytes 2801672 | tf_op jit(solution)/shard_map/ppermute | solution.py:467
  93.5 43.3 %collective-permute-start.8 = (bf16[12,304,128]{2,1,0:T(8,128)(2,1)}, bf16[12,304,128]{2,1,0:T(8,128)(2,1)S(1)}, u32[]{:S(2)}, u32[]{:S(2)}) collective-permute-start(bf16[12,304,128]{2,1,0:T(8,128)(2,1)} %get-tuple-element.71), channel_id=1, source_target_pairs={{0,96},{32,0},{64,32},{96,64},{1,97},{33,1},{65,33},{97,65},{2,98}... | collective-permute-start | bytes 2801672 | tf_op jit(solution)/shard_map/ppermute | solution.py:467
  98.6 18.6 %all-to-all-start.2 = ((bf16[32,16,640]{2,1,0:T(8,128)(2,1)}), bf16[32,16,640]{2,1,0:T(8,128)(2,1)S(1)}, u32[]{:S(2)}, u32[]{:S(2)}) async-start(bf16[32,16,640]{2,1,0:T(8,128)(2,1)} %bitcast.24), calls=%async_computation.2 | async-start | bytes 1310720 | tf_op jit(solution)/shard_map/all_to_all | solution.py:459
  118.9 0.7 copy-start
  119.6 19.0 %all-to-all-start.3 = ((f32[4,16,640]{2,1,0:T(8,128)}), f32[4,16,640]{2,1,0:T(8,128)S(1)}, u32[]{:S(2)}, u32[]{:S(2)}) async-start(f32[4,16,640]{2,1,0:T(8,128)} %copy-done), calls=%async_computation.3 | async-start | bytes 327680 | tf_op jit(solution)/shard_map/all_to_all | solution.py:463

commit v6 on v5

--- a/solution.py
+++ b/solution.py
@@ -496,13 +496,13 @@
     latent[0], turned = tie(latent[0], turned)
     pieces = [along(x, d) for d, x in zip((1, 2, 3), split(table, turned))]
     handed = hand(table, turned, pieces)
+    handed = lax.ppermute(handed, "seq", [(j, j ^ 1) for j in range(32)])
 
     stripes, latent[1], handed, *pieces = tie(over_seq(latent[0]), latent[1], handed, *pieces)
 
     one, two, three, cache = pack(starts[0], table, stripes, None)
     following, one, two, three = tie(latent[1], one, two, three)
     one, two, three = along(one, 1), along(two, 2), along(three, 3)
-    handed = lax.ppermute(handed, "seq", [(j, j ^ 1) for j in range(32)])
     partial = attend(table, turned, pieces, handed, latent)
     stripes, partial, *first = tie(over_seq(following), partial, one, two, three)
 

time: 140 us -> 140 us (level)
    all_to_all x3, waiting for transfers between devices: 21.4 us -> 18.4 us  [over_seq(): return lax.all_to_all(x, 'seq', split_axis=0, concat_axis=0, tiled=True)]
    ppermute x9, waiting for transfers between devices: 39.3 us -> 42 us  [along(): return lax.ppermute(x, 'grp', [(i, (i + d) % 4) for i in range(4)])]
  transfers between devices with their start and end apart: 14 -> 14, of which waited for: 8 -> 8; matrix products, arithmetic and copies ran while one was open for 2% -> 2% of each run, Pallas kernels for 20% -> 19%
where the time goes in v6:
time: 140 us
  waiting for transfers between devices  60.4 us (43%)
  starting transfers between devices  38.2 us (27%)
  Pallas kernels  36.3 us (26%)
  local copies, waits for them, and re-layouts  2.16 us (2%)
  matrix products  1.66 us (1%)
    ppermute x9, waiting for transfers between devices, along(): return lax.ppermute(x, 'grp', [(i, (i + d) % 4) for i in range(4)])  42 us
    all_to_all x3, starting transfers between devices, over_seq(): return lax.all_to_all(x, 'seq', split_axis=0, concat_axis=0, tiled=True)  20.9 us
    all_to_all x3, waiting for transfers between devices, over_seq(): return lax.all_to_all(x, 'seq', split_axis=0, concat_axis=0, tiled=True)  18.4 us
    ppermute x9, starting transfers between devices, along(): return lax.ppermute(x, 'grp', [(i, (i + d) % 4) for i in range(4)])  12.8 us
    pallas_call x1, Pallas kernels, attend(): pl.pallas_call(functools.partial(attend_kernel, steps), grid=(steps,), ou...  10.4 us
    pallas_call x2, Pallas kernels, dequantize(): pl.pallas_call(functools.partial(dequantize_kernel, start, per_step, step...  8.76 us
    pallas_call x3, Pallas kernels, put(): pl.pallas_call(functools.partial(put_later_kernel if later else put_kerne...  6.58 us
    pallas_call x2, Pallas kernels, pack(): pl.pallas_call(functools.partial(pack_kernel, start), out_shape=(one, one...  4.7 us
  transfers between devices with their start and end apart: 14, of which 8 were waited for; matrix products, arithmetic and copies ran while one was open for 2% of the time, Pallas kernels for 19%

profile of v6, /device:TPU:1, one launch (start us, length us, event | category | flops | bytes accessed | tf_op | source)
XLA Modules:
  0.0 139.6 jit_solution(11194515076991625983)
XLA Ops:
  0.6 4.3 %dequantize.2.refs_5_ = bf16[32,272,128]{2,1,0:T(8,128)(2,1)} custom-call(s32[4,4]{1,0:T(4,128)} %lengths.3, s32[4,4]{1,0:T(4,128)} %padding.3, bf16[576,4096]{1,0:T(8,128)(2,1)} %bitcast.19, f32[32,576]{1,0:T(8,128)} %scale.3, s32[16,32]{1,0:T(8,128)} %bitcast.25, bf16[32,16,128]{2,1,0:T(8,128)(2,1)} %values.3), custom_call_target="tpu_custom_call" | custom-call | bytes 4456448 | tf_op jit(solution)/shard_map/dequantize/pallas_call | solution.py:104
  4.9 9.6 %all-to-all-start = ((bf16[32,272,128]{2,1,0:T(8,128)(2,1)}), bf16[32,272,128]{2,1,0:T(8,128)(2,1)S(1)}, u32[]{:S(2)}, u32[]{:S(2)}) async-start(bf16[32,272,128]{2,1,0:T(8,128)(2,1)} %dequantize.2.refs_5_), calls=%async_computation | async-start | bytes 4456448 | tf_op jit(solution)/shard_map/all_to_all | solution.py:459
  16.0 2.5 %split.1 = (bf16[288,512]{1,0:T(8,128)(2,1)}, bf16[288,512]{1,0:T(8,128)(2,1)}, bf16[288,512]{1,0:T(8,128)(2,1)}) custom-call(s32[14]{0:T(128)S(1)} %concatenate.3.table, bf16[4,576,512]{2,1,0:T(8,128)(2,1)} %bitcast.21), custom_call_target="tpu_custom_call" | custom-call | bytes 1048576 | tf_op jit(solution)/shard_map/split/pallas_call | solution.py:254
  19.8 2.5 %collective-permute-start.1 = (bf16[288,512]{1,0:T(8,128)(2,1)}, bf16[288,512]{1,0:T(8,128)(2,1)S(1)}, u32[]{:S(2)}, u32[]{:S(2)}) collective-permute-start(bf16[288,512]{1,0:T(8,128)(2,1)} %get-tuple-element.42), channel_id=1, source_target_pairs={{0,64},{32,96},{64,0},{96,32},{1,65},{33,97},{65,1},{97,33},{2,66}... | collective-permute-start | bytes 884744 | tf_op jit(solution)/shard_map/ppermute | solution.py:467
  23.4 5.0 %collective-permute-done.in1.refs_1_ = bf16[288,512]{1,0:T(8,128)(2,1)S(1)} collective-permute-done((bf16[288,512]{1,0:T(8,128)(2,1)}, bf16[288,512]{1,0:T(8,128)(2,1)S(1)}, u32[]{:S(2)}, u32[]{:S(2)}) %collective-permute-start) | collective-permute-done | bytes 294944 | tf_op jit(solution)/shard_map/ppermute | solution.py:467
  28.4 7.3 %collective-permute-done.1.in2.refs_2_ = bf16[288,512]{1,0:T(8,128)(2,1)S(1)} collective-permute-done((bf16[288,512]{1,0:T(8,128)(2,1)}, bf16[288,512]{1,0:T(8,128)(2,1)S(1)}, u32[]{:S(2)}, u32[]{:S(2)}) %collective-permute-start.1) | collective-permute-done | bytes 294944 | tf_op jit(solution)/shard_map/ppermute | solution.py:467
  37.5 4.5 %dequantize.3.refs_6_ = bf16[32,304,128]{2,1,0:T(8,128)(2,1)} custom-call(s32[4,4]{1,0:T(4,128)} %lengths.3, s32[4,4]{1,0:T(4,128)} %padding.3, bf16[576,4096]{1,0:T(8,128)(2,1)} %bitcast.20, f32[32,576]{1,0:T(8,128)} %scale.3, s32[16,32]{1,0:T(8,128)} %bitcast.26, bf16[32,16,128]{2,1,0:T(8,128)(2,1)} %values.3), custom_call_target="tpu_custom_call" | custom-call | bytes 4980736 | tf_op jit(solution)/shard_map/dequantize/pallas_call | solution.py:104
  41.9 2.3 %all-to-all-done.stripes = bf16[32,272,128]{2,1,0:T(8,128)(2,1)S(1)} async-done(((bf16[32,272,128]{2,1,0:T(8,128)(2,1)}), bf16[32,272,128]{2,1,0:T(8,128)(2,1)S(1)}, u32[]{:S(2)}, u32[]{:S(2)}) %all-to-all-start) | async-done | bytes 2228256 | tf_op jit(solution)/shard_map/all_to_all | solution.py:459
  44.2 2.3 %pack.2 = (bf16[12,272,128]{2,1,0:T(8,128)(2,1)}, bf16[12,272,128]{2,1,0:T(8,128)(2,1)}, bf16[12,272,128]{2,1,0:T(8,128)(2,1)}, bf16[4,12,576,128]{3,2,1,0:T(8,128)(2,1)}) custom-call(s32[14]{0:T(128)S(1)} %concatenate.3.table, bf16[32,272,128]{2,1,0:T(8,128)(2,1)S(1)} %all-to-all-done.stripes), custom_call_target="tpu_custom_call" | custom-call | bytes 6684672 | tf_op jit(solution)/shard_map/pack/pallas_call | solution.py:154
  47.8 2.5 %collective-permute-start.5 = (bf16[12,272,128]{2,1,0:T(8,128)(2,1)}, bf16[12,272,128]{2,1,0:T(8,128)(2,1)}, u32[]{:S(2)}, u32[]{:S(2)}) collective-permute-start(bf16[12,272,128]{2,1,0:T(8,128)(2,1)} %get-tuple-element.55), channel_id=1, source_target_pairs={{0,64},{32,96},{64,0},{96,32},{1,65},{33,97},{65,1},{97,33},{2,66}... | collective-permute-start | bytes 2506760 | tf_op jit(solution)/shard_map/ppermute | solution.py:467
  51.4 5.5 %all-to-all-start.1 = ((bf16[32,304,128]{2,1,0:T(8,128)(2,1)}), bf16[32,304,128]{2,1,0:T(8,128)(2,1)S(1)}, u32[]{:S(2)}, u32[]{:S(2)}) async-start(bf16[32,304,128]{2,1,0:T(8,128)(2,1)} %dequantize.3.refs_6_), calls=%async_computation.1 | async-start | bytes 4980736 | tf_op jit(solution)/shard_map/all_to_all | solution.py:459
  56.9 10.4 %attend.1 = bf16[512,640]{1,0:T(8,128)(2,1)} custom-call(s32[14]{0:T(128)S(1)} %concatenate.3.table, bf16[4,576,512]{2,1,0:T(8,128)(2,1)} %bitcast.23, bf16[288,512]{1,0:T(8,128)(2,1)S(1)} %collective-permute-done.in1.refs_1_, bf16[288,512]{1,0:T(8,128)(2,1)S(1)} %collective-permute-done.1.in2.refs_2_, ...), custom_call_target="tpu_custom_call" | custom-call | flops 42949672960 | tf_op jit(solution)/shard_map/attend/pallas_call | solution.py:368
  67.3 18.9 %collective-permute-done.5.refs_1_ = bf16[12,272,128]{2,1,0:T(8,128)(2,1)} collective-permute-done((bf16[12,272,128]{2,1,0:T(8,128)(2,1)}, bf16[12,272,128]{2,1,0:T(8,128)(2,1)}, u32[]{:S(2)}, u32[]{:S(2)}) %collective-permute-start.5) | collective-permute-done | bytes 835616 | tf_op jit(solution)/shard_map/ppermute | solution.py:467
  86.2 3.2 %all-to-all-done.1.stripes = bf16[32,304,128]{2,1,0:T(8,128)(2,1)S(1)} async-done(((bf16[32,304,128]{2,1,0:T(8,128)(2,1)}), bf16[32,304,128]{2,1,0:T(8,128)(2,1)S(1)}, u32[]{:S(2)}, u32[]{:S(2)}) %all-to-all-start.1) | async-done | bytes 2490400 | tf_op jit(solution)/shard_map/all_to_all | solution.py:459
  89.5 2.4 %pack.3 = (bf16[12,304,128]{2,1,0:T(8,128)(2,1)}, bf16[12,304,128]{2,1,0:T(8,128)(2,1)}, bf16[12,304,128]{2,1,0:T(8,128)(2,1)}, bf16[4,12,576,128]{3,2,1,0:T(8,128)(2,1)}) custom-call(s32[14]{0:T(128)S(1)} %concatenate.3.table, bf16[32,304,128]{2,1,0:T(8,128)(2,1)S(1)} %all-to-all-done.1.stripes, ...), custom_call_target="tpu_custom_call", output_to_operand_aliasing={{3}: (2, {})} | custom-call | bytes 7471104 | tf_op jit(solution)/shard_map/pack/pallas_call | solution.py:154
  92.8 2.2 %collective-permute-start.8 = (bf16[12,304,128]{2,1,0:T(8,128)(2,1)}, bf16[12,304,128]{2,1,0:T(8,128)(2,1)S(1)}, u32[]{:S(2)}, u32[]{:S(2)}) collective-permute-start(bf16[12,304,128]{2,1,0:T(8,128)(2,1)} %get-tuple-element.71), channel_id=1, source_target_pairs={{0,96},{32,0},{64,32},{96,64},{1,97},{33,1},{65,33},{97,65},{2,98}... | collective-permute-start | bytes 2801672 | tf_op jit(solution)/shard_map/ppermute | solution.py:467
  95.0 3.2 %put.3.refs_1_ = bf16[4,12,576,128]{3,2,1,0:T(8,128)(2,1)} custom-call(s32[14]{0:T(128)S(1)} %concatenate.3.table, bf16[12,272,128]{2,1,0:T(8,128)(2,1)} %collective-permute-done.4.refs_0_, bf16[12,272,128]{2,1,0:T(8,128)(2,1)} %collective-permute-done.5.refs_1_, ...), custom_call_target="tpu_custom_call", output_to_operand_aliasing={{}: (4, {})} | custom-call | flops 42949672960 | tf_op jit(solution)/shard_map/put/pallas_call | solution.py:214
  98.2 5.8 %all-to-all-start.2 = ((bf16[32,16,640]{2,1,0:T(8,128)(2,1)}), bf16[32,16,640]{2,1,0:T(8,128)(2,1)S(1)}, u32[]{:S(2)}, u32[]{:S(2)}) async-start(bf16[32,16,640]{2,1,0:T(8,128)(2,1)} %bitcast.24), calls=%async_computation.2 | async-start | bytes 1310720 | tf_op jit(solution)/shard_map/all_to_all | solution.py:459
  104.2 12.8 %all-to-all-done.2.partials = bf16[32,16,640]{2,1,0:T(8,128)(2,1)S(1)} async-done(((bf16[32,16,640]{2,1,0:T(8,128)(2,1)}), bf16[32,16,640]{2,1,0:T(8,128)(2,1)S(1)}, u32[]{:S(2)}, u32[]{:S(2)}) %all-to-all-start.2) | async-done | bytes 655392 | tf_op jit(solution)/shard_map/all_to_all | solution.py:459
  117.0 1.7 %join.1 = f32[4,16,640]{2,1,0:T(8,128)S(1)} custom-call(s32[14]{0:T(128)S(1)} %concatenate.3.table, bf16[32,16,640]{2,1,0:T(8,128)(2,1)S(1)} %all-to-all-done.2.partials), custom_call_target="tpu_custom_call" | custom-call | bytes 1048576 | tf_op jit(solution)/shard_map/join/pallas_call | solution.py:408
  119.4 3.3 %all-to-all-start.3 = ((f32[4,16,640]{2,1,0:T(8,128)}), f32[4,16,640]{2,1,0:T(8,128)S(1)}, u32[]{:S(2)}, u32[]{:S(2)}) async-start(f32[4,16,640]{2,1,0:T(8,128)} %copy-done), calls=%async_computation.3 | async-start | bytes 327680 | tf_op jit(solution)/shard_map/all_to_all | solution.py:463
  122.8 1.7 %fusion.scores = f32[4,16,4]{2,1,0:T(8,128)S(1)} fusion(bf16[4,4,576]{2,1,0:T(4,128)(2,1)S(1)} %copy-done.1, bf16[4,512,576]{1,2,0:T(8,128)(2,1)} %param.16, s32[]{:T(128)S(6)} %select_n.24, pred[16,4]{1,0:T(8,128)(4,1)S(1)} %iota_compare_fusion), kind=kOutput, calls=%fused_computation.1 | convolution fusion | flops 295424 | bytes 609348 | tf_op jit(solution)/shard_map/yeu,ynu->yen/dot_general | solution.py:438
  126.0 10.8 %collective-permute-done.7.refs_0_ = bf16[12,304,128]{2,1,0:T(8,128)(2,1)S(1)} collective-permute-done((bf16[12,304,128]{2,1,0:T(8,128)(2,1)}, bf16[12,304,128]{2,1,0:T(8,128)(2,1)S(1)}, u32[]{:S(2)}, u32[]{:S(2)}) %collective-permute-start.7) | collective-permute-done | bytes 933920 | tf_op jit(solution)/shard_map/ppermute | solution.py:467
  136.8 1.8 %put.5 = bf16[4,12,576,128]{3,2,1,0:T(8,128)(2,1)} custom-call(s32[14]{0:T(128)S(1)} %concatenate.3.table, bf16[12,304,128]{2,1,0:T(8,128)(2,1)S(1)} %collective-permute-done.7.refs_0_, bf16[12,304,128]{2,1,0:T(8,128)(2,1)S(1)} %collective-permute-done.8.refs_1_, bf16[4,12,576,128]{3,2,1,0:T(8,128)(2,1)} %put.4.refs_2_), custom_call_target="tpu_custom_call", output_to_operand_aliasing={{}: (3, {})} | custom-call | bytes 3735552 | tf_op jit(solution)/shard_map/put/pallas_call | solution.py:214
  (26 shorter events, 12.4 us)
Async XLA Ops:
  4.9 39.3 %all-to-all-start = ((bf16[32,272,128]{2,1,0:T(8,128)(2,1)}), bf16[32,272,128]{2,1,0:T(8,128)(2,1)S(1)}, u32[]{:S(2)}, u32[]{:S(2)}) async-start(bf16[32,272,128]{2,1,0:T(8,128)(2,1)} %dequantize.2.refs_5_), calls=%async_computation | async-start | bytes 4456448 | tf_op jit(solution)/shard_map/all_to_all | solution.py:459
  18.5 9.9 %collective-permute-start = (bf16[288,512]{1,0:T(8,128)(2,1)}, bf16[288,512]{1,0:T(8,128)(2,1)S(1)}, u32[]{:S(2)}, u32[]{:S(2)}) collective-permute-start(bf16[288,512]{1,0:T(8,128)(2,1)} %get-tuple-element.41), channel_id=1, source_target_pairs={{0,32},{32,64},{64,96},{96,0},{1,33},{33,65},{65,97},{97,1},{2,34}... | collective-permute-start | bytes 884744 | tf_op jit(solution)/shard_map/ppermute | solution.py:467
  19.8 15.9 %collective-permute-start.1 = (bf16[288,512]{1,0:T(8,128)(2,1)}, bf16[288,512]{1,0:T(8,128)(2,1)S(1)}, u32[]{:S(2)}, u32[]{:S(2)}) collective-permute-start(bf16[288,512]{1,0:T(8,128)(2,1)} %get-tuple-element.42), channel_id=1, source_target_pairs={{0,64},{32,96},{64,0},{96,32},{1,65},{33,97},{65,1},{97,33},{2,66}... | collective-permute-start | bytes 884744 | tf_op jit(solution)/shard_map/ppermute | solution.py:467
  22.2 13.4 %collective-permute-start.2 = (bf16[288,512]{1,0:T(8,128)(2,1)}, bf16[288,512]{1,0:T(8,128)(2,1)S(1)}, u32[]{:S(2)}, u32[]{:S(2)}) collective-permute-start(bf16[288,512]{1,0:T(8,128)(2,1)} %get-tuple-element.43), channel_id=1, source_target_pairs={{0,96},{32,0},{64,32},{96,64},{1,97},{33,1},{65,33},{97,65},{2,98}... | collective-permute-start | bytes 884744 | tf_op jit(solution)/shard_map/ppermute | solution.py:467
  36.3 5.6 %collective-permute-start.3 = (bf16[288,512]{1,0:T(8,128)(2,1)S(1)}, bf16[288,512]{1,0:T(8,128)(2,1)}, u32[]{:S(2)}, u32[]{:S(2)}) collective-permute-start(bf16[288,512]{1,0:T(8,128)(2,1)S(1)} %hand.1), channel_id=1, source_target_pairs={{0,1},{1,0},{2,3},{3,2},{4,5},{5,4},{6,7},{7,6},{8,9},{9,8},{10,11... | collective-permute-start | bytes 884744 | tf_op jit(solution)/shard_map/ppermute | solution.py:499
  46.5 20.8 %collective-permute-start.4 = (bf16[12,272,128]{2,1,0:T(8,128)(2,1)}, bf16[12,272,128]{2,1,0:T(8,128)(2,1)}, u32[]{:S(2)}, u32[]{:S(2)}) collective-permute-start(bf16[12,272,128]{2,1,0:T(8,128)(2,1)} %get-tuple-element.54), channel_id=1, source_target_pairs={{0,32},{32,64},{64,96},{96,0},{1,33},{33,65},{65,97},{97,1},{2,34}... | collective-permute-start | bytes 2506760 | tf_op jit(solution)/shard_map/ppermute | solution.py:467
  47.8 38.4 %collective-permute-start.5 = (bf16[12,272,128]{2,1,0:T(8,128)(2,1)}, bf16[12,272,128]{2,1,0:T(8,128)(2,1)}, u32[]{:S(2)}, u32[]{:S(2)}) collective-permute-start(bf16[12,272,128]{2,1,0:T(8,128)(2,1)} %get-tuple-element.55), channel_id=1, source_target_pairs={{0,64},{32,96},{64,0},{96,32},{1,65},{33,97},{65,1},{97,33},{2,66}... | collective-permute-start | bytes 2506760 | tf_op jit(solution)/shard_map/ppermute | solution.py:467
  50.3 36.0 %collective-permute-start.6 = (bf16[12,272,128]{2,1,0:T(8,128)(2,1)}, bf16[12,272,128]{2,1,0:T(8,128)(2,1)}, u32[]{:S(2)}, u32[]{:S(2)}) collective-permute-start(bf16[12,272,128]{2,1,0:T(8,128)(2,1)} %get-tuple-element.56), channel_id=1, source_target_pairs={{0,96},{32,0},{64,32},{96,64},{1,97},{33,1},{65,33},{97,65},{2,98}... | collective-permute-start | bytes 2506760 | tf_op jit(solution)/shard_map/ppermute | solution.py:467
  51.4 38.0 %all-to-all-start.1 = ((bf16[32,304,128]{2,1,0:T(8,128)(2,1)}), bf16[32,304,128]{2,1,0:T(8,128)(2,1)S(1)}, u32[]{:S(2)}, u32[]{:S(2)}) async-start(bf16[32,304,128]{2,1,0:T(8,128)(2,1)} %dequantize.3.refs_6_), calls=%async_computation.1 | async-start | bytes 4980736 | tf_op jit(solution)/shard_map/all_to_all | solution.py:459
  91.9 30.9 %copy-start.1 = (bf16[4,4,576]{2,1,0:T(4,128)(2,1)S(1)}, bf16[4,4,576]{2,1,0:T(4,128)(2,1)}, u32[]{:S(2)}) copy-start(bf16[4,4,576]{2,1,0:T(4,128)(2,1)} %fresh.1) | copy-start | bytes 55300
  91.9 32.6 %collective-permute-start.9 = (bf16[12,304,128]{2,1,0:T(8,128)(2,1)}, bf16[12,304,128]{2,1,0:T(8,128)(2,1)S(1)}, u32[]{:S(2)}, u32[]{:S(2)}) collective-permute-start(bf16[12,304,128]{2,1,0:T(8,128)(2,1)} %get-tuple-element.72), channel_id=1, source_target_pairs={{0,64},{32,96},{64,0},{96,32},{1,65},{33,97},{65,1},{97,33},{2,66}... | collective-permute-start | bytes 2801672 | tf_op jit(solution)/shard_map/ppermute | solution.py:467
  92.3 44.5 %collective-permute-start.7 = (bf16[12,304,128]{2,1,0:T(8,128)(2,1)}, bf16[12,304,128]{2,1,0:T(8,128)(2,1)S(1)}, u32[]{:S(2)}, u32[]{:S(2)}) collective-permute-start(bf16[12,304,128]{2,1,0:T(8,128)(2,1)} %get-tuple-element.70), channel_id=1, source_target_pairs={{0,32},{32,64},{64,96},{96,0},{1,33},{33,65},{65,97},{97,1},{2,34}... | collective-permute-start | bytes 2801672 | tf_op jit(solution)/shard_map/ppermute | solution.py:467
  92.8 44.0 %collective-permute-start.8 = (bf16[12,304,128]{2,1,0:T(8,128)(2,1)}, bf16[12,304,128]{2,1,0:T(8,128)(2,1)S(1)}, u32[]{:S(2)}, u32[]{:S(2)}) collective-permute-start(bf16[12,304,128]{2,1,0:T(8,128)(2,1)} %get-tuple-element.71), channel_id=1, source_target_pairs={{0,96},{32,0},{64,32},{96,64},{1,97},{33,1},{65,33},{97,65},{2,98}... | collective-permute-start | bytes 2801672 | tf_op jit(solution)/shard_map/ppermute | solution.py:467
  98.2 18.8 %all-to-all-start.2 = ((bf16[32,16,640]{2,1,0:T(8,128)(2,1)}), bf16[32,16,640]{2,1,0:T(8,128)(2,1)S(1)}, u32[]{:S(2)}, u32[]{:S(2)}) async-start(bf16[32,16,640]{2,1,0:T(8,128)(2,1)} %bitcast.24), calls=%async_computation.2 | async-start | bytes 1310720 | tf_op jit(solution)/shard_map/all_to_all | solution.py:459
  118.7 0.7 copy-start
  119.4 19.2 %all-to-all-start.3 = ((f32[4,16,640]{2,1,0:T(8,128)}), f32[4,16,640]{2,1,0:T(8,128)S(1)}, u32[]{:S(2)}, u32[]{:S(2)}) async-start(f32[4,16,640]{2,1,0:T(8,128)} %copy-done), calls=%async_computation.3 | async-start | bytes 327680 | tf_op jit(solution)/shard_map/all_to_all | solution.py:463

commit v7 on v6

--- a/solution.py
+++ b/solution.py
@@ -12,7 +12,7 @@
 HEADS = 128
 NEG_FILL = -1e30
 SCORE_SCALE = 192.0 ** (-0.5)
-CHUNKS = (272, 304)
+CHUNKS = (288, 288)
 KEY_TILE = 16
 KEY_PART = 4
 NOTE_LANES = 128

time: 140 us -> 139 us (level)
  waiting for transfers between devices: 60.4 us -> 54 us
  Pallas kernels: 36.3 us -> 39.2 us
  starting transfers between devices: 38.2 us -> 40.6 us
    ppermute x9, waiting for transfers between devices: 42 us -> 38.1 us  [along(): return lax.ppermute(x, 'grp', [(i, (i + d) % 4) for i in range(4)])]
    all_to_all x3, waiting for transfers between devices: 18.4 us -> 15.9 us  [over_seq(): return lax.all_to_all(x, 'seq', split_axis=0, concat_axis=0, tiled=True)]
    ppermute x9, starting transfers between devices: 12.8 us -> 14.7 us  [along(): return lax.ppermute(x, 'grp', [(i, (i + d) % 4) for i in range(4)])]
  transfers between devices with their start and end apart: 14 -> 14, of which waited for: 8 -> 6; matrix products, arithmetic and copies ran while one was open for 2% -> 2% of each run, Pallas kernels for 19% -> 21%
where the time goes in v7:
time: 139 us; the launch traced here: 138 us
  waiting for transfers between devices  54 us (39%)
  starting transfers between devices  40.6 us (29%)
  Pallas kernels  39.2 us (28%)
  matrix products  1.66 us (1%)
  local copies, waits for them, and re-layouts  1.48 us (1%)
    ppermute x9, waiting for transfers between devices, along(): return lax.ppermute(x, 'grp', [(i, (i + d) % 4) for i in range(4)])  38.1 us
    all_to_all x3, starting transfers between devices, over_seq(): return lax.all_to_all(x, 'seq', split_axis=0, concat_axis=0, tiled=True)  21.5 us
    all_to_all x3, waiting for transfers between devices, over_seq(): return lax.all_to_all(x, 'seq', split_axis=0, concat_axis=0, tiled=True)  15.9 us
    ppermute x9, starting transfers between devices, along(): return lax.ppermute(x, 'grp', [(i, (i + d) % 4) for i in range(4)])  14.7 us
    pallas_call x1, Pallas kernels, attend(): pl.pallas_call(functools.partial(attend_kernel, steps), grid=(steps,), ou...  11.7 us
    pallas_call x2, Pallas kernels, dequantize(): pl.pallas_call(functools.partial(dequantize_kernel, start, per_step, step...  8.83 us
    pallas_call x3, Pallas kernels, put(): pl.pallas_call(functools.partial(put_later_kernel if later else put_kerne...  6.6 us
    pallas_call x2, Pallas kernels, pack(): pl.pallas_call(functools.partial(pack_kernel, start), out_shape=(one, one...  4.73 us
  transfers between devices with their start and end apart: 14, of which 6 were waited for; matrix products, arithmetic and copies ran while one was open for 2% of the time, Pallas kernels for 21%

profile of v7, /device:TPU:1, one launch (start us, length us, event | category | flops | bytes accessed | tf_op | source)
XLA Modules:
  0.0 137.9 jit_solution(13111396033851695799)
XLA Ops:
  0.6 4.4 %dequantize.2.refs_5_ = bf16[32,288,128]{2,1,0:T(8,128)(2,1)} custom-call(s32[4,4]{1,0:T(4,128)} %lengths.3, s32[4,4]{1,0:T(4,128)} %padding.3, bf16[576,4096]{1,0:T(8,128)(2,1)} %bitcast.19, f32[32,576]{1,0:T(8,128)} %scale.3, s32[16,32]{1,0:T(8,128)} %bitcast.25, bf16[32,16,128]{2,1,0:T(8,128)(2,1)} %values.3), custom_call_target="tpu_custom_call" | custom-call | bytes 4718592 | tf_op jit(solution)/shard_map/dequantize/pallas_call | solution.py:104
  5.1 9.6 %all-to-all-start = ((bf16[32,288,128]{2,1,0:T(8,128)(2,1)}), bf16[32,288,128]{2,1,0:T(8,128)(2,1)S(1)}, u32[]{:S(2)}, u32[]{:S(2)}) async-start(bf16[32,288,128]{2,1,0:T(8,128)(2,1)} %dequantize.2.refs_5_), calls=%async_computation | async-start | bytes 4718592 | tf_op jit(solution)/shard_map/all_to_all | solution.py:459
  16.2 2.5 %split.1 = (bf16[288,512]{1,0:T(8,128)(2,1)}, bf16[288,512]{1,0:T(8,128)(2,1)}, bf16[288,512]{1,0:T(8,128)(2,1)}) custom-call(s32[14]{0:T(128)S(1)} %concatenate.3.table, bf16[4,576,512]{2,1,0:T(8,128)(2,1)} %bitcast.21), custom_call_target="tpu_custom_call" | custom-call | bytes 1048576 | tf_op jit(solution)/shard_map/split/pallas_call | solution.py:254
  19.9 2.4 %collective-permute-start.1 = (bf16[288,512]{1,0:T(8,128)(2,1)}, bf16[288,512]{1,0:T(8,128)(2,1)S(1)}, u32[]{:S(2)}, u32[]{:S(2)}) collective-permute-start(bf16[288,512]{1,0:T(8,128)(2,1)} %get-tuple-element.42), channel_id=1, source_target_pairs={{0,64},{32,96},{64,0},{96,32},{1,65},{33,97},{65,1},{97,33},{2,66}... | collective-permute-start | bytes 884744 | tf_op jit(solution)/shard_map/ppermute | solution.py:467
  23.5 5.0 %collective-permute-done.in1.refs_1_ = bf16[288,512]{1,0:T(8,128)(2,1)S(1)} collective-permute-done((bf16[288,512]{1,0:T(8,128)(2,1)}, bf16[288,512]{1,0:T(8,128)(2,1)S(1)}, u32[]{:S(2)}, u32[]{:S(2)}) %collective-permute-start) | collective-permute-done | bytes 294944 | tf_op jit(solution)/shard_map/ppermute | solution.py:467
  28.5 7.3 %collective-permute-done.1.in2.refs_2_ = bf16[288,512]{1,0:T(8,128)(2,1)S(1)} collective-permute-done((bf16[288,512]{1,0:T(8,128)(2,1)}, bf16[288,512]{1,0:T(8,128)(2,1)S(1)}, u32[]{:S(2)}, u32[]{:S(2)}) %collective-permute-start.1) | collective-permute-done | bytes 294944 | tf_op jit(solution)/shard_map/ppermute | solution.py:467
  38.5 4.4 %dequantize.3.refs_6_ = bf16[32,288,128]{2,1,0:T(8,128)(2,1)} custom-call(s32[4,4]{1,0:T(4,128)} %lengths.3, s32[4,4]{1,0:T(4,128)} %padding.3, bf16[576,4096]{1,0:T(8,128)(2,1)} %bitcast.20, f32[32,576]{1,0:T(8,128)} %scale.3, s32[16,32]{1,0:T(8,128)} %bitcast.26, bf16[32,16,128]{2,1,0:T(8,128)(2,1)} %values.3), custom_call_target="tpu_custom_call" | custom-call | bytes 4718592 | tf_op jit(solution)/shard_map/dequantize/pallas_call | solution.py:104
  42.9 2.9 %all-to-all-done.stripes = bf16[32,288,128]{2,1,0:T(8,128)(2,1)S(1)} async-done(((bf16[32,288,128]{2,1,0:T(8,128)(2,1)}), bf16[32,288,128]{2,1,0:T(8,128)(2,1)S(1)}, u32[]{:S(2)}, u32[]{:S(2)}) %all-to-all-start) | async-done | bytes 2359328 | tf_op jit(solution)/shard_map/all_to_all | solution.py:459
  45.8 2.4 %pack.2 = (bf16[12,288,128]{2,1,0:T(8,128)(2,1)}, bf16[12,288,128]{2,1,0:T(8,128)(2,1)}, bf16[12,288,128]{2,1,0:T(8,128)(2,1)}, bf16[4,12,576,128]{3,2,1,0:T(8,128)(2,1)}) custom-call(s32[14]{0:T(128)S(1)} %concatenate.3.table, bf16[32,288,128]{2,1,0:T(8,128)(2,1)S(1)} %all-to-all-done.stripes), custom_call_target="tpu_custom_call" | custom-call | bytes 7077888 | tf_op jit(solution)/shard_map/pack/pallas_call | solution.py:154
  49.5 2.4 %collective-permute-start.5 = (bf16[12,288,128]{2,1,0:T(8,128)(2,1)}, bf16[12,288,128]{2,1,0:T(8,128)(2,1)}, u32[]{:S(2)}, u32[]{:S(2)}) collective-permute-start(bf16[12,288,128]{2,1,0:T(8,128)(2,1)} %get-tuple-element.55), channel_id=1, source_target_pairs={{0,64},{32,96},{64,0},{96,32},{1,65},{33,97},{65,1},{97,33},{2,66}... | collective-permute-start | bytes 2654216 | tf_op jit(solution)/shard_map/ppermute | solution.py:467
  53.1 5.5 %all-to-all-start.1 = ((bf16[32,288,128]{2,1,0:T(8,128)(2,1)}), bf16[32,288,128]{2,1,0:T(8,128)(2,1)S(1)}, u32[]{:S(2)}, u32[]{:S(2)}) async-start(bf16[32,288,128]{2,1,0:T(8,128)(2,1)} %dequantize.3.refs_6_), calls=%async_computation.1 | async-start | bytes 4718592 | tf_op jit(solution)/shard_map/all_to_all | solution.py:459
  58.5 11.7 %attend.1 = bf16[512,640]{1,0:T(8,128)(2,1)} custom-call(s32[14]{0:T(128)S(1)} %concatenate.3.table, bf16[4,576,512]{2,1,0:T(8,128)(2,1)} %bitcast.23, bf16[288,512]{1,0:T(8,128)(2,1)S(1)} %collective-permute-done.in1.refs_1_, bf16[288,512]{1,0:T(8,128)(2,1)S(1)} %collective-permute-done.1.in2.refs_2_, ...), custom_call_target="tpu_custom_call" | custom-call | flops 42949672960 | tf_op jit(solution)/shard_map/attend/pallas_call | solution.py:368
  70.2 19.8 %collective-permute-done.5.refs_1_ = bf16[12,288,128]{2,1,0:T(8,128)(2,1)} collective-permute-done((bf16[12,288,128]{2,1,0:T(8,128)(2,1)}, bf16[12,288,128]{2,1,0:T(8,128)(2,1)}, u32[]{:S(2)}, u32[]{:S(2)}) %collective-permute-start.5) | collective-permute-done | bytes 884768 | tf_op jit(solution)/shard_map/ppermute | solution.py:467
  90.0 2.4 %pack.3 = (bf16[12,288,128]{2,1,0:T(8,128)(2,1)}, bf16[12,288,128]{2,1,0:T(8,128)(2,1)}, bf16[12,288,128]{2,1,0:T(8,128)(2,1)}, bf16[4,12,576,128]{3,2,1,0:T(8,128)(2,1)}) custom-call(s32[14]{0:T(128)S(1)} %concatenate.3.table, bf16[32,288,128]{2,1,0:T(8,128)(2,1)S(1)} %all-to-all-done.1.stripes, ...), custom_call_target="tpu_custom_call", output_to_operand_aliasing={{3}: (2, {})} | custom-call | bytes 7077888 | tf_op jit(solution)/shard_map/pack/pallas_call | solution.py:154
  92.3 2.2 %collective-permute-start.9 = (bf16[12,288,128]{2,1,0:T(8,128)(2,1)}, bf16[12,288,128]{2,1,0:T(8,128)(2,1)S(1)}, u32[]{:S(2)}, u32[]{:S(2)}) collective-permute-start(bf16[12,288,128]{2,1,0:T(8,128)(2,1)} %get-tuple-element.72), channel_id=1, source_target_pairs={{0,64},{32,96},{64,0},{96,32},{1,65},{33,97},{65,1},{97,33},{2,66}... | collective-permute-start | bytes 2654216 | tf_op jit(solution)/shard_map/ppermute | solution.py:467
  94.6 1.7 %collective-permute-start.7 = (bf16[12,288,128]{2,1,0:T(8,128)(2,1)}, bf16[12,288,128]{2,1,0:T(8,128)(2,1)S(1)}, u32[]{:S(2)}, u32[]{:S(2)}) collective-permute-start(bf16[12,288,128]{2,1,0:T(8,128)(2,1)} %get-tuple-element.70), channel_id=1, source_target_pairs={{0,32},{32,64},{64,96},{96,0},{1,33},{33,65},{65,97},{97,1},{2,34}... | collective-permute-start | bytes 2654216 | tf_op jit(solution)/shard_map/ppermute | solution.py:467
  97.2 3.3 %put.3.refs_1_ = bf16[4,12,576,128]{3,2,1,0:T(8,128)(2,1)} custom-call(s32[14]{0:T(128)S(1)} %concatenate.3.table, bf16[12,288,128]{2,1,0:T(8,128)(2,1)} %collective-permute-done.4.refs_0_, bf16[12,288,128]{2,1,0:T(8,128)(2,1)} %collective-permute-done.5.refs_1_, ...), custom_call_target="tpu_custom_call", output_to_operand_aliasing={{}: (4, {})} | custom-call | flops 42949672960 | tf_op jit(solution)/shard_map/put/pallas_call | solution.py:214
  100.6 6.5 %all-to-all-start.2 = ((bf16[32,16,640]{2,1,0:T(8,128)(2,1)}), bf16[32,16,640]{2,1,0:T(8,128)(2,1)S(1)}, u32[]{:S(2)}, u32[]{:S(2)}) async-start(bf16[32,16,640]{2,1,0:T(8,128)(2,1)} %bitcast.24), calls=%async_computation.2 | async-start | bytes 1310720 | tf_op jit(solution)/shard_map/all_to_all | solution.py:459
  107.1 13.0 %all-to-all-done.2.partials = bf16[32,16,640]{2,1,0:T(8,128)(2,1)S(1)} async-done(((bf16[32,16,640]{2,1,0:T(8,128)(2,1)}), bf16[32,16,640]{2,1,0:T(8,128)(2,1)S(1)}, u32[]{:S(2)}, u32[]{:S(2)}) %all-to-all-start.2) | async-done | bytes 655392 | tf_op jit(solution)/shard_map/all_to_all | solution.py:459
  120.1 2.4 %join.1 = f32[4,16,640]{2,1,0:T(8,128)} custom-call(s32[14]{0:T(128)S(1)} %concatenate.3.table, bf16[32,16,640]{2,1,0:T(8,128)(2,1)S(1)} %all-to-all-done.2.partials), custom_call_target="tpu_custom_call" | custom-call | bytes 1048576 | tf_op jit(solution)/shard_map/join/pallas_call | solution.py:408
  122.5 3.3 %all-to-all-start.3 = ((f32[4,16,640]{2,1,0:T(8,128)}), f32[4,16,640]{2,1,0:T(8,128)S(1)}, u32[]{:S(2)}, u32[]{:S(2)}) async-start(f32[4,16,640]{2,1,0:T(8,128)} %join.1), calls=%async_computation.3 | async-start | bytes 327680 | tf_op jit(solution)/shard_map/all_to_all | solution.py:463
  125.8 1.7 %fusion.scores = f32[4,16,4]{2,1,0:T(8,128)S(1)} fusion(bf16[4,4,576]{2,1,0:T(4,128)(2,1)S(1)} %copy-done, bf16[4,512,576]{1,2,0:T(8,128)(2,1)} %param.16, s32[]{:T(128)S(6)} %select_n.24, pred[16,4]{1,0:T(8,128)(4,1)S(1)} %iota_compare_fusion), kind=kOutput, calls=%fused_computation.1 | convolution fusion | flops 295424 | bytes 609348 | tf_op jit(solution)/shard_map/yeu,ynu->yen/dot_general | solution.py:438
  129.0 6.1 %collective-permute-done.7.refs_0_ = bf16[12,288,128]{2,1,0:T(8,128)(2,1)S(1)} collective-permute-done((bf16[12,288,128]{2,1,0:T(8,128)(2,1)}, bf16[12,288,128]{2,1,0:T(8,128)(2,1)S(1)}, u32[]{:S(2)}, u32[]{:S(2)}) %collective-permute-start.7) | collective-permute-done | bytes 884768 | tf_op jit(solution)/shard_map/ppermute | solution.py:467
  135.1 1.8 %put.5 = bf16[4,12,576,128]{3,2,1,0:T(8,128)(2,1)} custom-call(s32[14]{0:T(128)S(1)} %concatenate.3.table, bf16[12,288,128]{2,1,0:T(8,128)(2,1)S(1)} %collective-permute-done.7.refs_0_, bf16[12,288,128]{2,1,0:T(8,128)(2,1)S(1)} %collective-permute-done.8.refs_1_, bf16[4,12,576,128]{3,2,1,0:T(8,128)(2,1)} %put.4.refs_2_), custom_call_target="tpu_custom_call", output_to_operand_aliasing={{}: (3, {})} | custom-call | bytes 3538944 | tf_op jit(solution)/shard_map/put/pallas_call | solution.py:214
  (24 shorter events, 12.5 us)
Async XLA Ops:
  5.1 40.7 %all-to-all-start = ((bf16[32,288,128]{2,1,0:T(8,128)(2,1)}), bf16[32,288,128]{2,1,0:T(8,128)(2,1)S(1)}, u32[]{:S(2)}, u32[]{:S(2)}) async-start(bf16[32,288,128]{2,1,0:T(8,128)(2,1)} %dequantize.2.refs_5_), calls=%async_computation | async-start | bytes 4718592 | tf_op jit(solution)/shard_map/all_to_all | solution.py:459
  18.6 9.9 %collective-permute-start = (bf16[288,512]{1,0:T(8,128)(2,1)}, bf16[288,512]{1,0:T(8,128)(2,1)S(1)}, u32[]{:S(2)}, u32[]{:S(2)}) collective-permute-start(bf16[288,512]{1,0:T(8,128)(2,1)} %get-tuple-element.41), channel_id=1, source_target_pairs={{0,32},{32,64},{64,96},{96,0},{1,33},{33,65},{65,97},{97,1},{2,34}... | collective-permute-start | bytes 884744 | tf_op jit(solution)/shard_map/ppermute | solution.py:467
  19.9 15.9 %collective-permute-start.1 = (bf16[288,512]{1,0:T(8,128)(2,1)}, bf16[288,512]{1,0:T(8,128)(2,1)S(1)}, u32[]{:S(2)}, u32[]{:S(2)}) collective-permute-start(bf16[288,512]{1,0:T(8,128)(2,1)} %get-tuple-element.42), channel_id=1, source_target_pairs={{0,64},{32,96},{64,0},{96,32},{1,65},{33,97},{65,1},{97,33},{2,66}... | collective-permute-start | bytes 884744 | tf_op jit(solution)/shard_map/ppermute | solution.py:467
  22.4 13.4 %collective-permute-start.2 = (bf16[288,512]{1,0:T(8,128)(2,1)}, bf16[288,512]{1,0:T(8,128)(2,1)S(1)}, u32[]{:S(2)}, u32[]{:S(2)}) collective-permute-start(bf16[288,512]{1,0:T(8,128)(2,1)} %get-tuple-element.43), channel_id=1, source_target_pairs={{0,96},{32,0},{64,32},{96,64},{1,97},{33,1},{65,33},{97,65},{2,98}... | collective-permute-start | bytes 884744 | tf_op jit(solution)/shard_map/ppermute | solution.py:467
  37.3 5.5 %collective-permute-start.3 = (bf16[288,512]{1,0:T(8,128)(2,1)S(1)}, bf16[288,512]{1,0:T(8,128)(2,1)}, u32[]{:S(2)}, u32[]{:S(2)}) collective-permute-start(bf16[288,512]{1,0:T(8,128)(2,1)S(1)} %hand.1), channel_id=1, source_target_pairs={{0,1},{1,0},{2,3},{3,2},{4,5},{5,4},{6,7},{7,6},{8,9},{9,8},{10,11... | collective-permute-start | bytes 884744 | tf_op jit(solution)/shard_map/ppermute | solution.py:499
  48.2 22.0 %collective-permute-start.4 = (bf16[12,288,128]{2,1,0:T(8,128)(2,1)}, bf16[12,288,128]{2,1,0:T(8,128)(2,1)}, u32[]{:S(2)}, u32[]{:S(2)}) collective-permute-start(bf16[12,288,128]{2,1,0:T(8,128)(2,1)} %get-tuple-element.54), channel_id=1, source_target_pairs={{0,32},{32,64},{64,96},{96,0},{1,33},{33,65},{65,97},{97,1},{2,34}... | collective-permute-start | bytes 2654216 | tf_op jit(solution)/shard_map/ppermute | solution.py:467
  49.5 40.5 %collective-permute-start.5 = (bf16[12,288,128]{2,1,0:T(8,128)(2,1)}, bf16[12,288,128]{2,1,0:T(8,128)(2,1)}, u32[]{:S(2)}, u32[]{:S(2)}) collective-permute-start(bf16[12,288,128]{2,1,0:T(8,128)(2,1)} %get-tuple-element.55), channel_id=1, source_target_pairs={{0,64},{32,96},{64,0},{96,32},{1,65},{33,97},{65,1},{97,33},{2,66}... | collective-permute-start | bytes 2654216 | tf_op jit(solution)/shard_map/ppermute | solution.py:467
  51.9 38.1 %collective-permute-start.6 = (bf16[12,288,128]{2,1,0:T(8,128)(2,1)}, bf16[12,288,128]{2,1,0:T(8,128)(2,1)}, u32[]{:S(2)}, u32[]{:S(2)}) collective-permute-start(bf16[12,288,128]{2,1,0:T(8,128)(2,1)} %get-tuple-element.56), channel_id=1, source_target_pairs={{0,96},{32,0},{64,32},{96,64},{1,97},{33,1},{65,33},{97,65},{2,98}... | collective-permute-start | bytes 2654216 | tf_op jit(solution)/shard_map/ppermute | solution.py:467
  53.1 36.9 %all-to-all-start.1 = ((bf16[32,288,128]{2,1,0:T(8,128)(2,1)}), bf16[32,288,128]{2,1,0:T(8,128)(2,1)S(1)}, u32[]{:S(2)}, u32[]{:S(2)}) async-start(bf16[32,288,128]{2,1,0:T(8,128)(2,1)} %dequantize.3.refs_6_), calls=%async_computation.1 | async-start | bytes 4718592 | tf_op jit(solution)/shard_map/all_to_all | solution.py:459
  92.3 35.2 %collective-permute-start.9 = (bf16[12,288,128]{2,1,0:T(8,128)(2,1)}, bf16[12,288,128]{2,1,0:T(8,128)(2,1)S(1)}, u32[]{:S(2)}, u32[]{:S(2)}) collective-permute-start(bf16[12,288,128]{2,1,0:T(8,128)(2,1)} %get-tuple-element.72), channel_id=1, source_target_pairs={{0,64},{32,96},{64,0},{96,32},{1,65},{33,97},{65,1},{97,33},{2,66}... | collective-permute-start | bytes 2654216 | tf_op jit(solution)/shard_map/ppermute | solution.py:467
  94.6 40.6 %collective-permute-start.7 = (bf16[12,288,128]{2,1,0:T(8,128)(2,1)}, bf16[12,288,128]{2,1,0:T(8,128)(2,1)S(1)}, u32[]{:S(2)}, u32[]{:S(2)}) collective-permute-start(bf16[12,288,128]{2,1,0:T(8,128)(2,1)} %get-tuple-element.70), channel_id=1, source_target_pairs={{0,32},{32,64},{64,96},{96,0},{1,33},{33,65},{65,97},{97,1},{2,34}... | collective-permute-start | bytes 2654216 | tf_op jit(solution)/shard_map/ppermute | solution.py:467
  96.3 38.8 %collective-permute-start.8 = (bf16[12,288,128]{2,1,0:T(8,128)(2,1)}, bf16[12,288,128]{2,1,0:T(8,128)(2,1)S(1)}, u32[]{:S(2)}, u32[]{:S(2)}) collective-permute-start(bf16[12,288,128]{2,1,0:T(8,128)(2,1)} %get-tuple-element.71), channel_id=1, source_target_pairs={{0,96},{32,0},{64,32},{96,64},{1,97},{33,1},{65,33},{97,65},{2,98}... | collective-permute-start | bytes 2654216 | tf_op jit(solution)/shard_map/ppermute | solution.py:467
  100.5 25.3 %copy-start = (bf16[4,4,576]{2,1,0:T(4,128)(2,1)S(1)}, bf16[4,4,576]{2,1,0:T(4,128)(2,1)}, u32[]{:S(2)}) copy-start(bf16[4,4,576]{2,1,0:T(4,128)(2,1)} %fresh.1) | copy-start | bytes 55300
  100.6 19.5 %all-to-all-start.2 = ((bf16[32,16,640]{2,1,0:T(8,128)(2,1)}), bf16[32,16,640]{2,1,0:T(8,128)(2,1)S(1)}, u32[]{:S(2)}, u32[]{:S(2)}) async-start(bf16[32,16,640]{2,1,0:T(8,128)(2,1)} %bitcast.24), calls=%async_computation.2 | async-start | bytes 1310720 | tf_op jit(solution)/shard_map/all_to_all | solution.py:459
  122.5 14.4 %all-to-all-start.3 = ((f32[4,16,640]{2,1,0:T(8,128)}), f32[4,16,640]{2,1,0:T(8,128)S(1)}, u32[]{:S(2)}, u32[]{:S(2)}) async-start(f32[4,16,640]{2,1,0:T(8,128)} %join.1), calls=%async_computation.3 | async-start | bytes 327680 | tf_op jit(solution)/shard_map/all_to_all | solution.py:463
